TPU v7x, 32 devices: a whole 2x2x4 slice. The times are simulated.
32 devices in a mesh: groups: 2 (over y), seq: 4 (over z), mp: 4 (over x, core).
Axes of the slice: x: 2, y: 2, z: 4, core: 2. Of those that a mesh axis runs over, the one named last changes fastest.
Arguments:
- node_vectors: bfloat16 [1024, 2048], P(('groups', 'seq'), 'mp'), parts along dimension 0, may hold values from -6 to 6
- standardize_multiplier: float32 [2048], replicated, may hold values from 0.1 to 1.9
- probe_matrix: bfloat16 [2048, 1024], P(None, 'mp'), may hold values from -1 to 1
- lookup_matrix: bfloat16 [2048, 1024], P(None, 'mp'), may hold values from -1 to 1
- content_matrix: bfloat16 [2048, 1024], P(None, 'mp'), may hold values from -0.125 to 0.125
- softness_per_group: float32 [8], P('mp'), may hold values from 0.5 to 12
- exit_matrix: bfloat16 [1024, 2048], P('mp'), may hold values from -0.1875 to 0.1875
Outputs:
- mixed: bfloat16 [1024, 2048], P(('groups', 'seq'), 'mp'), parts along dimension 0
There are 2 independent parts, one for each index of `groups`. A program takes and returns all parts, laid end to end along the dimension named above; an argument that names none is the same for every part. Nothing has to cross between parts.
All inputs are finite; a program needn't handle non-finite values.
Results may differ from a plain program's by a relative error of at most 0.011.
Values may be sent and summed in bfloat16 or wider, within the bound.
No kernel may reach another device: no remote copies, remote signals or barrier semaphores. Data moves between devices by JAX's collectives and lax.ppermute only.
A program may use at most 64 MiB of HBM per device.

v0:
```python
import math

import jax
import jax.numpy as jnp
from jax import lax
from jax.sharding import PartitionSpec as P


def attend(state_in, blocks, query_heads, inverse_root_span, resident_groups, channel_span):
    running_max, running_sum, weighted = state_in
    key_block, value_block = blocks
    count = key_block.shape[0]
    key_heads = key_block.reshape(count, resident_groups, channel_span)
    value_heads = value_block.reshape(count, resident_groups, channel_span)
    scores = (
        jnp.einsum("rhd,nhd->hrn", query_heads, key_heads, preferred_element_type=jnp.float32)
        * inverse_root_span[:, None, None]
    )
    new_max = jnp.max(scores, axis=-1)
    rescale = jnp.exp(running_max - new_max)
    weights = jnp.exp(scores - new_max[:, :, None])
    running_sum = running_sum * rescale + jnp.sum(weights, axis=-1)
    update = jnp.einsum(
        "hrn,nhd->hrd",
        weights.astype(jnp.bfloat16),
        value_heads,
        preferred_element_type=jnp.float32,
    )
    weighted = weighted * rescale[:, :, None] + update
    return (new_max, running_sum, weighted)


def per_device(
    node_vectors,
    standardize_multiplier,
    probe_matrix,
    lookup_matrix,
    content_matrix,
    softness_per_group,
    exit_matrix,
):
    full_rows = lax.all_gather(node_vectors, "mp", axis=1, tiled=True)
    widened = full_rows.astype(jnp.float32)
    average = jnp.mean(widened, axis=-1, keepdims=True)
    centered = widened - average
    variance = jnp.mean(centered * centered, axis=-1, keepdims=True)
    normed = (centered * lax.rsqrt(variance + 1e-05) * standardize_multiplier).astype(jnp.bfloat16)
    queries = jnp.dot(normed, probe_matrix, preferred_element_type=jnp.float32).astype(jnp.bfloat16)
    key_rows = jnp.dot(normed, lookup_matrix, preferred_element_type=jnp.float32).astype(
        jnp.bfloat16
    )
    value_rows = jnp.dot(normed, content_matrix, preferred_element_type=jnp.float32).astype(
        jnp.bfloat16
    )
    resident_groups = softness_per_group.shape[0]
    head_cols = queries.shape[1]
    channel_span = head_cols // resident_groups
    token_count = queries.shape[0]
    query_heads = queries.reshape(token_count, resident_groups, channel_span)
    inverse_root_span = softness_per_group / math.sqrt(channel_span)
    initial = (
        jnp.full((resident_groups, token_count), -jnp.inf, jnp.float32),
        jnp.zeros((resident_groups, token_count), jnp.float32),
        jnp.zeros((resident_groups, token_count, channel_span), jnp.float32),
    )
    final = attend(
        initial,
        (
            lax.all_gather(key_rows, "seq", axis=0, tiled=True),
            lax.all_gather(value_rows, "seq", axis=0, tiled=True),
        ),
        query_heads,
        inverse_root_span,
        resident_groups,
        channel_span,
    )
    heads_out = (
        (final[2] / final[1][:, :, None])
        .transpose(1, 0, 2)
        .reshape(token_count, head_cols)
        .astype(jnp.bfloat16)
    )
    partial_sums = jnp.dot(heads_out, exit_matrix, preferred_element_type=jnp.float32)
    summed = lax.psum_scatter(
        partial_sums.astype(jnp.bfloat16), "mp", scatter_dimension=1, tiled=True
    ).astype(jnp.float32)
    return (node_vectors.astype(jnp.float32) + summed).astype(jnp.bfloat16)


def solution(mesh):
    return jax.shard_map(
        per_device,
        mesh=mesh,
        in_specs=(
            P(("groups", "seq"), "mp"),
            P(),
            P(None, "mp"),
            P(None, "mp"),
            P(None, "mp"),
            P("mp"),
            P("mp", None),
        ),
        out_specs=P(("groups", "seq"), "mp"),
        check_vma=False,
    )
```

profile of v0, /device:TPU:0, one launch (start us, length us, event | category | flops | bytes accessed | tf_op | source)
XLA Modules:
  0.0 81.6 jit_solution(14585379958456140718)
XLA Ops:
  6.5 0.0 copy-start
  6.5 0.0 copy-start.2
  6.5 0.0 reduce-scatter.2.cloned.1.call-start
  6.5 0.8 broadcast_multiply_fusion
  7.3 8.8 %all_gather.9 = bf16[128,2048]{1,0:T(8,128)(2,1)S(1)} all-gather(bf16[128,512]{1,0:T(8,128)(2,1)} %param.7), channel_id=1, replica_groups=mesh['groups'=2,'seq'=4,'mp'=4] {'mp'}, dimensions={1}, use_global_device_ids=true | all-gather | bytes 655360 | tf_op jit(solution)/shard_map/all_gather | solution.py:42
  16.2 0.2 convert_reduce_fusion
  16.3 0.0 copy-start.5
  16.3 0.3 fusion.6
  16.6 0.0 copy-done.2
  16.6 0.4 copy-done.5
  17.0 0.0 copy-start.3
  17.0 0.4 convolution_convert_fusion.2
  17.4 0.9 %copy-done.3 = bf16[2048,256]{1,0:T(8,128)(2,1)S(1)} copy-done((bf16[2048,256]{1,0:T(8,128)(2,1)S(1)}, bf16[2048,256]{1,0:T(8,128)(2,1)}, u32[]{:S(2)}) %copy-start.3) | copy-done | bytes 1048600
  18.2 0.0 copy-start.4
  18.3 0.4 convolution_convert_fusion.1
  18.6 0.9 %copy-done.4 = bf16[2048,256]{1,0:T(8,128)(2,1)S(1)} copy-done((bf16[2048,256]{1,0:T(8,128)(2,1)S(1)}, bf16[2048,256]{1,0:T(8,128)(2,1)}, u32[]{:S(2)}) %copy-start.4) | copy-done | bytes 1048600
  19.5 0.4 fusion.5
  19.8 14.1 %all_gather.11 = bf16[512,256]{1,0:T(8,128)(2,1)S(1)} all-gather(bf16[128,256]{1,0:T(8,128)(2,1)S(1)} %convolution_convert_fusion.1), channel_id=1, replica_groups=mesh['groups'=2,'seq'=4,'mp'=4] {'seq'}, dimensions={0}, use_global_device_ids=true | all-gather | bytes 327680 | tf_op jit(solution)/shard_map/all_gather | solution.py:70
  34.0 0.1 copy.11
  34.1 14.4 %all_gather.10 = bf16[512,256]{1,0:T(8,128)(2,1)S(1)} all-gather(bf16[128,256]{1,0:T(8,128)(2,1)S(1)} %convolution_convert_fusion.2), channel_id=1, replica_groups=mesh['groups'=2,'seq'=4,'mp'=4] {'seq'}, dimensions={0}, use_global_device_ids=true | all-gather | bytes 327680 | tf_op jit(solution)/shard_map/all_gather | solution.py:69
  48.5 0.3 fusion.20
  48.9 0.2 fusion.9
  49.1 0.3 fusion.4
  49.4 0.0 copy-done
  49.5 1.1 %convolution_convert_fusion = bf16[128,2048]{1,0:T(8,128)(2,1)} fusion(bf16[128,256]{0,1:T(8,128)(2,1)S(1)} %bitcast.39, bf16[256,2048]{1,0:T(8,128)(2,1)S(1)} %copy-done), kind=kOutput, calls=%fused_computation | convolution fusion | flops 134479872 | bytes 1638400 | tf_op jit(solution)/shard_map/dot_general | solution.py:83
  50.6 0.0 copy-start.1
  50.6 0.0 reduce-scatter.2.cloned.1.call-update
  50.6 22.5 %reduce-scatter.2.cloned.1.call-done = bf16[128,512]{1,0:T(8,128)(2,1)} async-done(((bf16[128,2048]{1,0:T(8,128)(2,1)}), bf16[128,512]{1,0:T(8,128)(2,1)}) %reduce-scatter.2.cloned.1.call-update) | async-done | bytes 131088 | tf_op jit(solution)/shard_map/reduce_scatter | solution.py:84
  73.1 0.0 copy-done.1
  73.1 1.6 %add_convert_fusion = bf16[128,512]{1,0:T(8,128)(2,1)} fusion(bf16[128,512]{1,0:T(8,128)(2,1)} %reduce-scatter.2.cloned.1.call-done, bf16[128,512]{1,0:T(8,128)(2,1)S(1)} %copy-done.1), kind=kLoop, calls=%fused_computation.22 | loop fusion | flops 262144 | bytes 393216 | tf_op jit(solution)/shard_map/convert_element_type | solution.py:87
  (4 shorter events, 0.0 us)
Async XLA Ops:
  6.5 42.9 %copy-start = (bf16[256,2048]{1,0:T(8,128)(2,1)S(1)}, bf16[256,2048]{1,0:T(8,128)(2,1)}, u32[]{:S(2)}) copy-start(bf16[256,2048]{1,0:T(8,128)(2,1)} %param.13) | copy-start | bytes 3145732
  6.5 10.1 %copy-start.2 = (bf16[2048,256]{1,0:T(8,128)(2,1)S(1)}, bf16[2048,256]{1,0:T(8,128)(2,1)}, u32[]{:S(2)}) copy-start(bf16[2048,256]{1,0:T(8,128)(2,1)} %param.10) | copy-start | bytes 3145732
  6.5 66.6 %reduce-scatter.2.cloned.1.call-start = ((), (), s32[]{:S(2)}) async-start(), calls=%async_computation.1 | async-start | bytes 655360 | tf_op jit(solution)/shard_map/reduce_scatter | solution.py:84
  16.3 0.7 copy-start.5
  17.0 1.2 %copy-start.3 = (bf16[2048,256]{1,0:T(8,128)(2,1)S(1)}, bf16[2048,256]{1,0:T(8,128)(2,1)}, u32[]{:S(2)}) copy-start(bf16[2048,256]{1,0:T(8,128)(2,1)} %param.11) | copy-start | bytes 3145732
  18.2 1.2 %copy-start.4 = (bf16[2048,256]{1,0:T(8,128)(2,1)S(1)}, bf16[2048,256]{1,0:T(8,128)(2,1)}, u32[]{:S(2)}) copy-start(bf16[2048,256]{1,0:T(8,128)(2,1)} %param.9) | copy-start | bytes 3145732
  50.6 22.6 %copy-start.1 = (bf16[128,512]{1,0:T(8,128)(2,1)S(1)}, bf16[128,512]{1,0:T(8,128)(2,1)}, u32[]{:S(2)}) copy-start(bf16[128,512]{1,0:T(8,128)(2,1)} %param.7) | copy-start | bytes 393220
Sparse Core Ops, SparseCore 0:
  50.7 22.3 reduce-scatter.1
where the time goes:
time: 81.9 us; the launch traced here: 81.6 us
  blocking collectives  37.4 us (46%)
  waiting for transfers between devices  22.5 us (27%)
  between operations  13.5 us (16%)
  other arithmetic  3.1 us (4%)
  matrix products  2.86 us (3%)
  local copies, waits for them, and re-layouts  2.25 us (3%)
    reduce_scatter x1, waiting for transfers between devices, per_device(): lax.psum_scatter(partial_sums.astype(jnp.bfloat16), 'mp', scatter_dimensi...  22.5 us
    all_gather x1, blocking collectives, per_device(): lax.all_gather(key_rows, 'seq', axis=0, tiled=True)  14.4 us
    all_gather x1, blocking collectives, per_device(): lax.all_gather(value_rows, 'seq', axis=0, tiled=True)  14.1 us
    all_gather x1, blocking collectives, per_device(): full_rows = lax.all_gather(node_vectors, 'mp', axis=1, tiled=True)  8.82 us
    unnamed x12, local copies, waits for them, and re-layouts  2.11 us
  transfers between devices with their start and end apart: 1, of which 1 were waited for; matrix products, arithmetic and copies ran while one was open for 0% of the time, Pallas kernels for 0%

commit v1 on v0

v1 whole, which is shorter than its diff:
```python
import math

import jax
import jax.numpy as jnp
from jax import lax
from jax.sharding import PartitionSpec as P


def swap(block, axis, count, distance):
    return lax.ppermute(block, axis, [(i, i ^ distance) for i in range(count)])


def gather_blocks(block, axis, count):
    blocks = {0: block}
    distance = count // 2
    while distance:
        blocks.update({k ^ distance: swap(b, axis, count, distance) for k, b in list(blocks.items())})
        distance //= 2
    return [blocks[k] for k in range(count)]


def attend(query_heads, key_rows, value_rows, factor, channel_span):
    heads = query_heads.shape[1]
    count = key_rows.shape[0]
    key_heads = key_rows.reshape(count, heads, channel_span)
    value_heads = value_rows.reshape(count, heads, channel_span)
    scores = (
        jnp.einsum("rhd,nhd->hrn", query_heads, key_heads, preferred_element_type=jnp.float32)
        * factor[:, None, None]
    )
    weights = jnp.exp(scores - jnp.max(scores, axis=-1, keepdims=True))
    totals = jnp.sum(weights, axis=-1)
    weighted = jnp.einsum(
        "hrn,nhd->hrd",
        weights.astype(jnp.bfloat16),
        value_heads,
        preferred_element_type=jnp.float32,
    )
    return weighted / totals[:, :, None]


def per_device(mesh, node_vectors, gain, probe, lookup, content, softness, exit_matrix):
    mp, seq = mesh.shape["mp"], mesh.shape["seq"]
    me = lax.axis_index("mp")
    full_rows = lax.all_gather(node_vectors, "mp", axis=1, tiled=True)
    widened = full_rows.astype(jnp.float32)
    average = jnp.mean(widened, axis=-1, keepdims=True)
    centered = widened - average
    variance = jnp.mean(centered * centered, axis=-1, keepdims=True)
    normed = (centered * lax.rsqrt(variance + 1e-05) * gain).astype(jnp.bfloat16)
    key_rows = jnp.dot(normed, lookup, preferred_element_type=jnp.float32).astype(jnp.bfloat16)
    value_rows = jnp.dot(normed, content, preferred_element_type=jnp.float32).astype(jnp.bfloat16)
    queries = jnp.dot(normed, probe, preferred_element_type=jnp.float32).astype(jnp.bfloat16)
    heads = softness.shape[0]
    head_cols = queries.shape[1]
    channel_span = head_cols // heads
    rows = queries.shape[0]
    both = jnp.concatenate([key_rows, value_rows], axis=1)
    all_rows = jnp.concatenate(gather_blocks(both, "seq", seq), axis=0)
    heads_out = (
        attend(
            queries.reshape(rows, heads, channel_span),
            all_rows[:, :head_cols],
            all_rows[:, head_cols:],
            softness / math.sqrt(channel_span),
            channel_span,
        )
        .transpose(1, 0, 2)
        .reshape(rows, head_cols)
        .astype(jnp.bfloat16)
    )
    partial = jnp.dot(heads_out, exit_matrix, preferred_element_type=jnp.float32)
    width = partial.shape[1] // mp
    shares = {
        k: lax.dynamic_slice_in_dim(partial, (me ^ k) * width, width, axis=1) for k in range(mp)
    }
    distance = 1
    while distance < mp:
        shares = {
            k: shares[k]
            + swap(shares[k ^ distance].astype(jnp.bfloat16), "mp", mp, distance).astype(jnp.float32)
            for k in shares
            if not k & distance
        }
        distance *= 2
    return (node_vectors.astype(jnp.float32) + shares[0]).astype(jnp.bfloat16)


def solution(mesh):
    return jax.shard_map(
        lambda *arrays: per_device(mesh, *arrays),
        mesh=mesh,
        in_specs=(
            P(("groups", "seq"), "mp"),
            P(),
            P(None, "mp"),
            P(None, "mp"),
            P(None, "mp"),
            P("mp"),
            P("mp", None),
        ),
        out_specs=P(("groups", "seq"), "mp"),
        check_vma=False,
    )
```

time: 81.9 us -> 35.6 us (0.43)
  blocking collectives: 37.4 us -> 8.95 us
  between operations: 13.5 us -> 0.14 us
  waiting for transfers between devices: 22.5 us -> 14 us
  starting transfers between devices: 0.01 us -> 6.53 us
  other arithmetic: 3.1 us -> 1.48 us
    all_gather x2 -> x0, blocking collectives: 28.5 us -> none  [the longest x1 14.4 us: per_device(): lax.all_gather(key_rows, 'seq', axis=0, tiled=True)]
    reduce_scatter x1 -> x0, waiting for transfers between devices: 22.5 us -> none  [per_device(): lax.psum_scatter(partial_sums.astype(jnp.bfloat16), 'mp', scatter_dimensi...]
    ppermute x0 -> x6, waiting for transfers between devices: none -> 14 us  [swap(): return lax.ppermute(block, axis, [(i, i ^ distance) for i in range(count)])]
    ppermute x0 -> x6, starting transfers between devices: none -> 6.53 us  [swap(): return lax.ppermute(block, axis, [(i, i ^ distance) for i in range(count)])]
    convert_element_type x1 -> x2, other arithmetic: 1.59 us -> 0.75 us  [the longest x1 0.72 us: per_device(): return (node_vectors.astype(jnp.float32) + shares[0]).astype(jnp.bfloat16)]
    unnamed x12 -> x15, local copies, waits for them, and re-layouts: 2.11 us -> 1.96 us
  transfers between devices with their start and end apart: 1 -> 6, of which waited for: 1 -> 4; matrix products, arithmetic and copies ran while one was open for 0% -> 1% of each run, Pallas kernels for 0% -> 0%
where the time goes in v1:
time: 35.6 us; the launch traced here: 35.4 us
  waiting for transfers between devices  14 us (39%)
  blocking collectives  8.95 us (25%)
  starting transfers between devices  6.53 us (18%)
  local copies, waits for them, and re-layouts  2.14 us (6%)
  matrix products  2.1 us (6%)
  other arithmetic  1.48 us (4%)
    ppermute x6, waiting for transfers between devices, swap(): return lax.ppermute(block, axis, [(i, i ^ distance) for i in range(count)])  14 us
    all_gather x1, blocking collectives, per_device(): full_rows = lax.all_gather(node_vectors, 'mp', axis=1, tiled=True)  8.95 us
    ppermute x6, starting transfers between devices, swap(): return lax.ppermute(block, axis, [(i, i ^ distance) for i in range(count)])  6.53 us
    unnamed x15, local copies, waits for them, and re-layouts  1.96 us
    convert_element_type x1, other arithmetic, per_device(): return (node_vectors.astype(jnp.float32) + shares[0]).astype(jnp.bfloat16)  0.72 us
  transfers between devices with their start and end apart: 6, of which 4 were waited for; matrix products, arithmetic and copies ran while one was open for 1% of the time, Pallas kernels for 0%

profile of v1, /device:TPU:0, one launch (start us, length us, event | category | flops | bytes accessed | tf_op | source)
XLA Modules:
  0.0 35.4 jit_solution(11849262324453274013)
XLA Ops:
  0.0 0.0 copy-start
  0.0 0.0 copy-start.2
  0.0 8.9 %all_gather.3 = bf16[128,2048]{1,0:T(8,128)(2,1)S(1)} all-gather(bf16[128,512]{1,0:T(8,128)(2,1)} %param.7), channel_id=1, replica_groups=mesh['groups'=2,'seq'=4,'mp'=4] {'mp'}, dimensions={1}, use_global_device_ids=true | all-gather | bytes 655360 | tf_op jit(solution)/shard_map/all_gather | solution.py:45
  9.0 0.2 convert_reduce_fusion
  9.1 0.0 copy-start.5
  9.1 0.3 fusion.5
  9.4 0.0 copy-done.2
  9.4 0.4 %copy-done.5 = f32[2048]{0:T(1024)S(1)} copy-done((f32[2048]{0:T(1024)S(1)}, f32[2048]{0:T(1024)}, u32[]{:S(2)}) %copy-start.5) | copy-done | bytes 8216
  9.8 0.0 copy-start.3
  9.8 0.4 %convolution_convert_fusion.1 = bf16[128,256]{1,0:T(8,128)(2,1)S(1)} fusion(bf16[2048,256]{1,0:T(8,128)(2,1)S(1)} %copy-done.2, bf16[128,2048]{1,0:T(8,128)(2,1)S(1)} %all_gather.3, f32[2048]{0:T(1024)S(1)} %copy-done.5, f32[128]{0:T(128)S(1)} %add_rsqrt_fusion, f32[128]{0:T(128)S(1)} %broadcast_multiply_fusion.1), kind=kOutput, calls=%fused_computation.9 | convolution fusion | flops 135561216 | bytes 1647616 | tf_op jit(solution)/shard_map/dot_general | solution.py:51
  10.2 0.8 %copy-done.3 = bf16[2048,256]{1,0:T(8,128)(2,1)S(1)} copy-done((bf16[2048,256]{1,0:T(8,128)(2,1)S(1)}, bf16[2048,256]{1,0:T(8,128)(2,1)}, u32[]{:S(2)}) %copy-start.3) | copy-done | bytes 1048600
  11.0 0.0 copy-start.4
  11.0 0.4 %convolution_convert_fusion = bf16[128,256]{1,0:T(8,128)(2,1)S(1)} fusion(bf16[2048,256]{1,0:T(8,128)(2,1)S(1)} %copy-done.3, bf16[128,2048]{1,0:T(8,128)(2,1)S(1)} %all_gather.3, f32[2048]{0:T(1024)S(1)} %copy-done.5, f32[128]{0:T(128)S(1)} %add_rsqrt_fusion, f32[128]{0:T(128)S(1)} %broadcast_multiply_fusion.1), kind=kOutput, calls=%fused_computation.8 | convolution fusion | flops 135561216 | bytes 1647616 | tf_op jit(solution)/shard_map/dot_general | solution.py:52
  11.4 2.7 %collective-permute-start.1 = (bf16[128,512]{1,0:T(8,128)(2,1)S(1)}, bf16[128,512]{1,0:T(8,128)(2,1)S(1)}, u32[]{:S(2)}, u32[]{:S(2)}) collective-permute-start(bf16[128,512]{1,0:T(8,128)(2,1)S(1)} %pad_maximum_fusion.1), channel_id=1, source_target_pairs={{0,8},{4,12},{8,0},{12,4},{1,9},{5,13},{9,1},{13,5},{2,10},{6,14},... | collective-permute-start | bytes 393224 | tf_op jit(solution)/shard_map/ppermute | solution.py:10
  14.1 1.6 %collective-permute-start = (bf16[128,512]{1,0:T(8,128)(2,1)S(1)}, bf16[128,512]{1,0:T(8,128)(2,1)S(1)}, u32[]{:S(2)}, u32[]{:S(2)}) collective-permute-start(bf16[128,512]{1,0:T(8,128)(2,1)S(1)} %pad_maximum_fusion.1), channel_id=1, source_target_pairs={{0,4},{4,0},{8,12},{12,8},{1,5},{5,1},{9,13},{13,9},{2,6},{6,2},{1... | collective-permute-start | bytes 393224 | tf_op jit(solution)/shard_map/ppermute | solution.py:10
  15.7 0.0 copy-start.6
  15.7 0.7 %copy-done.6 = f32[2]{0:T(128)S(1)} copy-done((f32[2]{0:T(128)S(1)}, f32[2]{0:T(128)}, u32[]{:S(2)}) %copy-start.6) | copy-done | bytes 32
  16.3 4.7 %collective-permute-done.1 = bf16[128,512]{1,0:T(8,128)(2,1)S(1)} collective-permute-done((bf16[128,512]{1,0:T(8,128)(2,1)S(1)}, bf16[128,512]{1,0:T(8,128)(2,1)S(1)}, u32[]{:S(2)}, u32[]{:S(2)}) %collective-permute-start.1) | collective-permute-done | bytes 131104 | tf_op jit(solution)/shard_map/ppermute | solution.py:10
  21.1 0.6 %collective-permute-start.2 = (bf16[128,512]{1,0:T(8,128)(2,1)S(1)}, bf16[128,512]{1,0:T(8,128)(2,1)S(1)}, u32[]{:S(2)}, u32[]{:S(2)}) collective-permute-start(bf16[128,512]{1,0:T(8,128)(2,1)S(1)} %collective-permute-done.1), channel_id=1, source_target_pairs={{0,4},{4,0},{8,12},{12,8},{1,5},{5,1},{9,13},{13,9},{2,6},{6,2},{1... | collective-permute-start | bytes 393224 | tf_op jit(solution)/shard_map/ppermute | solution.py:10
  21.6 0.0 copy-done.4
  21.7 0.4 %fusion.4 = bf16[16,2,8,128]{3,2,1,0:T(8,128)(2,1)S(1)} fusion(bf16[2048,256]{1,0:T(8,128)(2,1)S(1)} %copy-done.4, bf16[128,2048]{1,0:T(8,128)(2,1)S(1)} %all_gather.3, f32[2048]{0:T(1024)S(1)} %copy-done.5, f32[128]{0:T(128)S(1)} %add_rsqrt_fusion, f32[128]{0:T(128)S(1)} %broadcast_multiply_fusion.1), kind=kOutput, calls=%fused_computation.11 | convolution fusion | flops 135561216 | bytes 1647616 | tf_op jit(solution)/shard_map/dot_general | solution.py:53
  22.0 0.0 collective-permute-done
  22.0 4.0 %collective-permute-done.2 = bf16[128,512]{1,0:T(8,128)(2,1)S(1)} collective-permute-done((bf16[128,512]{1,0:T(8,128)(2,1)S(1)}, bf16[128,512]{1,0:T(8,128)(2,1)S(1)}, u32[]{:S(2)}, u32[]{:S(2)}) %collective-permute-start.2) | collective-permute-done | bytes 131104 | tf_op jit(solution)/shard_map/ppermute | solution.py:10
  26.1 0.1 copy.11
  26.3 0.3 fusion.19
  26.6 0.2 fusion.8
  26.8 0.3 fusion.3
  27.2 0.0 copy-done
  27.2 0.3 fusion.20
  27.6 0.1 collective-permute-start.4
  27.7 0.0 copy-start.1
  27.7 0.5 %collective-permute-start.3 = (bf16[128,512]{1,0:T(8,128)(2,1)S(1)}, bf16[128,512]{1,0:T(8,128)(2,1)S(1)}, u32[]{:S(2)}, u32[]{:S(2)}) collective-permute-start(bf16[128,512]{1,0:T(8,128)(2,1)S(1)} %get-tuple-element.5), channel_id=1, source_target_pairs={{0,1},{1,0},{2,3},{3,2},{4,5},{5,4},{6,7},{7,6},{8,9},{9,8},{10,11... | collective-permute-start | bytes 393224 | tf_op jit(solution)/shard_map/ppermute | solution.py:10
  28.1 0.8 %collective-permute-done.4 = bf16[128,512]{1,0:T(8,128)(2,1)S(1)} collective-permute-done((bf16[128,512]{1,0:T(8,128)(2,1)S(1)}, bf16[128,512]{1,0:T(8,128)(2,1)S(1)}, u32[]{:S(2)}, u32[]{:S(2)}) %collective-permute-start.4) | collective-permute-done | bytes 131104 | tf_op jit(solution)/shard_map/ppermute | solution.py:10
  29.0 1.2 %collective-permute-start.5 = (bf16[128,512]{1,0:T(8,128)(2,1)S(1)}, bf16[128,512]{1,0:T(8,128)(2,1)S(1)}, u32[]{:S(2)}, u32[]{:S(2)}) collective-permute-start(bf16[128,512]{1,0:T(8,128)(2,1)S(1)} %add_convert_fusion.1), channel_id=1, source_target_pairs={{0,2},{1,3},{2,0},{3,1},{4,6},{5,7},{6,4},{7,5},{8,10},{9,11},{10,... | collective-permute-start | bytes 393224 | tf_op jit(solution)/shard_map/ppermute | solution.py:10
  30.2 0.0 collective-permute-done.3
  30.2 4.4 %collective-permute-done.5 = bf16[128,512]{1,0:T(8,128)(2,1)S(1)} collective-permute-done((bf16[128,512]{1,0:T(8,128)(2,1)S(1)}, bf16[128,512]{1,0:T(8,128)(2,1)S(1)}, u32[]{:S(2)}, u32[]{:S(2)}) %collective-permute-start.5) | collective-permute-done | bytes 131104 | tf_op jit(solution)/shard_map/ppermute | solution.py:10
  34.6 0.0 copy-done.1
  34.6 0.7 %add_convert_fusion = bf16[128,512]{1,0:T(8,128)(2,1)} fusion(bf16[128,512]{1,0:T(8,128)(2,1)S(1)} %collective-permute-done.5, bf16[128,512]{1,0:T(8,128)(2,1)S(1)} %collective-permute-done.3, f32[128,2048]{1,0:T(8,128)S(1)} %fusion.20, s32[]{:T(128)S(6)} %select_n.12, bf16[128,512]{1,0:T(8,128)(2,1)S(1)} %copy-done.1), kind=kLoop, calls=%fused_computation.22 | loop fusion | flops 458752 | bytes 786436 | tf_op jit(solution)/shard_map/convert_element_type | solution.py:86
  (8 shorter events, 0.2 us)
Async XLA Ops:
  0.0 27.2 %copy-start = (bf16[256,2048]{1,0:T(8,128)(2,1)S(1)}, bf16[256,2048]{1,0:T(8,128)(2,1)}, u32[]{:S(2)}) copy-start(bf16[256,2048]{1,0:T(8,128)(2,1)} %param.13) | copy-start | bytes 3145732
  0.0 9.4 %copy-start.2 = (bf16[2048,256]{1,0:T(8,128)(2,1)S(1)}, bf16[2048,256]{1,0:T(8,128)(2,1)}, u32[]{:S(2)}) copy-start(bf16[2048,256]{1,0:T(8,128)(2,1)} %param.10) | copy-start | bytes 3145732
  9.1 0.7 %copy-start.5 = (f32[2048]{0:T(1024)S(1)}, f32[2048]{0:T(1024)}, u32[]{:S(2)}) copy-start(f32[2048]{0:T(1024)} %param.8) | copy-start | bytes 24580
  9.8 1.2 %copy-start.3 = (bf16[2048,256]{1,0:T(8,128)(2,1)S(1)}, bf16[2048,256]{1,0:T(8,128)(2,1)}, u32[]{:S(2)}) copy-start(bf16[2048,256]{1,0:T(8,128)(2,1)} %param.11) | copy-start | bytes 3145732
  11.0 10.6 %copy-start.4 = (bf16[2048,256]{1,0:T(8,128)(2,1)S(1)}, bf16[2048,256]{1,0:T(8,128)(2,1)}, u32[]{:S(2)}) copy-start(bf16[2048,256]{1,0:T(8,128)(2,1)} %param.9) | copy-start | bytes 3145732
  11.4 9.6 %collective-permute-start.1 = (bf16[128,512]{1,0:T(8,128)(2,1)S(1)}, bf16[128,512]{1,0:T(8,128)(2,1)S(1)}, u32[]{:S(2)}, u32[]{:S(2)}) collective-permute-start(bf16[128,512]{1,0:T(8,128)(2,1)S(1)} %pad_maximum_fusion.1), channel_id=1, source_target_pairs={{0,8},{4,12},{8,0},{12,4},{1,9},{5,13},{9,1},{13,5},{2,10},{6,14},... | collective-permute-start | bytes 393224 | tf_op jit(solution)/shard_map/ppermute | solution.py:10
  14.1 7.9 %collective-permute-start = (bf16[128,512]{1,0:T(8,128)(2,1)S(1)}, bf16[128,512]{1,0:T(8,128)(2,1)S(1)}, u32[]{:S(2)}, u32[]{:S(2)}) collective-permute-start(bf16[128,512]{1,0:T(8,128)(2,1)S(1)} %pad_maximum_fusion.1), channel_id=1, source_target_pairs={{0,4},{4,0},{8,12},{12,8},{1,5},{5,1},{9,13},{13,9},{2,6},{6,2},{1... | collective-permute-start | bytes 393224 | tf_op jit(solution)/shard_map/ppermute | solution.py:10
  15.7 0.7 %copy-start.6 = (f32[2]{0:T(128)S(1)}, f32[2]{0:T(128)}, u32[]{:S(2)}) copy-start(f32[2]{0:T(128)} %param.12) | copy-start | bytes 28
  21.1 5.0 %collective-permute-start.2 = (bf16[128,512]{1,0:T(8,128)(2,1)S(1)}, bf16[128,512]{1,0:T(8,128)(2,1)S(1)}, u32[]{:S(2)}, u32[]{:S(2)}) collective-permute-start(bf16[128,512]{1,0:T(8,128)(2,1)S(1)} %collective-permute-done.1), channel_id=1, source_target_pairs={{0,4},{4,0},{8,12},{12,8},{1,5},{5,1},{9,13},{13,9},{2,6},{6,2},{1... | collective-permute-start | bytes 393224 | tf_op jit(solution)/shard_map/ppermute | solution.py:10
  27.6 1.4 %collective-permute-start.4 = (bf16[128,512]{1,0:T(8,128)(2,1)S(1)}, bf16[128,512]{1,0:T(8,128)(2,1)S(1)}, u32[]{:S(2)}, u32[]{:S(2)}) collective-permute-start(bf16[128,512]{1,0:T(8,128)(2,1)S(1)} %get-tuple-element.6), channel_id=1, source_target_pairs={{0,1},{1,0},{2,3},{3,2},{4,5},{5,4},{6,7},{7,6},{8,9},{9,8},{10,11... | collective-permute-start | bytes 393224 | tf_op jit(solution)/shard_map/ppermute | solution.py:10
  27.7 7.0 %copy-start.1 = (bf16[128,512]{1,0:T(8,128)(2,1)S(1)}, bf16[128,512]{1,0:T(8,128)(2,1)}, u32[]{:S(2)}) copy-start(bf16[128,512]{1,0:T(8,128)(2,1)} %param.7) | copy-start | bytes 393220
  27.7 2.5 %collective-permute-start.3 = (bf16[128,512]{1,0:T(8,128)(2,1)S(1)}, bf16[128,512]{1,0:T(8,128)(2,1)S(1)}, u32[]{:S(2)}, u32[]{:S(2)}) collective-permute-start(bf16[128,512]{1,0:T(8,128)(2,1)S(1)} %get-tuple-element.5), channel_id=1, source_target_pairs={{0,1},{1,0},{2,3},{3,2},{4,5},{5,4},{6,7},{7,6},{8,9},{9,8},{10,11... | collective-permute-start | bytes 393224 | tf_op jit(solution)/shard_map/ppermute | solution.py:10
  29.0 5.6 %collective-permute-start.5 = (bf16[128,512]{1,0:T(8,128)(2,1)S(1)}, bf16[128,512]{1,0:T(8,128)(2,1)S(1)}, u32[]{:S(2)}, u32[]{:S(2)}) collective-permute-start(bf16[128,512]{1,0:T(8,128)(2,1)S(1)} %add_convert_fusion.1), channel_id=1, source_target_pairs={{0,2},{1,3},{2,0},{3,1},{4,6},{5,7},{6,4},{7,5},{8,10},{9,11},{10,... | collective-permute-start | bytes 393224 | tf_op jit(solution)/shard_map/ppermute | solution.py:10

commit v2 on v1

v2 whole, which is shorter than its diff:
```python
import functools
import math

import jax
import jax.numpy as jnp
from jax import lax
from jax.experimental import pallas as pl
from jax.experimental.pallas import tpu as pltpu
from jax.sharding import PartitionSpec as P

F32, BF16 = jnp.float32, jnp.bfloat16
VMEM = pl.BlockSpec(memory_space=pltpu.VMEM)
HBM = pl.BlockSpec(memory_space=pltpu.HBM)
PARAMS = pltpu.CompilerParams(vmem_limit_bytes=16 << 20)
LANES = 128


def swap(block, axis, count, distance):
    return lax.ppermute(block, axis, [(i, i ^ distance) for i in range(count)])


def after(value, *others):
    return lax.optimization_barrier((value, *others))[0]


def prepare_kernel(mp, heads, gain_ref, probe_ref, lookup_ref, content_ref, exit_ref, *refs):
    groups = mp.bit_length() - 1
    weights_ref, sums_ref, gain_out_ref, own_ref = refs[:4]
    far_refs = refs[4 : 4 + groups]
    rows_ref, sems, gain_sem, exit_sems = refs[4 + groups :]
    me = lax.axis_index("mp")
    depth, cols = probe_ref.shape
    parts = sems.shape[0]
    chunk = depth // parts
    gain_copy = pltpu.make_async_copy(gain_ref, gain_out_ref, gain_sem)
    gain_copy.start()
    copies = []
    for c in range(parts):
        rows = pl.ds(c * chunk, chunk)
        moves = [(probe_ref, 0, cols, 0)]
        for h in range(heads):
            moves.append((lookup_ref, h * LANES, LANES, cols + 2 * h * LANES))
            moves.append((content_ref, h * LANES, LANES, cols + (2 * h + 1) * LANES))
        copies.append([])
        for i, (ref, start, width, to) in enumerate(moves):
            copy = pltpu.make_async_copy(
                ref.at[rows, pl.ds(start, width)], weights_ref.at[rows, pl.ds(to, width)], sems.at[c, i]
            )
            copy.start()
            copies[c].append(copy)
    width = own_ref.shape[1]
    exits = []
    for k in range(mp):
        to = far_refs[k.bit_length() - 1].at[k - (1 << (k.bit_length() - 1))] if k else own_ref
        columns = pl.ds(pl.multiple_of((me ^ k) * width, width), width)
        exits.append(pltpu.make_async_copy(exit_ref.at[:, columns], to, exit_sems.at[k]))
        exits[k].start()
    gain_copy.wait()
    gain = gain_out_ref[...]
    high = gain.astype(BF16)
    rows_ref[...] = jnp.zeros_like(rows_ref)
    rows_ref[0:1, :] = high
    rows_ref[16:17, :] = (gain - high.astype(F32)).astype(BF16)
    for c in range(parts):
        for copy in copies[c]:
            copy.wait()
        span = pl.ds(c * chunk, chunk)
        part = jnp.dot(rows_ref[:, span], weights_ref[span, :], preferred_element_type=F32)
        part = part[0:8, :] + part[16:24, :]
        if c == 0:
            sums_ref[...] = part
        else:
            sums_ref[...] += part
    for copy in exits:
        copy.wait()


def prepare(mp, heads, gain, probe, lookup, content, exit_matrix):
    depth, cols = probe.shape
    deep, wide = exit_matrix.shape
    parts = 4
    groups = mp.bit_length() - 1
    out_shape = [
        pltpu.VMEM((depth, 3 * cols), BF16),
        pltpu.VMEM((8, 3 * cols), F32),
        pltpu.VMEM((1, depth), F32),
        pltpu.VMEM((deep, wide // mp), BF16),
    ] + [pltpu.VMEM((1 << i, deep, wide // mp), BF16) for i in range(groups)]
    weights, sums, gain, own, *far = pl.pallas_call(
        functools.partial(prepare_kernel, mp, heads),
        out_shape=out_shape,
        in_specs=[HBM] * 5,
        out_specs=[VMEM] * len(out_shape),
        scratch_shapes=[
            pltpu.VMEM((32, depth), BF16),
            pltpu.SemaphoreType.DMA((parts, 1 + 2 * heads)),
            pltpu.SemaphoreType.DMA,
            pltpu.SemaphoreType.DMA((mp,)),
        ],
        compiler_params=PARAMS,
        cost_estimate=pl.CostEstimate(
            flops=16 * depth * 3 * cols, bytes_accessed=18 * depth * cols, transcendentals=0
        ),
        name="prepare",
    )(
        *(
            pltpu.with_memory_space_constraint(w, pltpu.HBM)
            for w in (gain[None, :], probe, lookup, content, exit_matrix)
        )
    )
    return weights, sums, gain, own, far


def scaled_blocks(blocks, shift, gain_ref):
    me = lax.axis_index("mp")
    found = []
    for k, block in enumerate(blocks):
        width = block.shape[1]
        gain = gain_ref[0:1, pl.ds(pl.multiple_of((me ^ k) * width, width), width)]
        found.append(((block[...].astype(F32) - shift) * gain).astype(BF16))
    return found


def matmul(blocks, weights_ref, start, width):
    me = lax.axis_index("mp")
    total = None
    for k, block in enumerate(blocks):
        depth = block.shape[1]
        w = weights_ref[pl.ds(pl.multiple_of((me ^ k) * depth, depth), depth), pl.ds(start, width)]
        part = jnp.dot(block[...], w, preferred_element_type=F32)
        total = part if total is None else total + part
    return total


def first_kernel(count, start, *refs):
    blocks = refs[:count]
    weights_ref, sums_ref, gain_ref, out_ref, offset_ref, scale_ref, *scaled_refs = refs[count:]
    rows, width = blocks[0].shape
    depth = count * width
    shift = jnp.mean(blocks[0][...].astype(F32), axis=1, keepdims=True)
    scaled = scaled_blocks(blocks, shift, gain_ref)
    for value, ref in zip(scaled, scaled_refs):
        ref[...] = value
    total = matmul(scaled, weights_ref, start, out_ref.shape[1])
    one = jnp.zeros((rows, 1), F32)
    two = jnp.zeros((rows, 1), F32)
    for block in blocks:
        moved = block[...].astype(F32) - shift
        one += jnp.sum(moved, axis=1, keepdims=True)
        two += jnp.sum(moved * moved, axis=1, keepdims=True)
    offset = one / depth
    scale = lax.rsqrt(two / depth - offset * offset + 1e-05)
    out_ref[...] = (scale * (total - offset * sums_ref[0:1, pl.ds(start, out_ref.shape[1])])).astype(BF16)
    offset_ref[...] = jnp.broadcast_to(offset, offset_ref.shape)
    scale_ref[...] = jnp.broadcast_to(scale, scale_ref.shape)


def query_kernel(count, cols, *refs):
    blocks = refs[:count]
    weights_ref, sums_ref, offset_ref, scale_ref, factor_ref, q_ref = refs[count:]
    total = matmul(blocks, weights_ref, 0, cols)
    total -= offset_ref[:, 0:1] * sums_ref[0:1, 0:cols]
    q_ref[...] = (scale_ref[:, 0:1] * factor_ref[...] * total).astype(BF16)


def project(blocks, weights, sums, gain, factor):
    rows, width = blocks[0].shape
    cols = weights.shape[1] // 3
    pairs, offset, scale, *scaled = pl.pallas_call(
        functools.partial(first_kernel, len(blocks), cols),
        out_shape=[
            pltpu.VMEM((rows, 2 * cols), BF16),
            pltpu.VMEM((rows, LANES), F32),
            pltpu.VMEM((rows, LANES), F32),
        ]
        + [pltpu.VMEM(b.shape, BF16) for b in blocks],
        in_specs=[VMEM] * (len(blocks) + 3),
        out_specs=[VMEM] * (3 + len(blocks)),
        compiler_params=PARAMS,
        name="keys_values",
    )(*blocks, weights, sums, gain)
    queries = pl.pallas_call(
        functools.partial(query_kernel, len(blocks), cols),
        out_shape=pltpu.VMEM((rows, cols), BF16),
        in_specs=[VMEM] * (len(blocks) + 5),
        out_specs=VMEM,
        compiler_params=PARAMS,
        cost_estimate=pl.CostEstimate(
            flops=16 * rows * weights.size, bytes_accessed=4 * weights.size, transcendentals=0
        ),
        name="queries",
    )(*scaled, weights, sums, offset, scale, factor)
    return queries, pairs


def attend_kernel(count, heads, q_ref, *refs):
    blocks, out_ref = refs[:count], refs[count]
    for h in range(heads):
        q = q_ref[:, pl.ds(h * LANES, LANES)]
        key, value = pl.ds(2 * h * LANES, LANES), pl.ds((2 * h + 1) * LANES, LANES)
        scores = [
            lax.dot_general(q, b[:, key], (((1,), (1,)), ((), ())), preferred_element_type=F32)
            for b in blocks
        ]
        top = functools.reduce(jnp.maximum, [jnp.max(s, axis=1, keepdims=True) for s in scores])
        total, weighted = 0.0, 0.0
        for s, b in zip(scores, blocks):
            weights = jnp.exp2(s - top)
            total += jnp.sum(weights, axis=1, keepdims=True)
            weighted += jnp.dot(weights.astype(BF16), b[:, value], preferred_element_type=F32)
        out_ref[:, pl.ds(h * LANES, LANES)] = (weighted / total).astype(BF16)


def attend(heads, queries, blocks):
    if len(blocks) > 8:
        merged = jnp.concatenate(blocks, axis=0)
        blocks = [merged[i : i + 1024] for i in range(0, merged.shape[0], 1024)]
    return pl.pallas_call(
        functools.partial(attend_kernel, len(blocks), heads),
        out_shape=pltpu.VMEM(queries.shape, BF16),
        in_specs=[VMEM] * (len(blocks) + 1),
        out_specs=VMEM,
        compiler_params=pltpu.CompilerParams(vmem_limit_bytes=(48 if len(blocks) > 4 else 16) << 20),
        name="attend",
    )(queries, *blocks)


def finish_kernel(count, x_ref, *refs):
    mixed, exits, out_ref = refs[:count], refs[count:-1], refs[-1]
    total = x_ref[...].astype(F32)
    for value, e in zip(mixed, exits):
        total += jnp.dot(value[...], e[...], preferred_element_type=F32)
    out_ref[...] = total.astype(out_ref.dtype)


def per_device(mesh, node_vectors, gain, probe, lookup, content, softness, exit_matrix):
    mp, seq = mesh.shape["mp"], mesh.shape["seq"]
    heads = softness.shape[0]
    cols = probe.shape[1]
    span = cols // heads
    factor = jnp.repeat(softness * (math.log2(math.e) / math.sqrt(span)), span)[None, :]

    weights, sums, gains, own, far = prepare(mp, heads, gain, probe, lookup, content, exit_matrix)
    blocks = {0: node_vectors}
    distance = mp // 2
    while distance:
        new = {k ^ distance: swap(b, "mp", mp, distance) for k, b in blocks.items()}
        if distance == mp // 2:
            new, sums = lax.optimization_barrier((new, sums))
        blocks.update(new)
        distance //= 2
    blocks = [blocks[k] for k in range(mp)]

    queries, pairs = project(blocks, weights, sums, gains, factor)
    found = {0: pairs}
    distance = seq // 2
    while distance:
        new = {}
        for k, b in found.items():
            if k == 0 and distance < seq // 2:
                b = after(b, queries)
            new[k ^ distance] = swap(b, "seq", seq, distance)
        found.update(new)
        distance //= 2
    attended = attend(heads, queries, [found[k] for k in range(seq)])

    pieces, pending = {0: own}, {1 << i: [(0, f)] for i, f in enumerate(far)}
    distance = mp // 2
    while distance:
        for r, stack in pending[distance]:
            if distance < mp // 2:
                stack = after(stack, attended)
            moved = swap(stack, "mp", mp, distance)
            pieces[r ^ distance] = moved[0]
            low = 1
            while low < distance:
                pending[low].append((r ^ distance, moved[low : 2 * low]))
                low *= 2
        distance //= 2

    mixed = {k: swap(attended, "mp", mp, k) if k else attended for k in range(mp)}
    return pl.pallas_call(
        functools.partial(finish_kernel, mp),
        out_shape=jax.ShapeDtypeStruct(node_vectors.shape, node_vectors.dtype),
        in_specs=[VMEM] * (1 + 2 * mp),
        out_specs=VMEM,
        compiler_params=PARAMS,
        name="finish",
    )(node_vectors, *(mixed[k] for k in range(mp)), *(pieces[k] for k in range(mp)))


def solution(mesh):
    return jax.shard_map(
        lambda *arrays: per_device(mesh, *arrays),
        mesh=mesh,
        in_specs=(
            P(("groups", "seq"), "mp"),
            P(),
            P(None, "mp"),
            P(None, "mp"),
            P(None, "mp"),
            P("mp"),
            P("mp", None),
        ),
        out_specs=P(("groups", "seq"), "mp"),
        check_vma=False,
    )
```

time: 35.6 us -> 31.4 us (0.88)
  blocking collectives: 8.95 us -> 0 us
  Pallas kernels: 0 us -> 5.82 us
  starting transfers between devices: 6.53 us -> 10.6 us
  matrix products: 2.1 us -> 0 us
  local copies, waits for them, and re-layouts: 2.14 us -> 0.11 us
  other arithmetic: 1.48 us -> 0.01 us
  waiting for transfers between devices: 14 us -> 14.7 us
    all_gather x1 -> x0, blocking collectives: 8.95 us -> none  [per_device(): full_rows = lax.all_gather(node_vectors, 'mp', axis=1, tiled=True)]
    pallas_call x0 -> x5, Pallas kernels: none -> 5.82 us  [the longest x1 3.06 us: prepare(): pl.pallas_call(functools.partial(prepare_kernel, mp, heads), out_shape=ou...]
    ppermute x6 -> x12, starting transfers between devices: 6.53 us -> 10.6 us  [swap(): return lax.ppermute(block, axis, [(i, i ^ distance) for i in range(count)])]
    dot_general x6 -> x0, matrix products: 2.1 us -> none  [the longest x1 0.37 us: per_device(): jnp.dot(normed, probe, preferred_element_type=jnp.float32)]
    unnamed x15 -> x4, local copies, waits for them, and re-layouts: 1.96 us -> 0.01 us
    convert_element_type x2 -> x0, other arithmetic: 0.75 us -> none  [the longest x1 0.72 us: per_device(): return (node_vectors.astype(jnp.float32) + shares[0]).astype(jnp.bfloat16)]
    reduce_sum x3 -> x0, other arithmetic: 0.67 us -> none  [the longest x1 0.29 us: per_device(): variance = jnp.mean(centered * centered, axis=-1, keepdims=True)]
    ppermute x6 -> x12, waiting for transfers between devices: 14 us -> 14.7 us  [swap(): return lax.ppermute(block, axis, [(i, i ^ distance) for i in range(count)])]
  transfers between devices with their start and end apart: 6 -> 12, of which waited for: 4 -> 7; matrix products, arithmetic and copies ran while one was open for 1% -> 0% of each run, Pallas kernels for 0% -> 13%
where the time goes in v2:
time: 31.4 us; the launch traced here: 31.3 us
  waiting for transfers between devices  14.7 us (47%)
  starting transfers between devices  10.6 us (34%)
  Pallas kernels  5.82 us (19%)
    ppermute x12, waiting for transfers between devices, swap(): return lax.ppermute(block, axis, [(i, i ^ distance) for i in range(count)])  14.7 us
    ppermute x12, starting transfers between devices, swap(): return lax.ppermute(block, axis, [(i, i ^ distance) for i in range(count)])  10.6 us
    pallas_call x1, Pallas kernels, prepare(): pl.pallas_call(functools.partial(prepare_kernel, mp, heads), out_shape=ou...  3.06 us
    pallas_call x1, Pallas kernels, per_device(): pl.pallas_call(functools.partial(finish_kernel, mp), out_shape=jax.ShapeD...  0.97 us
    pallas_call x1, Pallas kernels, attend(): pl.pallas_call(functools.partial(attend_kernel, len(blocks), heads), out_...  0.81 us
    pallas_call x1, Pallas kernels, project(): pl.pallas_call(functools.partial(first_kernel, len(blocks), cols), out_sh...  0.66 us
  transfers between devices with their start and end apart: 12, of which 7 were waited for; matrix products, arithmetic and copies ran while one was open for 0% of the time, Pallas kernels for 13%

profile of v2, /device:TPU:0, one launch (start us, length us, event | category | flops | bytes accessed | tf_op | source)
XLA Modules:
  0.0 31.3 jit_solution(8363220357759015762)
XLA Ops:
  0.0 0.0 copy-start
  0.0 0.0 copy-start.1
  0.0 2.9 %collective-permute-start.1 = (bf16[128,512]{1,0:T(8,128)(2,1)}, bf16[128,512]{1,0:T(8,128)(2,1)S(1)}, u32[]{:S(2)}, u32[]{:S(2)}) collective-permute-start(bf16[128,512]{1,0:T(8,128)(2,1)} %x_ref.1), channel_id=1, source_target_pairs={{0,2},{1,3},{2,0},{3,1},{4,6},{5,7},{6,4},{7,5},{8,10},{9,11},{10,... | collective-permute-start | bytes 393224 | tf_op jit(solution)/shard_map/ppermute | solution.py:19
  2.9 0.0 collective-permute-start
  2.9 3.1 %prepare.1 = (bf16[2048,768]{1,0:T(8,128)(2,1)S(1)}, f32[8,768]{1,0:T(8,128)S(1)}, f32[1,2048]{1,0:T(1,128)S(1)}, bf16[256,512]{1,0:T(8,128)(2,1)S(1)}, bf16[1,2...) custom-call(f32[1,2048]{1,0:T(1,128)} %bitcast.9, bf16[2048,256]{1,0:T(8,128)(2,1)} %probe_ref.1, ...), custom_call_target="tpu_custom_call" | custom-call | flops 25165824 | bytes 9437184 | tf_op jit(solution)/shard_map/prepare/pallas_call | solution.py:89
  6.0 0.1 collective-permute-start.10
  6.2 0.5 %collective-permute-done.1.refs_2_ = bf16[128,512]{1,0:T(8,128)(2,1)S(1)} collective-permute-done((bf16[128,512]{1,0:T(8,128)(2,1)}, bf16[128,512]{1,0:T(8,128)(2,1)S(1)}, u32[]{:S(2)}, u32[]{:S(2)}) %collective-permute-start.1) | collective-permute-done | bytes 131104 | tf_op jit(solution)/shard_map/ppermute | solution.py:19
  6.7 0.0 collective-permute-start.2
  6.7 0.0 copy-done.1
  6.7 0.0 collective-permute-done.refs_1_
  6.7 1.3 %collective-permute-done.2.refs_3_ = bf16[128,512]{1,0:T(8,128)(2,1)S(1)} collective-permute-done((bf16[128,512]{1,0:T(8,128)(2,1)S(1)}, bf16[128,512]{1,0:T(8,128)(2,1)S(1)}, u32[]{:S(2)}, u32[]{:S(2)}) %collective-permute-start.2) | collective-permute-done | bytes 131104 | tf_op jit(solution)/shard_map/ppermute | solution.py:19
  8.1 0.0 copy-done
  8.1 0.7 %keys_values.1 = (bf16[128,512]{1,0:T(8,128)(2,1)S(1)}, f32[128,128]{1,0:T(8,128)S(1)}, f32[128,128]{1,0:T(8,128)S(1)}, bf16[128,512]{1,0:T(8,128)(2,1)S(1)}, bf...) custom-call(bf16[128,512]{1,0:T(8,128)(2,1)S(1)} %copy-done, ...), custom_call_target="tpu_custom_call" | custom-call | tf_op jit(solution)/shard_map/keys_values/pallas_call | solution.py:169
  8.7 2.8 %collective-permute-start.4 = (bf16[128,512]{1,0:T(8,128)(2,1)S(1)}, bf16[128,512]{1,0:T(8,128)(2,1)S(1)}, u32[]{:S(2)}, u32[]{:S(2)}) collective-permute-start(bf16[128,512]{1,0:T(8,128)(2,1)S(1)} %get-tuple-element.35.refs_0_), channel_id=1, source_target_pairs={{0,8},{4,12},{8,0},{12,4},{1,9},{5,13},{9,1},{13,5},{2,10},{6,14},... | collective-permute-start | bytes 393224 | tf_op jit(solution)/shard_map/ppermute | solution.py:19
  11.6 0.1 broadcast_in_dim.7
  11.6 0.3 queries.1.q_ref
  12.0 1.6 %collective-permute-start.3 = (bf16[128,512]{1,0:T(8,128)(2,1)S(1)}, bf16[128,512]{1,0:T(8,128)(2,1)S(1)}, u32[]{:S(2)}, u32[]{:S(2)}) collective-permute-start(bf16[128,512]{1,0:T(8,128)(2,1)S(1)} %get-tuple-element.35.refs_0_), channel_id=1, source_target_pairs={{0,4},{4,0},{8,12},{12,8},{1,5},{5,1},{9,13},{13,9},{2,6},{6,2},{1... | collective-permute-start | bytes 393224 | tf_op jit(solution)/shard_map/ppermute | solution.py:19
  13.6 4.7 %collective-permute-done.4.refs_2_ = bf16[128,512]{1,0:T(8,128)(2,1)S(1)} collective-permute-done((bf16[128,512]{1,0:T(8,128)(2,1)S(1)}, bf16[128,512]{1,0:T(8,128)(2,1)S(1)}, u32[]{:S(2)}, u32[]{:S(2)}) %collective-permute-start.4) | collective-permute-done | bytes 131104 | tf_op jit(solution)/shard_map/ppermute | solution.py:19
  18.3 0.6 %collective-permute-start.5 = (bf16[128,512]{1,0:T(8,128)(2,1)S(1)}, bf16[128,512]{1,0:T(8,128)(2,1)S(1)}, u32[]{:S(2)}, u32[]{:S(2)}) collective-permute-start(bf16[128,512]{1,0:T(8,128)(2,1)S(1)} %collective-permute-done.4.refs_2_), channel_id=1, source_target_pairs={{0,4},{4,0},{8,12},{12,8},{1,5},{5,1},{9,13},{13,9},{2,6},{6,2},{1... | collective-permute-start | bytes 393224 | tf_op jit(solution)/shard_map/ppermute | solution.py:19
  18.9 1.5 %collective-permute-done.10 = bf16[2,256,512]{2,1,0:T(8,128)(2,1)S(1)} collective-permute-done((bf16[2,256,512]{2,1,0:T(8,128)(2,1)S(1)}, bf16[2,256,512]{2,1,0:T(8,128)(2,1)S(1)}, u32[]{:S(2)}, u32[]{:S(2)}) %collective-permute-start.10) | collective-permute-done | bytes 524320 | tf_op jit(solution)/shard_map/ppermute | solution.py:19
  20.5 0.0 collective-permute-done.3.refs_1_
  20.5 2.8 %collective-permute-done.5.refs_3_ = bf16[128,512]{1,0:T(8,128)(2,1)S(1)} collective-permute-done((bf16[128,512]{1,0:T(8,128)(2,1)S(1)}, bf16[128,512]{1,0:T(8,128)(2,1)S(1)}, u32[]{:S(2)}, u32[]{:S(2)}) %collective-permute-start.5) | collective-permute-done | bytes 131104 | tf_op jit(solution)/shard_map/ppermute | solution.py:19
  23.3 0.8 %attend.1.refs_0_ = bf16[128,256]{1,0:T(8,128)(2,1)S(1)} custom-call(bf16[128,256]{1,0:T(8,128)(2,1)S(1)} %queries.1.q_ref, bf16[128,512]{1,0:T(8,128)(2,1)S(1)} %get-tuple-element.35.refs_0_, bf16[128,512]{1,0:T(8,128)(2,1)S(1)} %collective-permute-done.3.refs_1_, bf16[128,512]{1,0:T(8,128)(2,1)S(1)} %collective-permute-done.4.refs_2_, ...), custom_call_target="tpu_custom_call" | custom-call | tf_op jit(solution)/shard_map/attend/pallas_call | solution.py:218
  24.1 0.1 collective-permute-start.11
  24.2 0.5 %collective-permute-start.9 = (bf16[1,256,512]{2,1,0:T(8,128)(2,1)S(1)}, bf16[1,256,512]{2,1,0:T(8,128)(2,1)S(1)}, u32[]{:S(2)}, u32[]{:S(2)}) collective-permute-start(bf16[1,256,512]{2,1,0:T(8,128)(2,1)S(1)} %get-tuple-element.38), channel_id=1, source_target_pairs={{0,1},{1,0},{2,3},{3,2},{4,5},{5,4},{6,7},{7,6},{8,9},{9,8},{10,11... | collective-permute-start | bytes 786440 | tf_op jit(solution)/shard_map/ppermute | solution.py:19
  24.7 0.1 collective-permute-start.6
  24.7 1.5 %collective-permute-start.7 = (bf16[128,256]{1,0:T(8,128)(2,1)S(1)}, bf16[128,256]{1,0:T(8,128)(2,1)S(1)}, u32[]{:S(2)}, u32[]{:S(2)}) collective-permute-start(bf16[128,256]{1,0:T(8,128)(2,1)S(1)} %attend.1.refs_0_), channel_id=1, source_target_pairs={{0,2},{1,3},{2,0},{3,1},{4,6},{5,7},{6,4},{7,5},{8,10},{9,11},{10,... | collective-permute-start | bytes 196616 | tf_op jit(solution)/shard_map/ppermute | solution.py:19
  26.3 0.3 collective-permute-start.8
  26.5 0.0 collective-permute-done.6.refs_1_
  26.5 2.6 %collective-permute-done.7.refs_2_ = bf16[128,256]{1,0:T(8,128)(2,1)S(1)} collective-permute-done((bf16[128,256]{1,0:T(8,128)(2,1)S(1)}, bf16[128,256]{1,0:T(8,128)(2,1)S(1)}, u32[]{:S(2)}, u32[]{:S(2)}) %collective-permute-start.7) | collective-permute-done | bytes 65568 | tf_op jit(solution)/shard_map/ppermute | solution.py:19
  29.2 1.1 %collective-permute-done.8.refs_3_ = bf16[128,256]{1,0:T(8,128)(2,1)S(1)} collective-permute-done((bf16[128,256]{1,0:T(8,128)(2,1)S(1)}, bf16[128,256]{1,0:T(8,128)(2,1)S(1)}, u32[]{:S(2)}, u32[]{:S(2)}) %collective-permute-start.8) | collective-permute-done | bytes 65568 | tf_op jit(solution)/shard_map/ppermute | solution.py:19
  30.3 0.0 collective-permute-done.11
  30.3 0.0 collective-permute-done.9
  30.3 1.0 %finish.1 = bf16[128,512]{1,0:T(8,128)(2,1)} custom-call(bf16[128,512]{1,0:T(8,128)(2,1)S(1)} %copy-done, bf16[128,256]{1,0:T(8,128)(2,1)S(1)} %attend.1.refs_0_, bf16[128,256]{1,0:T(8,128)(2,1)S(1)} %collective-permute-done.6.refs_1_, bf16[128,256]{1,0:T(8,128)(2,1)S(1)} %collective-permute-done.7.refs_2_, ...), custom_call_target="tpu_custom_call" | custom-call | tf_op jit(solution)/shard_map/finish/pallas_call | solution.py:282
  (2 shorter events, 0.0 us)
Async XLA Ops:
  0.0 8.1 %copy-start = (bf16[128,512]{1,0:T(8,128)(2,1)S(1)}, bf16[128,512]{1,0:T(8,128)(2,1)}, u32[]{:S(2)}) copy-start(bf16[128,512]{1,0:T(8,128)(2,1)} %x_ref.1) | copy-start | bytes 393220
  0.0 6.7 %copy-start.1 = (f32[2]{0:T(128)S(1)}, f32[2]{0:T(128)}, u32[]{:S(2)}) copy-start(f32[2]{0:T(128)} %param.12) | copy-start | bytes 28
  0.0 6.7 %collective-permute-start.1 = (bf16[128,512]{1,0:T(8,128)(2,1)}, bf16[128,512]{1,0:T(8,128)(2,1)S(1)}, u32[]{:S(2)}, u32[]{:S(2)}) collective-permute-start(bf16[128,512]{1,0:T(8,128)(2,1)} %x_ref.1), channel_id=1, source_target_pairs={{0,2},{1,3},{2,0},{3,1},{4,6},{5,7},{6,4},{7,5},{8,10},{9,11},{10,... | collective-permute-start | bytes 393224 | tf_op jit(solution)/shard_map/ppermute | solution.py:19
  2.9 3.8 %collective-permute-start = (bf16[128,512]{1,0:T(8,128)(2,1)}, bf16[128,512]{1,0:T(8,128)(2,1)S(1)}, u32[]{:S(2)}, u32[]{:S(2)}) collective-permute-start(bf16[128,512]{1,0:T(8,128)(2,1)} %x_ref.1), channel_id=1, source_target_pairs={{0,1},{1,0},{2,3},{3,2},{4,5},{5,4},{6,7},{7,6},{8,9},{9,8},{10,11... | collective-permute-start | bytes 393224 | tf_op jit(solution)/shard_map/ppermute | solution.py:19
  6.0 14.4 %collective-permute-start.10 = (bf16[2,256,512]{2,1,0:T(8,128)(2,1)S(1)}, bf16[2,256,512]{2,1,0:T(8,128)(2,1)S(1)}, u32[]{:S(2)}, u32[]{:S(2)}) collective-permute-start(bf16[2,256,512]{2,1,0:T(8,128)(2,1)S(1)} %get-tuple-element.39), channel_id=1, source_target_pairs={{0,2},{1,3},{2,0},{3,1},{4,6},{5,7},{6,4},{7,5},{8,10},{9,11},{10,... | collective-permute-start | bytes 1572872 | tf_op jit(solution)/shard_map/ppermute | solution.py:19
  6.7 1.3 %collective-permute-start.2 = (bf16[128,512]{1,0:T(8,128)(2,1)S(1)}, bf16[128,512]{1,0:T(8,128)(2,1)S(1)}, u32[]{:S(2)}, u32[]{:S(2)}) collective-permute-start(bf16[128,512]{1,0:T(8,128)(2,1)S(1)} %collective-permute-done.1.refs_2_), channel_id=1, source_target_pairs={{0,1},{1,0},{2,3},{3,2},{4,5},{5,4},{6,7},{7,6},{8,9},{9,8},{10,11... | collective-permute-start | bytes 393224 | tf_op jit(solution)/shard_map/ppermute | solution.py:19
  8.7 9.6 %collective-permute-start.4 = (bf16[128,512]{1,0:T(8,128)(2,1)S(1)}, bf16[128,512]{1,0:T(8,128)(2,1)S(1)}, u32[]{:S(2)}, u32[]{:S(2)}) collective-permute-start(bf16[128,512]{1,0:T(8,128)(2,1)S(1)} %get-tuple-element.35.refs_0_), channel_id=1, source_target_pairs={{0,8},{4,12},{8,0},{12,4},{1,9},{5,13},{9,1},{13,5},{2,10},{6,14},... | collective-permute-start | bytes 393224 | tf_op jit(solution)/shard_map/ppermute | solution.py:19
  12.0 8.5 %collective-permute-start.3 = (bf16[128,512]{1,0:T(8,128)(2,1)S(1)}, bf16[128,512]{1,0:T(8,128)(2,1)S(1)}, u32[]{:S(2)}, u32[]{:S(2)}) collective-permute-start(bf16[128,512]{1,0:T(8,128)(2,1)S(1)} %get-tuple-element.35.refs_0_), channel_id=1, source_target_pairs={{0,4},{4,0},{8,12},{12,8},{1,5},{5,1},{9,13},{13,9},{2,6},{6,2},{1... | collective-permute-start | bytes 393224 | tf_op jit(solution)/shard_map/ppermute | solution.py:19
  18.3 5.0 %collective-permute-start.5 = (bf16[128,512]{1,0:T(8,128)(2,1)S(1)}, bf16[128,512]{1,0:T(8,128)(2,1)S(1)}, u32[]{:S(2)}, u32[]{:S(2)}) collective-permute-start(bf16[128,512]{1,0:T(8,128)(2,1)S(1)} %collective-permute-done.4.refs_2_), channel_id=1, source_target_pairs={{0,4},{4,0},{8,12},{12,8},{1,5},{5,1},{9,13},{13,9},{2,6},{6,2},{1... | collective-permute-start | bytes 393224 | tf_op jit(solution)/shard_map/ppermute | solution.py:19
  24.1 6.2 %collective-permute-start.11 = (bf16[1,256,512]{2,1,0:T(8,128)(2,1)S(1)}, bf16[1,256,512]{2,1,0:T(8,128)(2,1)S(1)}, u32[]{:S(2)}, u32[]{:S(2)}) collective-permute-start(bf16[1,256,512]{2,1,0:T(8,128)(2,1)S(1)} %get-tuple-element.40), channel_id=1, source_target_pairs={{0,1},{1,0},{2,3},{3,2},{4,5},{5,4},{6,7},{7,6},{8,9},{9,8},{10,11... | collective-permute-start | bytes 786440 | tf_op jit(solution)/shard_map/ppermute | solution.py:19
  24.2 6.2 %collective-permute-start.9 = (bf16[1,256,512]{2,1,0:T(8,128)(2,1)S(1)}, bf16[1,256,512]{2,1,0:T(8,128)(2,1)S(1)}, u32[]{:S(2)}, u32[]{:S(2)}) collective-permute-start(bf16[1,256,512]{2,1,0:T(8,128)(2,1)S(1)} %get-tuple-element.38), channel_id=1, source_target_pairs={{0,1},{1,0},{2,3},{3,2},{4,5},{5,4},{6,7},{7,6},{8,9},{9,8},{10,11... | collective-permute-start | bytes 786440 | tf_op jit(solution)/shard_map/ppermute | solution.py:19
  24.7 1.9 %collective-permute-start.6 = (bf16[128,256]{1,0:T(8,128)(2,1)S(1)}, bf16[128,256]{1,0:T(8,128)(2,1)S(1)}, u32[]{:S(2)}, u32[]{:S(2)}) collective-permute-start(bf16[128,256]{1,0:T(8,128)(2,1)S(1)} %attend.1.refs_0_), channel_id=1, source_target_pairs={{0,1},{1,0},{2,3},{3,2},{4,5},{5,4},{6,7},{7,6},{8,9},{9,8},{10,11... | collective-permute-start | bytes 196616 | tf_op jit(solution)/shard_map/ppermute | solution.py:19
  24.7 4.4 %collective-permute-start.7 = (bf16[128,256]{1,0:T(8,128)(2,1)S(1)}, bf16[128,256]{1,0:T(8,128)(2,1)S(1)}, u32[]{:S(2)}, u32[]{:S(2)}) collective-permute-start(bf16[128,256]{1,0:T(8,128)(2,1)S(1)} %attend.1.refs_0_), channel_id=1, source_target_pairs={{0,2},{1,3},{2,0},{3,1},{4,6},{5,7},{6,4},{7,5},{8,10},{9,11},{10,... | collective-permute-start | bytes 196616 | tf_op jit(solution)/shard_map/ppermute | solution.py:19
  26.3 4.0 %collective-permute-start.8 = (bf16[128,256]{1,0:T(8,128)(2,1)S(1)}, bf16[128,256]{1,0:T(8,128)(2,1)S(1)}, u32[]{:S(2)}, u32[]{:S(2)}) collective-permute-start(bf16[128,256]{1,0:T(8,128)(2,1)S(1)} %attend.1.refs_0_), channel_id=1, source_target_pairs={{0,3},{1,2},{2,1},{3,0},{4,7},{5,6},{6,5},{7,4},{8,11},{9,10},{10,... | collective-permute-start | bytes 196616 | tf_op jit(solution)/shard_map/ppermute | solution.py:19

commit v3 on v1

v3 whole, which is shorter than its diff:
```python
import functools
import math

import jax
import jax.numpy as jnp
from jax import lax
from jax.experimental import pallas as pl
from jax.experimental.pallas import tpu as pltpu
from jax.sharding import PartitionSpec as P

F32, BF16 = jnp.float32, jnp.bfloat16
VMEM = pl.BlockSpec(memory_space=pltpu.VMEM)
HBM = pl.BlockSpec(memory_space=pltpu.HBM)
LANES = 128


def call(kernel, name, out_shape, operands, work=0, limit=16, specs=None, scratch=()):
    return pl.pallas_call(
        kernel,
        out_shape=out_shape,
        in_specs=specs or [VMEM] * len(operands),
        out_specs=[VMEM] * len(out_shape),
        scratch_shapes=scratch,
        compiler_params=pltpu.CompilerParams(vmem_limit_bytes=limit << 20),
        cost_estimate=pl.CostEstimate(flops=work, bytes_accessed=work // 64, transcendentals=0),
        name=name,
    )(*operands)


def swap(block, axis, count, distance):
    return lax.ppermute(block, axis, [(i, i ^ distance) for i in range(count)])


def after(value, *others):
    return lax.optimization_barrier((value, *others))[0]


def prepare_kernel(mp, gain_ref, probe_ref, lookup_ref, content_ref, exit_ref, *refs):
    weight_refs, (sums_ref, gain_out_ref, own_ref, far_ref) = refs[:3], refs[3:7]
    rows_ref, sems, gain_sem, exit_sems = refs[7:]
    me = lax.axis_index("mp")
    depth, cols = probe_ref.shape
    parts = sems.shape[0]
    chunk = depth // parts
    gain_copy = pltpu.make_async_copy(gain_ref, gain_out_ref, gain_sem)
    gain_copy.start()
    copies = []
    for c in range(parts):
        rows = pl.ds(c * chunk, chunk)
        copies.append([])
        for i, ref in enumerate((probe_ref, lookup_ref, content_ref)):
            copy = pltpu.make_async_copy(ref.at[rows, :], weight_refs[i].at[rows, :], sems.at[c, i])
            copy.start()
            copies[c].append(copy)
    half, _, width = own_ref.shape
    exits = []
    for k in range(mp):
        to = own_ref.at[k] if k < half else far_ref.at[k - half]
        columns = pl.ds(pl.multiple_of((me ^ k) * width, width), width)
        exits.append(pltpu.make_async_copy(exit_ref.at[:, columns], to, exit_sems.at[k]))
        exits[k].start()
    gain_copy.wait()
    gain = gain_out_ref[...]
    high = gain.astype(BF16)
    rows_ref[...] = jnp.zeros_like(rows_ref)
    rows_ref[0:1, :] = high
    rows_ref[16:17, :] = (gain - high.astype(F32)).astype(BF16)
    for c in range(parts):
        for copy in copies[c]:
            copy.wait()
        span = pl.ds(c * chunk, chunk)
        for i, ref in enumerate(weight_refs):
            part = jnp.dot(rows_ref[:, span], ref[span, :], preferred_element_type=F32)
            part = part[0:8, :] + part[16:24, :]
            if c == 0:
                sums_ref[i] = part
            else:
                sums_ref[i] += part
    for copy in exits:
        copy.wait()


def prepare(mp, gain, probe, lookup, content, exit_matrix):
    depth, cols = probe.shape
    deep, wide = exit_matrix.shape
    parts = 4
    stack = pltpu.VMEM((mp // 2, deep, wide // mp), BF16)
    probe, lookup, content, sums, gain, own, far = call(
        functools.partial(prepare_kernel, mp),
        "prepare",
        [pltpu.VMEM((depth, cols), BF16)] * 3
        + [pltpu.VMEM((3, 8, cols), F32), pltpu.VMEM((1, depth), F32), stack, stack],
        [
            pltpu.with_memory_space_constraint(w, pltpu.HBM)
            for w in (gain[None, :], probe, lookup, content, exit_matrix)
        ],
        work=48 * depth * cols,
        specs=[HBM] * 5,
        scratch=[
            pltpu.VMEM((32, depth), BF16),
            pltpu.SemaphoreType.DMA((parts, 3)),
            pltpu.SemaphoreType.DMA,
            pltpu.SemaphoreType.DMA((mp,)),
        ],
    )
    return (probe, lookup, content), sums, gain, own, far


def matmul(blocks, places, weight_ref):
    me = lax.axis_index("mp")
    total = None
    for k, block in zip(places, blocks):
        depth = block.shape[1]
        w = weight_ref[pl.ds(pl.multiple_of((me ^ k) * depth, depth), depth), :]
        part = jnp.dot(block[...], w, preferred_element_type=F32)
        total = part if total is None else total + part
    return total


def take_in(blocks, places, shift, gain_ref, scaled_refs, weight_refs):
    me = lax.axis_index("mp")
    one, two, scaled = 0.0, 0.0, []
    for k, block, ref in zip(places, blocks, scaled_refs):
        width = block.shape[1]
        gain = gain_ref[0:1, pl.ds(pl.multiple_of((me ^ k) * width, width), width)]
        moved = block[...].astype(F32) - shift
        value = (moved * gain).astype(BF16)
        ref[...] = value
        scaled.append(value)
        one += jnp.sum(moved, axis=1, keepdims=True)
        two += jnp.sum(moved * moved, axis=1, keepdims=True)
    return one, two, [matmul(scaled, places, ref) for ref in weight_refs]


def early_kernel(places, *refs):
    count = len(places)
    blocks = refs[:count]
    lookup_ref, content_ref, gain_ref, stats_ref, keys_ref, values_ref = refs[count : count + 6]
    scaled_refs = refs[count + 6 :]
    shift = jnp.mean(blocks[0][...].astype(F32), axis=1, keepdims=True)
    one, two, (keys, values) = take_in(
        blocks, places, shift, gain_ref, scaled_refs, (lookup_ref, content_ref)
    )
    keys_ref[...] = keys
    values_ref[...] = values
    for i, value in enumerate((shift, one, two)):
        stats_ref[i] = jnp.broadcast_to(value, stats_ref.shape[1:])


def late_kernel(places, depth, *refs):
    count = len(places)
    blocks = refs[:count]
    lookup_ref, content_ref, gain_ref, sums_ref, stats_ref, keys_ref, values_ref = refs[count : count + 7]
    out_ref, final_ref, *scaled_refs = refs[count + 7 :]
    one, two, products = take_in(
        blocks, places, stats_ref[0, :, 0:1], gain_ref, scaled_refs, (lookup_ref, content_ref)
    )
    offset = (one + stats_ref[1, :, 0:1]) / depth
    scale = lax.rsqrt((two + stats_ref[2, :, 0:1]) / depth - offset * offset + 1e-05)
    for i, (product, ref) in enumerate(zip(products, (keys_ref, values_ref))):
        product = product + ref[...]
        product = (scale * (product - offset * sums_ref[i + 1, 0:1, :])).astype(BF16)
        for h in range(product.shape[1] // LANES):
            out_ref[:, pl.ds((2 * h + i) * LANES, LANES)] = product[:, h * LANES : (h + 1) * LANES]
    final_ref[0] = jnp.broadcast_to(offset, final_ref.shape[1:])
    final_ref[1] = jnp.broadcast_to(scale, final_ref.shape[1:])


def query_kernel(count, *refs):
    blocks = refs[:count]
    probe_ref, sums_ref, final_ref, factor_ref, q_ref = refs[count:]
    total = matmul(blocks, range(count), probe_ref) - final_ref[0, :, 0:1] * sums_ref[0, 0:1, :]
    q_ref[...] = (final_ref[1, :, 0:1] * factor_ref[...] * total).astype(BF16)


def project(blocks, weights, sums, gain, factor):
    rows, width = blocks[0].shape
    probe, lookup, content = weights
    cols = probe.shape[1]
    count = len(blocks)
    product = pltpu.VMEM((rows, cols), F32)
    block = pltpu.VMEM((rows, width), BF16)
    stats, keys, values, *scaled = call(
        functools.partial(early_kernel, range(count - 1)),
        "early",
        [pltpu.VMEM((3, rows, LANES), F32), product, product] + [block] * (count - 1),
        [*blocks[:-1], lookup, content, gain],
        work=16 * rows * probe.size,
    )
    pairs, final, last = call(
        functools.partial(late_kernel, range(count - 1, count), count * width),
        "late",
        [pltpu.VMEM((rows, 2 * cols), BF16), pltpu.VMEM((2, rows, LANES), F32), block],
        [blocks[-1], lookup, content, gain, sums, stats, keys, values],
    )
    (queries,) = call(
        functools.partial(query_kernel, count),
        "queries",
        [pltpu.VMEM((rows, cols), BF16)],
        [*scaled, last, probe, sums, final, factor],
        work=4 * rows * probe.size,
    )
    return queries, pairs


def attend_kernel(count, heads, q_ref, *refs):
    blocks, out_ref = refs[:count], refs[count]
    scores, tops, totals, weighted = [], [], [], []
    for h in range(heads):
        q = q_ref[:, pl.ds(h * LANES, LANES)]
        scores.append(
            [
                lax.dot_general(
                    q, b[:, pl.ds(2 * h * LANES, LANES)], (((1,), (1,)), ((), ())), preferred_element_type=F32
                )
                for b in blocks
            ]
        )
    for parts in scores:
        widest = functools.reduce(jnp.maximum, parts)
        tops.append(jnp.max(widest, axis=1, keepdims=True))
    weights = [[jnp.exp2(s - top) for s in parts] for parts, top in zip(scores, tops)]
    for h in range(heads):
        weighted.append(
            sum(
                jnp.dot(
                    w.astype(BF16), b[:, pl.ds((2 * h + 1) * LANES, LANES)], preferred_element_type=F32
                )
                for w, b in zip(weights[h], blocks)
            )
        )
        totals.append(jnp.sum(functools.reduce(jnp.add, weights[h]), axis=1, keepdims=True))
    for h in range(heads):
        out_ref[:, pl.ds(h * LANES, LANES)] = (weighted[h] / totals[h]).astype(BF16)


def attend(heads, queries, blocks):
    if len(blocks) > 8:
        merged = jnp.concatenate(blocks, axis=0)
        size = math.gcd(merged.shape[0], 1024)
        blocks = [merged[i : i + size] for i in range(0, merged.shape[0], size)]
    size = sum(b.shape[0] for b in blocks)
    (out,) = call(
        functools.partial(attend_kernel, len(blocks), heads),
        "attend",
        [pltpu.VMEM(queries.shape, BF16)],
        [queries, *blocks],
        limit=48 if size > 2048 else 16,
    )
    return out


def own_kernel(x_ref, mixed_ref, exit_ref, *out_refs):
    for k, ref in enumerate(out_refs):
        part = jnp.dot(mixed_ref[...], exit_ref[k], preferred_element_type=F32)
        ref[...] = part + x_ref[...].astype(F32) if k == 0 else part


def add_kernel(mixed_ref, exit_ref, *refs):
    count = len(refs) // 2
    for k in range(count):
        part = jnp.dot(mixed_ref[...], exit_ref[k], preferred_element_type=F32)
        refs[count + k][...] = (refs[k][...] + part).astype(refs[count + k].dtype)


def per_device(mesh, node_vectors, gain, probe, lookup, content, softness, exit_matrix):
    mp, seq = mesh.shape["mp"], mesh.shape["seq"]
    heads = softness.shape[0]
    cols = probe.shape[1]
    span = cols // heads
    top = mp // 2
    factor = jnp.repeat(softness * (math.log2(math.e) / math.sqrt(span)), span)[None, :]

    weights, sums, gains, own, far = prepare(mp, gain, probe, lookup, content, exit_matrix)
    blocks = {0: node_vectors}
    distance = top
    while distance:
        new = {k ^ distance: swap(b, "mp", mp, distance) for k, b in blocks.items()}
        if distance == top:
            new, sums = lax.optimization_barrier((new, sums))
        blocks.update(new)
        distance //= 2
    queries, pairs = project([blocks[k] for k in range(mp)], weights, sums, gains, factor)
    theirs = swap(far, "mp", mp, top)

    found = {0: pairs}
    distance = seq // 2
    while distance:
        new = {}
        for k, b in found.items():
            if k == 0 and distance < seq // 2:
                b = after(b, queries)
            new[k ^ distance] = swap(b, "seq", seq, distance)
        found.update(new)
        distance //= 2
    mixed = attend(heads, after(queries, theirs), [found[k] for k in range(seq)])

    rows, width = node_vectors.shape
    product, half = pltpu.VMEM((rows, width), F32), pltpu.VMEM((rows, width), BF16)
    mixed_far = swap(mixed, "mp", mp, top)
    parts = call(
        own_kernel, "own", [product] * top, [node_vectors, mixed, own], work=64 * rows * own.size
    )
    sent = call(add_kernel, "sent", [half] * (top - 1), [mixed_far, theirs[1:], *parts[1:]])
    (kept,) = call(
        add_kernel, "kept", [product], [mixed_far, theirs[:1], parts[0]], work=64 * rows * own.size
    )
    shares = {0: kept, **{k: sent[k - 1] for k in range(1, top)}}
    distance = 1
    while distance < top:
        shares = {
            k: shares[k].astype(F32)
            + swap(shares[k ^ distance].astype(BF16), "mp", mp, distance).astype(F32)
            for k in shares
            if not k & distance
        }
        distance *= 2
    return shares[0].astype(node_vectors.dtype)


def solution(mesh):
    return jax.shard_map(
        lambda *arrays: per_device(mesh, *arrays),
        mesh=mesh,
        in_specs=(
            P(("groups", "seq"), "mp"),
            P(),
            P(None, "mp"),
            P(None, "mp"),
            P(None, "mp"),
            P("mp"),
            P("mp", None),
        ),
        out_specs=P(("groups", "seq"), "mp"),
        check_vma=False,
    )
```

time: 35.6 us -> 30.3 us (0.85)
  blocking collectives: 8.95 us -> 0 us
  Pallas kernels: 0 us -> 5.26 us
  starting transfers between devices: 6.53 us -> 9.92 us
  matrix products: 2.1 us -> 0 us
  local copies, waits for them, and re-layouts: 2.14 us -> 0.12 us
  other arithmetic: 1.48 us -> 0.68 us
    all_gather x1 -> x0, blocking collectives: 8.95 us -> none  [per_device(): full_rows = lax.all_gather(node_vectors, 'mp', axis=1, tiled=True)]
    pallas_call x0 -> x8, Pallas kernels: none -> 5.26 us  [call(): pl.pallas_call(kernel, out_shape=out_shape, in_specs=specs or [VMEM] * le...]
    ppermute x6 -> x9, starting transfers between devices: 6.53 us -> 9.92 us  [swap(): return lax.ppermute(block, axis, [(i, i ^ distance) for i in range(count)])]
    dot_general x6 -> x0, matrix products: 2.1 us -> none  [the longest x1 0.37 us: per_device(): jnp.dot(normed, probe, preferred_element_type=jnp.float32)]
    unnamed x15 -> x4, local copies, waits for them, and re-layouts: 1.96 us -> 0.01 us
    reduce_sum x3 -> x0, other arithmetic: 0.67 us -> none  [the longest x1 0.29 us: per_device(): variance = jnp.mean(centered * centered, axis=-1, keepdims=True)]
    ppermute x6 -> x9, waiting for transfers between devices: 14 us -> 14.1 us  [swap(): return lax.ppermute(block, axis, [(i, i ^ distance) for i in range(count)])]
    convert_element_type x2 -> x1, other arithmetic: 0.75 us -> 0.68 us  [per_device(): return shares[0].astype(node_vectors.dtype)]
  transfers between devices with their start and end apart: 6 -> 9, of which waited for: 4 -> 7; matrix products, arithmetic and copies ran while one was open for 1% -> 0% of each run, Pallas kernels for 0% -> 15%
where the time goes in v3:
time: 30.3 us; the launch traced here: 30.2 us
  waiting for transfers between devices  14.1 us (47%)
  starting transfers between devices  9.92 us (33%)
  Pallas kernels  5.26 us (17%)
  other arithmetic  0.68 us (2%)
    ppermute x9, waiting for transfers between devices, swap(): return lax.ppermute(block, axis, [(i, i ^ distance) for i in range(count)])  14.1 us
    ppermute x9, starting transfers between devices, swap(): return lax.ppermute(block, axis, [(i, i ^ distance) for i in range(count)])  9.92 us
    pallas_call x8, Pallas kernels, call(): pl.pallas_call(kernel, out_shape=out_shape, in_specs=specs or [VMEM] * le...  5.26 us
    convert_element_type x1, other arithmetic, per_device(): return shares[0].astype(node_vectors.dtype)  0.68 us
  transfers between devices with their start and end apart: 9, of which 7 were waited for; matrix products, arithmetic and copies ran while one was open for 0% of the time, Pallas kernels for 15%

profile of v3, /device:TPU:0, one launch (start us, length us, event | category | flops | bytes accessed | tf_op | source)
XLA Modules:
  0.0 30.2 jit_solution(8576940580927694469)
XLA Ops:
  0.0 2.9 %collective-permute-start.1 = (bf16[128,512]{1,0:T(8,128)(2,1)}, bf16[128,512]{1,0:T(8,128)(2,1)S(1)}, u32[]{:S(2)}, u32[]{:S(2)}) collective-permute-start(bf16[128,512]{1,0:T(8,128)(2,1)} %x_ref.1), channel_id=1, source_target_pairs={{0,2},{1,3},{2,0},{3,1},{4,6},{5,7},{6,4},{7,5},{8,10},{9,11},{10,... | collective-permute-start | bytes 393224 | tf_op jit(solution)/shard_map/ppermute | solution.py:31
  2.9 0.0 collective-permute-start
  2.9 0.0 copy-start
  2.9 2.9 %prepare.1 = (bf16[2048,256]{1,0:T(8,128)(2,1)S(1)}, bf16[2048,256]{1,0:T(8,128)(2,1)S(1)}, bf16[2048,256]{1,0:T(8,128)(2,1)S(1)}, f32[3,8,256]{2,1,0:T(8,128)S(...) custom-call(f32[1,2048]{1,0:T(1,128)} %bitcast.3, ...), custom_call_target="tpu_custom_call" | custom-call | flops 25165824 | bytes 393216 | tf_op jit(solution)/shard_map/prepare/pallas_call | solution.py:18
  5.9 0.1 collective-permute-start.3
  6.0 0.7 %collective-permute-done.1.refs_2_ = bf16[128,512]{1,0:T(8,128)(2,1)S(1)} collective-permute-done((bf16[128,512]{1,0:T(8,128)(2,1)}, bf16[128,512]{1,0:T(8,128)(2,1)S(1)}, u32[]{:S(2)}, u32[]{:S(2)}) %collective-permute-start.1) | collective-permute-done | bytes 131104 | tf_op jit(solution)/shard_map/ppermute | solution.py:31
  6.6 0.0 collective-permute-start.2
  6.6 0.0 collective-permute-done.refs_1_
  6.7 0.0 copy-done
  6.7 0.5 %early.1 = (f32[3,128,128]{2,1,0:T(8,128)S(1)}, f32[128,256]{1,0:T(8,128)S(1)}, f32[128,256]{1,0:T(8,128)S(1)}, bf16[128,512]{1,0:T(8,128)(2,1)S(1)}, bf16[128,5...) custom-call(bf16[128,512]{1,0:T(8,128)(2,1)S(1)} %copy-done, bf16[128,512]{1,0:T(8,128)(2,1)S(1)} %collective-permute-done.refs_1_, ...), custom_call_target="tpu_custom_call" | custom-call | flops 1073741824 | bytes 16777216 | tf_op jit(solution)/shard_map/early/pallas_call | solution.py:18
  7.2 0.8 %collective-permute-done.2.refs_0_ = bf16[128,512]{1,0:T(8,128)(2,1)S(1)} collective-permute-done((bf16[128,512]{1,0:T(8,128)(2,1)S(1)}, bf16[128,512]{1,0:T(8,128)(2,1)S(1)}, u32[]{:S(2)}, u32[]{:S(2)}) %collective-permute-start.2) | collective-permute-done | bytes 131104 | tf_op jit(solution)/shard_map/ppermute | solution.py:31
  8.0 0.3 %late.1 = (bf16[128,512]{1,0:T(8,128)(2,1)S(1)}, f32[2,128,128]{2,1,0:T(8,128)S(1)}, bf16[128,512]{1,0:T(8,128)(2,1)S(1)}) custom-call(bf16[128,512]{1,0:T(8,128)(2,1)S(1)} %collective-permute-done.2.refs_0_, bf16[2048,256]{1,0:T(8,128)(2,1)S(1)} %get-tuple-element.29.refs_3_.refs_1_, bf16[2048,256]{1,0:T(8,128)(2,1)S(1)} %get-tuple-element.30.refs_4_.refs_2_, ...), custom_call_target="tpu_custom_call" | custom-call | tf_op jit(solution)/shard_map/late/pallas_call | solution.py:18
  8.3 0.0 copy-start.1
  8.3 2.9 %collective-permute-start.5 = (bf16[128,512]{1,0:T(8,128)(2,1)S(1)}, bf16[128,512]{1,0:T(8,128)(2,1)S(1)}, u32[]{:S(2)}, u32[]{:S(2)}) collective-permute-start(bf16[128,512]{1,0:T(8,128)(2,1)S(1)} %get-tuple-element.45.refs_0_), channel_id=1, source_target_pairs={{0,8},{4,12},{8,0},{12,4},{1,9},{5,13},{9,1},{13,5},{2,10},{6,14},... | collective-permute-start | bytes 393224 | tf_op jit(solution)/shard_map/ppermute | solution.py:31
  11.2 0.0 copy-done.1
  11.3 0.1 broadcast_in_dim.7
  11.3 0.3 %queries.1.q_ref = bf16[128,256]{1,0:T(8,128)(2,1)S(1)} custom-call(bf16[128,512]{1,0:T(8,128)(2,1)S(1)} %get-tuple-element.32.refs_0_, bf16[128,512]{1,0:T(8,128)(2,1)S(1)} %get-tuple-element.33.refs_1_, bf16[128,512]{1,0:T(8,128)(2,1)S(1)} %get-tuple-element.34.refs_2_, bf16[128,512]{1,0:T(8,128)(2,1)S(1)} %get-tuple-element.39.refs_3_, ...), custom_call_target="tpu_custom_call" | custom-call | flops 268435456 | bytes 4194304 | tf_op jit(solution)/shard_map/queries/pallas_call | solution.py:18
  11.6 1.6 %collective-permute-start.4 = (bf16[128,512]{1,0:T(8,128)(2,1)S(1)}, bf16[128,512]{1,0:T(8,128)(2,1)S(1)}, u32[]{:S(2)}, u32[]{:S(2)}) collective-permute-start(bf16[128,512]{1,0:T(8,128)(2,1)S(1)} %get-tuple-element.45.refs_0_), channel_id=1, source_target_pairs={{0,4},{4,0},{8,12},{12,8},{1,5},{5,1},{9,13},{13,9},{2,6},{6,2},{1... | collective-permute-start | bytes 393224 | tf_op jit(solution)/shard_map/ppermute | solution.py:31
  13.3 4.7 %collective-permute-done.5.refs_2_ = bf16[128,512]{1,0:T(8,128)(2,1)S(1)} collective-permute-done((bf16[128,512]{1,0:T(8,128)(2,1)S(1)}, bf16[128,512]{1,0:T(8,128)(2,1)S(1)}, u32[]{:S(2)}, u32[]{:S(2)}) %collective-permute-start.5) | collective-permute-done | bytes 131104 | tf_op jit(solution)/shard_map/ppermute | solution.py:31
  18.0 0.7 %collective-permute-start.6 = (bf16[128,512]{1,0:T(8,128)(2,1)S(1)}, bf16[128,512]{1,0:T(8,128)(2,1)S(1)}, u32[]{:S(2)}, u32[]{:S(2)}) collective-permute-start(bf16[128,512]{1,0:T(8,128)(2,1)S(1)} %collective-permute-done.5.refs_2_), channel_id=1, source_target_pairs={{0,4},{4,0},{8,12},{12,8},{1,5},{5,1},{9,13},{13,9},{2,6},{6,2},{1... | collective-permute-start | bytes 393224 | tf_op jit(solution)/shard_map/ppermute | solution.py:31
  18.6 1.6 %collective-permute-done.3 = bf16[2,256,512]{2,1,0:T(8,128)(2,1)S(1)} collective-permute-done((bf16[2,256,512]{2,1,0:T(8,128)(2,1)S(1)}, bf16[2,256,512]{2,1,0:T(8,128)(2,1)S(1)}, u32[]{:S(2)}, u32[]{:S(2)}) %collective-permute-start.3) | collective-permute-done | bytes 524320 | tf_op jit(solution)/shard_map/ppermute | solution.py:31
  20.3 0.0 collective-permute-done.4.refs_1_
  20.3 2.6 %collective-permute-done.6.refs_3_ = bf16[128,512]{1,0:T(8,128)(2,1)S(1)} collective-permute-done((bf16[128,512]{1,0:T(8,128)(2,1)S(1)}, bf16[128,512]{1,0:T(8,128)(2,1)S(1)}, u32[]{:S(2)}, u32[]{:S(2)}) %collective-permute-start.6) | collective-permute-done | bytes 131104 | tf_op jit(solution)/shard_map/ppermute | solution.py:31
  22.9 0.6 %attend.1.mixed_ref = bf16[128,256]{1,0:T(8,128)(2,1)S(1)} custom-call(bf16[128,256]{1,0:T(8,128)(2,1)S(1)} %queries.1.q_ref, bf16[128,512]{1,0:T(8,128)(2,1)S(1)} %get-tuple-element.45.refs_0_, bf16[128,512]{1,0:T(8,128)(2,1)S(1)} %collective-permute-done.4.refs_1_, bf16[128,512]{1,0:T(8,128)(2,1)S(1)} %collective-permute-done.5.refs_2_, ...), custom_call_target="tpu_custom_call" | custom-call | tf_op jit(solution)/shard_map/attend/pallas_call | solution.py:18
  23.5 1.6 %collective-permute-start.7 = (bf16[128,256]{1,0:T(8,128)(2,1)S(1)}, bf16[128,256]{1,0:T(8,128)(2,1)S(1)}, u32[]{:S(2)}, u32[]{:S(2)}) collective-permute-start(bf16[128,256]{1,0:T(8,128)(2,1)S(1)} %attend.1.mixed_ref), channel_id=1, source_target_pairs={{0,2},{1,3},{2,0},{3,1},{4,6},{5,7},{6,4},{7,5},{8,10},{9,11},{10,... | collective-permute-start | bytes 196616 | tf_op jit(solution)/shard_map/ppermute | solution.py:31
  25.2 0.2 own.1
  25.4 2.5 %collective-permute-done.7.mixed_ref = bf16[128,256]{1,0:T(8,128)(2,1)S(1)} collective-permute-done((bf16[128,256]{1,0:T(8,128)(2,1)S(1)}, bf16[128,256]{1,0:T(8,128)(2,1)S(1)}, u32[]{:S(2)}, u32[]{:S(2)}) %collective-permute-start.7) | collective-permute-done | bytes 65568 | tf_op jit(solution)/shard_map/ppermute | solution.py:31
  27.9 0.2 sent.1
  28.1 0.1 collective-permute-start.8
  28.1 0.2 kept.1
  28.3 1.1 %collective-permute-done.8 = bf16[128,512]{1,0:T(8,128)(2,1)S(1)} collective-permute-done((bf16[128,512]{1,0:T(8,128)(2,1)S(1)}, bf16[128,512]{1,0:T(8,128)(2,1)S(1)}, u32[]{:S(2)}, u32[]{:S(2)}) %collective-permute-start.8) | collective-permute-done | bytes 131104 | tf_op jit(solution)/shard_map/ppermute | solution.py:31
  29.5 0.7 %add_convert_fusion = bf16[128,512]{1,0:T(8,128)(2,1)} fusion(f32[128,512]{1,0:T(8,128)S(1)} %kept.1, bf16[128,512]{1,0:T(8,128)(2,1)S(1)} %collective-permute-done.8), kind=kLoop, calls=%fused_computation | loop fusion | flops 196608 | bytes 524288 | tf_op jit(solution)/shard_map/convert_element_type | solution.py:318
  (2 shorter events, 0.0 us)
Async XLA Ops:
  0.0 6.6 %collective-permute-start.1 = (bf16[128,512]{1,0:T(8,128)(2,1)}, bf16[128,512]{1,0:T(8,128)(2,1)S(1)}, u32[]{:S(2)}, u32[]{:S(2)}) collective-permute-start(bf16[128,512]{1,0:T(8,128)(2,1)} %x_ref.1), channel_id=1, source_target_pairs={{0,2},{1,3},{2,0},{3,1},{4,6},{5,7},{6,4},{7,5},{8,10},{9,11},{10,... | collective-permute-start | bytes 393224 | tf_op jit(solution)/shard_map/ppermute | solution.py:31
  2.9 3.7 %collective-permute-start = (bf16[128,512]{1,0:T(8,128)(2,1)}, bf16[128,512]{1,0:T(8,128)(2,1)S(1)}, u32[]{:S(2)}, u32[]{:S(2)}) collective-permute-start(bf16[128,512]{1,0:T(8,128)(2,1)} %x_ref.1), channel_id=1, source_target_pairs={{0,1},{1,0},{2,3},{3,2},{4,5},{5,4},{6,7},{7,6},{8,9},{9,8},{10,11... | collective-permute-start | bytes 393224 | tf_op jit(solution)/shard_map/ppermute | solution.py:31
  2.9 3.7 %copy-start = (bf16[128,512]{1,0:T(8,128)(2,1)S(1)}, bf16[128,512]{1,0:T(8,128)(2,1)}, u32[]{:S(2)}) copy-start(bf16[128,512]{1,0:T(8,128)(2,1)} %x_ref.1) | copy-start | bytes 393220
  5.9 14.4 %collective-permute-start.3 = (bf16[2,256,512]{2,1,0:T(8,128)(2,1)S(1)}, bf16[2,256,512]{2,1,0:T(8,128)(2,1)S(1)}, u32[]{:S(2)}, u32[]{:S(2)}) collective-permute-start(bf16[2,256,512]{2,1,0:T(8,128)(2,1)S(1)} %get-tuple-element.42), channel_id=1, source_target_pairs={{0,2},{1,3},{2,0},{3,1},{4,6},{5,7},{6,4},{7,5},{8,10},{9,11},{10,... | collective-permute-start | bytes 1572872 | tf_op jit(solution)/shard_map/ppermute | solution.py:31
  6.6 1.3 %collective-permute-start.2 = (bf16[128,512]{1,0:T(8,128)(2,1)S(1)}, bf16[128,512]{1,0:T(8,128)(2,1)S(1)}, u32[]{:S(2)}, u32[]{:S(2)}) collective-permute-start(bf16[128,512]{1,0:T(8,128)(2,1)S(1)} %collective-permute-done.1.refs_2_), channel_id=1, source_target_pairs={{0,1},{1,0},{2,3},{3,2},{4,5},{5,4},{6,7},{7,6},{8,9},{9,8},{10,11... | collective-permute-start | bytes 393224 | tf_op jit(solution)/shard_map/ppermute | solution.py:31
  8.3 2.9 %copy-start.1 = (f32[2]{0:T(128)S(1)}, f32[2]{0:T(128)}, u32[]{:S(2)}) copy-start(f32[2]{0:T(128)} %param.12) | copy-start | bytes 28
  8.3 9.6 %collective-permute-start.5 = (bf16[128,512]{1,0:T(8,128)(2,1)S(1)}, bf16[128,512]{1,0:T(8,128)(2,1)S(1)}, u32[]{:S(2)}, u32[]{:S(2)}) collective-permute-start(bf16[128,512]{1,0:T(8,128)(2,1)S(1)} %get-tuple-element.45.refs_0_), channel_id=1, source_target_pairs={{0,8},{4,12},{8,0},{12,4},{1,9},{5,13},{9,1},{13,5},{2,10},{6,14},... | collective-permute-start | bytes 393224 | tf_op jit(solution)/shard_map/ppermute | solution.py:31
  11.6 8.6 %collective-permute-start.4 = (bf16[128,512]{1,0:T(8,128)(2,1)S(1)}, bf16[128,512]{1,0:T(8,128)(2,1)S(1)}, u32[]{:S(2)}, u32[]{:S(2)}) collective-permute-start(bf16[128,512]{1,0:T(8,128)(2,1)S(1)} %get-tuple-element.45.refs_0_), channel_id=1, source_target_pairs={{0,4},{4,0},{8,12},{12,8},{1,5},{5,1},{9,13},{13,9},{2,6},{6,2},{1... | collective-permute-start | bytes 393224 | tf_op jit(solution)/shard_map/ppermute | solution.py:31
  18.0 5.0 %collective-permute-start.6 = (bf16[128,512]{1,0:T(8,128)(2,1)S(1)}, bf16[128,512]{1,0:T(8,128)(2,1)S(1)}, u32[]{:S(2)}, u32[]{:S(2)}) collective-permute-start(bf16[128,512]{1,0:T(8,128)(2,1)S(1)} %collective-permute-done.5.refs_2_), channel_id=1, source_target_pairs={{0,4},{4,0},{8,12},{12,8},{1,5},{5,1},{9,13},{13,9},{2,6},{6,2},{1... | collective-permute-start | bytes 393224 | tf_op jit(solution)/shard_map/ppermute | solution.py:31
  23.5 4.3 %collective-permute-start.7 = (bf16[128,256]{1,0:T(8,128)(2,1)S(1)}, bf16[128,256]{1,0:T(8,128)(2,1)S(1)}, u32[]{:S(2)}, u32[]{:S(2)}) collective-permute-start(bf16[128,256]{1,0:T(8,128)(2,1)S(1)} %attend.1.mixed_ref), channel_id=1, source_target_pairs={{0,2},{1,3},{2,0},{3,1},{4,6},{5,7},{6,4},{7,5},{8,10},{9,11},{10,... | collective-permute-start | bytes 196616 | tf_op jit(solution)/shard_map/ppermute | solution.py:31
  28.1 1.4 %collective-permute-start.8 = (bf16[128,512]{1,0:T(8,128)(2,1)S(1)}, bf16[128,512]{1,0:T(8,128)(2,1)S(1)}, u32[]{:S(2)}, u32[]{:S(2)}) collective-permute-start(bf16[128,512]{1,0:T(8,128)(2,1)S(1)} %sent.1), channel_id=1, source_target_pairs={{0,1},{1,0},{2,3},{3,2},{4,5},{5,4},{6,7},{7,6},{8,9},{9,8},{10,11... | collective-permute-start | bytes 393224 | tf_op jit(solution)/shard_map/ppermute | solution.py:31

commit v4 on v3

--- a/solution.py
+++ b/solution.py
@@ -147,30 +147,48 @@
         stats_ref[i] = jnp.broadcast_to(value, stats_ref.shape[1:])
 
 
+def parity():
+    return lax.rem(lax.axis_index("seq"), 2)
+
+
 def late_kernel(places, depth, *refs):
     count = len(places)
     blocks = refs[:count]
     lookup_ref, content_ref, gain_ref, sums_ref, stats_ref, keys_ref, values_ref = refs[count : count + 7]
-    out_ref, final_ref, *scaled_refs = refs[count + 7 :]
+    mine_ref, other_ref, final_ref, *scaled_refs = refs[count + 7 :]
     one, two, products = take_in(
         blocks, places, stats_ref[0, :, 0:1], gain_ref, scaled_refs, (lookup_ref, content_ref)
     )
     offset = (one + stats_ref[1, :, 0:1]) / depth
     scale = lax.rsqrt((two + stats_ref[2, :, 0:1]) / depth - offset * offset + 1e-05)
+    first = parity() == 0
     for i, (product, ref) in enumerate(zip(products, (keys_ref, values_ref))):
         product = product + ref[...]
-        product = (scale * (product - offset * sums_ref[i + 1, 0:1, :])).astype(BF16)
-        for h in range(product.shape[1] // LANES):
-            out_ref[:, pl.ds((2 * h + i) * LANES, LANES)] = product[:, h * LANES : (h + 1) * LANES]
+        product = scale * (product - offset * sums_ref[i + 1, 0:1, :])
+        half = product.shape[1] // 2
+        low, high = product[:, :half], product[:, half:]
+        for out_ref, part in (
+            (mine_ref, jnp.where(first, low, high)),
+            (other_ref, jnp.where(first, high, low)),
+        ):
+            part = part.astype(BF16)
+            for h in range(half // LANES):
+                out_ref[:, pl.ds((2 * h + i) * LANES, LANES)] = part[:, h * LANES : (h + 1) * LANES]
     final_ref[0] = jnp.broadcast_to(offset, final_ref.shape[1:])
     final_ref[1] = jnp.broadcast_to(scale, final_ref.shape[1:])
 
 
 def query_kernel(count, *refs):
     blocks = refs[:count]
-    probe_ref, sums_ref, final_ref, factor_ref, q_ref = refs[count:]
+    probe_ref, sums_ref, final_ref, factor_ref, other_ref, mine_ref, bundle_ref = refs[count:]
     total = matmul(blocks, range(count), probe_ref) - final_ref[0, :, 0:1] * sums_ref[0, 0:1, :]
-    q_ref[...] = (final_ref[1, :, 0:1] * factor_ref[...] * total).astype(BF16)
+    total = final_ref[1, :, 0:1] * factor_ref[...] * total
+    half = total.shape[1] // 2
+    low, high = total[:, :half], total[:, half:]
+    first = parity() == 0
+    mine_ref[...] = jnp.where(first, low, high).astype(BF16)
+    bundle_ref[:, pl.ds(0, 2 * half)] = other_ref[...]
+    bundle_ref[:, pl.ds(2 * half, half)] = jnp.where(first, high, low).astype(BF16)
 
 
 def project(blocks, weights, sums, gain, factor):
@@ -187,80 +205,95 @@
         [*blocks[:-1], lookup, content, gain],
         work=16 * rows * probe.size,
     )
-    pairs, final, last = call(
+    pair = pltpu.VMEM((rows, cols), BF16)
+    mine, other, final, last = call(
         functools.partial(late_kernel, range(count - 1, count), count * width),
         "late",
-        [pltpu.VMEM((rows, 2 * cols), BF16), pltpu.VMEM((2, rows, LANES), F32), block],
+        [pair, pair, pltpu.VMEM((2, rows, LANES), F32), block],
         [blocks[-1], lookup, content, gain, sums, stats, keys, values],
     )
-    (queries,) = call(
+    queries, bundle = call(
         functools.partial(query_kernel, count),
         "queries",
-        [pltpu.VMEM((rows, cols), BF16)],
-        [*scaled, last, probe, sums, final, factor],
-        work=4 * rows * probe.size,
-    )
-    return queries, pairs
-
-
-def attend_kernel(count, heads, q_ref, *refs):
-    blocks, out_ref = refs[:count], refs[count]
-    scores, tops, totals, weighted = [], [], [], []
-    for h in range(heads):
-        q = q_ref[:, pl.ds(h * LANES, LANES)]
-        scores.append(
-            [
-                lax.dot_general(
-                    q, b[:, pl.ds(2 * h * LANES, LANES)], (((1,), (1,)), ((), ())), preferred_element_type=F32
-                )
-                for b in blocks
-            ]
+        [pltpu.VMEM((rows, cols // 2), BF16), pltpu.VMEM((rows, 3 * cols // 2), BF16)],
+        [*scaled, last, probe, sums, final, factor, other],
+        work=16 * rows * probe.size,
+    )
+    return queries, mine, other, bundle
+
+
+def merge_kernel(*refs):
+    rows = refs[0].shape[0]
+    for i, ref in enumerate(refs[:-1]):
+        refs[-1][pl.ds(i * rows, rows), :] = ref[...]
+
+
+def attend_kernel(count, mine_ref, bundle_ref, *refs):
+    blocks, out_refs = refs[:count], refs[count:]
+    half = mine_ref.shape[1]
+    rows = mine_ref.shape[0]
+    for h in range(half // LANES):
+        q = jnp.concatenate(
+            [mine_ref[:, pl.ds(h * LANES, LANES)], bundle_ref[:, pl.ds(2 * half + h * LANES, LANES)]], axis=0
         )
-    for parts in scores:
-        widest = functools.reduce(jnp.maximum, parts)
-        tops.append(jnp.max(widest, axis=1, keepdims=True))
-    weights = [[jnp.exp2(s - top) for s in parts] for parts, top in zip(scores, tops)]
-    for h in range(heads):
-        weighted.append(
-            sum(
-                jnp.dot(
-                    w.astype(BF16), b[:, pl.ds((2 * h + 1) * LANES, LANES)], preferred_element_type=F32
-                )
-                for w, b in zip(weights[h], blocks)
+        scores = [
+            lax.dot_general(
+                q, b[:, pl.ds(2 * h * LANES, LANES)], (((1,), (1,)), ((), ())), preferred_element_type=F32
             )
+            for b in blocks
+        ]
+        top = functools.reduce(jnp.maximum, [jnp.max(s, axis=1, keepdims=True) for s in scores])
+        weights = [jnp.exp2(s - top) for s in scores]
+        weighted = sum(
+            jnp.dot(
+                w.astype(BF16), b[:, pl.ds((2 * h + 1) * LANES, LANES)], preferred_element_type=F32
+            )
+            for w, b in zip(weights, blocks)
         )
-        totals.append(jnp.sum(functools.reduce(jnp.add, weights[h]), axis=1, keepdims=True))
-    for h in range(heads):
-        out_ref[:, pl.ds(h * LANES, LANES)] = (weighted[h] / totals[h]).astype(BF16)
-
-
-def attend(heads, queries, blocks):
-    if len(blocks) > 8:
-        merged = jnp.concatenate(blocks, axis=0)
-        size = math.gcd(merged.shape[0], 1024)
-        blocks = [merged[i : i + size] for i in range(0, merged.shape[0], size)]
-    size = sum(b.shape[0] for b in blocks)
-    (out,) = call(
-        functools.partial(attend_kernel, len(blocks), heads),
+        total = sum(jnp.sum(w, axis=1, keepdims=True) for w in weights)
+        out = (weighted / total).astype(BF16)
+        for i, ref in enumerate(out_refs):
+            ref[:, pl.ds(h * LANES, LANES)] = out[i * rows : (i + 1) * rows, :]
+
+
+def attend(queries, bundle, blocks):
+    rows, wide = blocks[0].shape
+    (merged,) = call(
+        merge_kernel,
+        "merge",
+        [pltpu.VMEM((len(blocks) * rows, wide), BF16)],
+        blocks,
+        work=10000 * rows * wide * len(blocks),
+    )
+    size = merged.shape[0]
+    return call(
+        functools.partial(attend_kernel, 2),
         "attend",
-        [pltpu.VMEM(queries.shape, BF16)],
-        [queries, *blocks],
-        limit=48 if size > 2048 else 16,
-    )
-    return out
+        [pltpu.VMEM(queries.shape, BF16)] * 2,
+        [queries, bundle, bundle, merged],
+        limit=56 if size > 2048 else 16,
+    )
 
 
 def own_kernel(x_ref, mixed_ref, exit_ref, *out_refs):
+    deep = mixed_ref.shape[1]
+    rows = pl.ds(pl.multiple_of(parity() * deep, deep), deep)
     for k, ref in enumerate(out_refs):
-        part = jnp.dot(mixed_ref[...], exit_ref[k], preferred_element_type=F32)
+        part = jnp.dot(mixed_ref[...], exit_ref[k, rows, :], preferred_element_type=F32)
         ref[...] = part + x_ref[...].astype(F32) if k == 0 else part
 
 
-def add_kernel(mixed_ref, exit_ref, *refs):
-    count = len(refs) // 2
-    for k in range(count):
-        part = jnp.dot(mixed_ref[...], exit_ref[k], preferred_element_type=F32)
-        refs[count + k][...] = (refs[k][...] + part).astype(refs[count + k].dtype)
+def add_kernel(which, flips, *refs):
+    count, values = len(which), len(flips)
+    for i, k in enumerate(which):
+        total = refs[2 * values + i][...]
+        for j, flip in enumerate(flips):
+            deep = refs[j].shape[1]
+            at = 1 - parity() if flip else parity()
+            rows = pl.ds(pl.multiple_of(at * deep, deep), deep)
+            total += jnp.dot(refs[j][...], refs[values + j][k, rows, :], preferred_element_type=F32)
+        out_ref = refs[2 * values + count + i]
+        out_ref[...] = total.astype(out_ref.dtype)
 
 
 def per_device(mesh, node_vectors, gain, probe, lookup, content, softness, exit_matrix):
@@ -280,30 +313,41 @@
             new, sums = lax.optimization_barrier((new, sums))
         blocks.update(new)
         distance //= 2
-    queries, pairs = project([blocks[k] for k in range(mp)], weights, sums, gains, factor)
+    queries, mine, other, bundle = project(
+        [blocks[k] for k in range(mp)], weights, sums, gains, factor
+    )
     theirs = swap(far, "mp", mp, top)
 
-    found = {0: pairs}
-    distance = seq // 2
-    while distance:
-        new = {}
-        for k, b in found.items():
-            if k == 0 and distance < seq // 2:
-                b = after(b, queries)
-            new[k ^ distance] = swap(b, "seq", seq, distance)
-        found.update(new)
-        distance //= 2
-    mixed = attend(heads, after(queries, theirs), [found[k] for k in range(seq)])
+    found = {0: mine}
+    for k in sorted(range(1, seq), key=lambda k: (k == 1, k)):
+        found[k] = swap(bundle if k == 1 else other if k % 2 else mine, "seq", seq, k)
+    mixed, mixed_beside = attend(queries, found[1], [found[k] for k in range(seq) if k != 1])
 
     rows, width = node_vectors.shape
     product, half = pltpu.VMEM((rows, width), F32), pltpu.VMEM((rows, width), BF16)
-    mixed_far = swap(mixed, "mp", mp, top)
+    both = ("seq", "mp")
+    across = swap(mixed, both, seq * mp, top)
+    beside = swap(mixed_beside, both, seq * mp, mp)
+    corner = swap(mixed_beside, both, seq * mp, mp + top)
     parts = call(
-        own_kernel, "own", [product] * top, [node_vectors, mixed, own], work=64 * rows * own.size
-    )
-    sent = call(add_kernel, "sent", [half] * (top - 1), [mixed_far, theirs[1:], *parts[1:]])
+        own_kernel, "own", [product] * top, [node_vectors, mixed, own], work=1 * rows * own.size
+    )
+    parts = call(
+        functools.partial(add_kernel, range(top), (0, 1)),
+        "crossed",
+        [product] * top,
+        [across, corner, theirs, theirs, *parts],
+        work=64 * rows * own.size,
+    )
+    sent = call(
+        functools.partial(add_kernel, range(1, top), (1,)), "sent", [half] * (top - 1), [beside, own, *parts[1:]]
+    )
     (kept,) = call(
-        add_kernel, "kept", [product], [mixed_far, theirs[:1], parts[0]], work=64 * rows * own.size
+        functools.partial(add_kernel, range(1), (1,)),
+        "kept",
+        [product],
+        [beside, own, parts[0]],
+        work=64 * rows * own.size,
     )
     shares = {0: kept, **{k: sent[k - 1] for k in range(1, top)}}
     distance = 1

time: 30.3 us -> 28.6 us (0.944)
  waiting for transfers between devices: 14.1 us -> 10.9 us
  starting transfers between devices: 9.92 us -> 11.2 us
    ppermute x9 -> x11, waiting for transfers between devices: 14.1 us -> 10.9 us  [swap(): return lax.ppermute(block, axis, [(i, i ^ distance) for i in range(count)])]
    ppermute x9 -> x11, starting transfers between devices: 9.92 us -> 11.2 us  [swap(): return lax.ppermute(block, axis, [(i, i ^ distance) for i in range(count)])]
    pallas_call x8 -> x10, Pallas kernels: 5.26 us -> 5.45 us  [call(): pl.pallas_call(kernel, out_shape=out_shape, in_specs=specs or [VMEM] * le...]
  transfers between devices with their start and end apart: 9 -> 11, of which waited for: 7 -> 8; matrix products, arithmetic and copies ran while one was open for 0% -> 0% of each run, Pallas kernels for 15% -> 19%
where the time goes in v4:
time: 28.6 us; the launch traced here: 28.4 us
  starting transfers between devices  11.2 us (39%)
  waiting for transfers between devices  10.9 us (38%)
  Pallas kernels  5.45 us (19%)
  other arithmetic  0.69 us (2%)
    ppermute x11, starting transfers between devices, swap(): return lax.ppermute(block, axis, [(i, i ^ distance) for i in range(count)])  11.2 us
    ppermute x11, waiting for transfers between devices, swap(): return lax.ppermute(block, axis, [(i, i ^ distance) for i in range(count)])  10.9 us
    pallas_call x10, Pallas kernels, call(): pl.pallas_call(kernel, out_shape=out_shape, in_specs=specs or [VMEM] * le...  5.45 us
    convert_element_type x1, other arithmetic, per_device(): return shares[0].astype(node_vectors.dtype)  0.69 us
  transfers between devices with their start and end apart: 11, of which 8 were waited for; matrix products, arithmetic and copies ran while one was open for 0% of the time, Pallas kernels for 19%

profile of v4, /device:TPU:0, one launch (start us, length us, event | category | flops | bytes accessed | tf_op | source)
XLA Modules:
  0.0 28.4 jit_solution(8427521293842958106)
XLA Ops:
  0.0 2.9 %collective-permute-start.1 = (bf16[128,512]{1,0:T(8,128)(2,1)}, bf16[128,512]{1,0:T(8,128)(2,1)S(1)}, u32[]{:S(2)}, u32[]{:S(2)}) collective-permute-start(bf16[128,512]{1,0:T(8,128)(2,1)} %x_ref.1), channel_id=1, source_target_pairs={{0,2},{1,3},{2,0},{3,1},{4,6},{5,7},{6,4},{7,5},{8,10},{9,11},{10,... | collective-permute-start | bytes 393224 | tf_op jit(solution)/shard_map/ppermute | solution.py:31
  2.9 0.0 collective-permute-start
  2.9 0.0 copy-start
  2.9 2.9 %prepare.1 = (bf16[2048,256]{1,0:T(8,128)(2,1)S(1)}, bf16[2048,256]{1,0:T(8,128)(2,1)S(1)}, bf16[2048,256]{1,0:T(8,128)(2,1)S(1)}, f32[3,8,256]{2,1,0:T(8,128)S(...) custom-call(f32[1,2048]{1,0:T(1,128)} %bitcast.3, ...), custom_call_target="tpu_custom_call" | custom-call | flops 25165824 | bytes 393216 | tf_op jit(solution)/shard_map/prepare/pallas_call | solution.py:18
  5.9 0.0 copy-start.1
  5.9 0.1 collective-permute-start.9
  6.0 0.7 %collective-permute-done.1.refs_2_ = bf16[128,512]{1,0:T(8,128)(2,1)S(1)} collective-permute-done((bf16[128,512]{1,0:T(8,128)(2,1)}, bf16[128,512]{1,0:T(8,128)(2,1)S(1)}, u32[]{:S(2)}, u32[]{:S(2)}) %collective-permute-start.1) | collective-permute-done | bytes 131104 | tf_op jit(solution)/shard_map/ppermute | solution.py:31
  6.6 0.0 collective-permute-start.2
  6.6 0.0 copy-done.1
  6.7 0.0 collective-permute-done.refs_1_
  6.7 0.0 copy-done
  6.7 0.5 %early.1 = (f32[3,128,128]{2,1,0:T(8,128)S(1)}, f32[128,256]{1,0:T(8,128)S(1)}, f32[128,256]{1,0:T(8,128)S(1)}, bf16[128,512]{1,0:T(8,128)(2,1)S(1)}, bf16[128,5...) custom-call(bf16[128,512]{1,0:T(8,128)(2,1)S(1)} %copy-done, bf16[128,512]{1,0:T(8,128)(2,1)S(1)} %collective-permute-done.refs_1_, ...), custom_call_target="tpu_custom_call" | custom-call | flops 1073741824 | bytes 16777216 | tf_op jit(solution)/shard_map/early/pallas_call | solution.py:18
  7.2 0.8 %collective-permute-done.2.refs_0_ = bf16[128,512]{1,0:T(8,128)(2,1)S(1)} collective-permute-done((bf16[128,512]{1,0:T(8,128)(2,1)S(1)}, bf16[128,512]{1,0:T(8,128)(2,1)S(1)}, u32[]{:S(2)}, u32[]{:S(2)}) %collective-permute-start.2) | collective-permute-done | bytes 131104 | tf_op jit(solution)/shard_map/ppermute | solution.py:31
  8.0 0.3 %late.1 = (bf16[128,256]{1,0:T(8,128)(2,1)S(1)}, bf16[128,256]{1,0:T(8,128)(2,1)S(1)}, f32[2,128,128]{2,1,0:T(8,128)S(1)}, bf16[128,512]{1,0:T(8,128)(2,1)S(1)}) custom-call(bf16[128,512]{1,0:T(8,128)(2,1)S(1)} %collective-permute-done.2.refs_0_, bf16[2048,256]{1,0:T(8,128)(2,1)S(1)} %get-tuple-element.34.refs_3_.refs_1_, ...), custom_call_target="tpu_custom_call" | custom-call | tf_op jit(solution)/shard_map/late/pallas_call | solution.py:18
  8.3 2.9 %collective-permute-start.4 = (bf16[128,256]{1,0:T(8,128)(2,1)S(1)}, bf16[128,256]{1,0:T(8,128)(2,1)S(1)}, u32[]{:S(2)}, u32[]{:S(2)}) collective-permute-start(bf16[128,256]{1,0:T(8,128)(2,1)S(1)} %get-tuple-element.50.refs_0_), channel_id=1, source_target_pairs={{0,8},{4,12},{8,0},{12,4},{1,9},{5,13},{9,1},{13,5},{2,10},{6,14},... | collective-permute-start | bytes 196616 | tf_op jit(solution)/shard_map/ppermute | solution.py:31
  11.2 1.3 %collective-permute-start.5 = (bf16[128,256]{1,0:T(8,128)(2,1)S(1)}, bf16[128,256]{1,0:T(8,128)(2,1)S(1)}, u32[]{:S(2)}, u32[]{:S(2)}) collective-permute-start(bf16[128,256]{1,0:T(8,128)(2,1)S(1)} %get-tuple-element.47.refs_8_), channel_id=1, source_target_pairs={{0,12},{4,8},{8,4},{12,0},{1,13},{5,9},{9,5},{13,1},{2,14},{6,10},... | collective-permute-start | bytes 196616 | tf_op jit(solution)/shard_map/ppermute | solution.py:31
  12.6 0.1 broadcast_in_dim.7
  12.7 0.3 %queries.1 = (bf16[128,128]{1,0:T(8,128)(2,1)S(1)}, bf16[128,384]{1,0:T(8,128)(2,1)S(1)}) custom-call(bf16[128,512]{1,0:T(8,128)(2,1)S(1)} %get-tuple-element.37.refs_0_, bf16[128,512]{1,0:T(8,128)(2,1)S(1)} %get-tuple-element.38.refs_1_, bf16[128,512]{1,0:T(8,128)(2,1)S(1)} %get-tuple-element.39.refs_2_, bf16[128,512]{1,0:T(8,128)(2,1)S(1)} %get-tuple-element.44.refs_3_, ...), custom_call_target="tpu_custom_call" | custom-call | flops 1073741824 | bytes 16777216 | tf_op jit(solution)/shard_map/queries/pallas_call | solution.py:18
  13.0 0.3 %collective-permute-start.3 = (bf16[128,384]{1,0:T(8,128)(2,1)S(1)}, bf16[128,384]{1,0:T(8,128)(2,1)S(1)}, u32[]{:S(2)}, u32[]{:S(2)}) collective-permute-start(bf16[128,384]{1,0:T(8,128)(2,1)S(1)} %get-tuple-element.49), channel_id=1, source_target_pairs={{0,4},{4,0},{8,12},{12,8},{1,5},{5,1},{9,13},{13,9},{2,6},{6,2},{1... | collective-permute-start | bytes 294920 | tf_op jit(solution)/shard_map/ppermute | solution.py:31
  13.3 1.9 %collective-permute-done.4.refs_1_ = bf16[128,256]{1,0:T(8,128)(2,1)S(1)} collective-permute-done((bf16[128,256]{1,0:T(8,128)(2,1)S(1)}, bf16[128,256]{1,0:T(8,128)(2,1)S(1)}, u32[]{:S(2)}, u32[]{:S(2)}) %collective-permute-start.4) | collective-permute-done | bytes 65568 | tf_op jit(solution)/shard_map/ppermute | solution.py:31
  15.2 2.8 %collective-permute-done.5.refs_2_ = bf16[128,256]{1,0:T(8,128)(2,1)S(1)} collective-permute-done((bf16[128,256]{1,0:T(8,128)(2,1)S(1)}, bf16[128,256]{1,0:T(8,128)(2,1)S(1)}, u32[]{:S(2)}, u32[]{:S(2)}) %collective-permute-start.5) | collective-permute-done | bytes 65568 | tf_op jit(solution)/shard_map/ppermute | solution.py:31
  18.0 0.7 %collective-permute-done.3.bundle_ref.refs_0_ = bf16[128,384]{1,0:T(8,128)(2,1)S(1)} collective-permute-done((bf16[128,384]{1,0:T(8,128)(2,1)S(1)}, bf16[128,384]{1,0:T(8,128)(2,1)S(1)}, u32[]{:S(2)}, u32[]{:S(2)}) %collective-permute-start.3) | collective-permute-done | bytes 98336 | tf_op jit(solution)/shard_map/ppermute | solution.py:31
  18.8 0.5 %attend.1 = (bf16[128,128]{1,0:T(8,128)(2,1)S(1)}, bf16[128,128]{1,0:T(8,128)(2,1)S(1)}) custom-call(bf16[128,128]{1,0:T(8,128)(2,1)S(1)} %get-tuple-element.48.mine_ref, bf16[128,384]{1,0:T(8,128)(2,1)S(1)} %collective-permute-done.3.bundle_ref.refs_0_, bf16[128,384]{1,0:T(8,128)(2,1)S(1)} %collective-permute-done.3.bundle_ref.refs_0_, ...), custom_call_target="tpu_custom_call" | custom-call | tf_op jit(solution)/shard_map/attend/pallas_call | solution.py:18
  19.3 1.7 %collective-permute-start.7 = (bf16[128,128]{1,0:T(8,128)(2,1)S(1)}, bf16[128,128]{1,0:T(8,128)(2,1)S(1)}, u32[]{:S(2)}, u32[]{:S(2)}) collective-permute-start(bf16[128,128]{1,0:T(8,128)(2,1)S(1)} %get-tuple-element.53.mixed_ref), channel_id=1, source_target_pairs={{0,2},{1,3},{2,0},{3,1},{4,6},{5,7},{6,4},{7,5},{8,10},{9,11},{10,... | collective-permute-start | bytes 98312 | tf_op jit(solution)/shard_map/ppermute | solution.py:31
  21.0 0.0 collective-permute-start.8
  21.1 1.8 %collective-permute-start.6 = (bf16[128,128]{1,0:T(8,128)(2,1)S(1)}, bf16[128,128]{1,0:T(8,128)(2,1)S(1)}, u32[]{:S(2)}, u32[]{:S(2)}) collective-permute-start(bf16[128,128]{1,0:T(8,128)(2,1)S(1)} %get-tuple-element.51), channel_id=1, source_target_pairs={{0,4},{1,5},{2,6},{3,7},{4,0},{5,1},{6,2},{7,3},{8,12},{9,13},{10,... | collective-permute-start | bytes 98312 | tf_op jit(solution)/shard_map/ppermute | solution.py:31
  22.8 0.2 own.1
  23.1 0.2 collective-permute-done.7.refs_0_
  23.3 2.6 %collective-permute-done.8.refs_1_ = bf16[128,128]{1,0:T(8,128)(2,1)S(1)} collective-permute-done((bf16[128,128]{1,0:T(8,128)(2,1)S(1)}, bf16[128,128]{1,0:T(8,128)(2,1)S(1)}, u32[]{:S(2)}, u32[]{:S(2)}) %collective-permute-start.8) | collective-permute-done | bytes 32800 | tf_op jit(solution)/shard_map/ppermute | solution.py:31
  25.8 0.0 collective-permute-done.9.refs_2_.refs_3_
  25.8 0.3 crossed.1
  26.1 0.0 collective-permute-done.6.refs_0_
  26.1 0.2 sent.1
  26.3 0.1 collective-permute-start.10
  26.4 0.2 kept.1
  26.6 1.1 %collective-permute-done.10 = bf16[128,512]{1,0:T(8,128)(2,1)S(1)} collective-permute-done((bf16[128,512]{1,0:T(8,128)(2,1)S(1)}, bf16[128,512]{1,0:T(8,128)(2,1)S(1)}, u32[]{:S(2)}, u32[]{:S(2)}) %collective-permute-start.10) | collective-permute-done | bytes 131104 | tf_op jit(solution)/shard_map/ppermute | solution.py:31
  27.7 0.7 %add_convert_fusion = bf16[128,512]{1,0:T(8,128)(2,1)} fusion(f32[128,512]{1,0:T(8,128)S(1)} %kept.1, bf16[128,512]{1,0:T(8,128)(2,1)S(1)} %collective-permute-done.10), kind=kLoop, calls=%fused_computation | loop fusion | flops 196608 | bytes 524288 | tf_op jit(solution)/shard_map/convert_element_type | solution.py:362
  (2 shorter events, 0.0 us)
Async XLA Ops:
  0.0 6.6 %collective-permute-start.1 = (bf16[128,512]{1,0:T(8,128)(2,1)}, bf16[128,512]{1,0:T(8,128)(2,1)S(1)}, u32[]{:S(2)}, u32[]{:S(2)}) collective-permute-start(bf16[128,512]{1,0:T(8,128)(2,1)} %x_ref.1), channel_id=1, source_target_pairs={{0,2},{1,3},{2,0},{3,1},{4,6},{5,7},{6,4},{7,5},{8,10},{9,11},{10,... | collective-permute-start | bytes 393224 | tf_op jit(solution)/shard_map/ppermute | solution.py:31
  2.9 3.7 %collective-permute-start = (bf16[128,512]{1,0:T(8,128)(2,1)}, bf16[128,512]{1,0:T(8,128)(2,1)S(1)}, u32[]{:S(2)}, u32[]{:S(2)}) collective-permute-start(bf16[128,512]{1,0:T(8,128)(2,1)} %x_ref.1), channel_id=1, source_target_pairs={{0,1},{1,0},{2,3},{3,2},{4,5},{5,4},{6,7},{7,6},{8,9},{9,8},{10,11... | collective-permute-start | bytes 393224 | tf_op jit(solution)/shard_map/ppermute | solution.py:31
  2.9 3.7 %copy-start = (bf16[128,512]{1,0:T(8,128)(2,1)S(1)}, bf16[128,512]{1,0:T(8,128)(2,1)}, u32[]{:S(2)}) copy-start(bf16[128,512]{1,0:T(8,128)(2,1)} %x_ref.1) | copy-start | bytes 393220
  5.9 0.8 %copy-start.1 = (f32[2]{0:T(128)S(1)}, f32[2]{0:T(128)}, u32[]{:S(2)}) copy-start(f32[2]{0:T(128)} %param.12) | copy-start | bytes 28
  5.9 19.9 %collective-permute-start.9 = (bf16[2,256,512]{2,1,0:T(8,128)(2,1)S(1)}, bf16[2,256,512]{2,1,0:T(8,128)(2,1)S(1)}, u32[]{:S(2)}, u32[]{:S(2)}) collective-permute-start(bf16[2,256,512]{2,1,0:T(8,128)(2,1)S(1)} %get-tuple-element.54), channel_id=1, source_target_pairs={{0,2},{1,3},{2,0},{3,1},{4,6},{5,7},{6,4},{7,5},{8,10},{9,11},{10,... | collective-permute-start | bytes 1572872 | tf_op jit(solution)/shard_map/ppermute | solution.py:31
  6.6 1.3 %collective-permute-start.2 = (bf16[128,512]{1,0:T(8,128)(2,1)S(1)}, bf16[128,512]{1,0:T(8,128)(2,1)S(1)}, u32[]{:S(2)}, u32[]{:S(2)}) collective-permute-start(bf16[128,512]{1,0:T(8,128)(2,1)S(1)} %collective-permute-done.1.refs_2_), channel_id=1, source_target_pairs={{0,1},{1,0},{2,3},{3,2},{4,5},{5,4},{6,7},{7,6},{8,9},{9,8},{10,11... | collective-permute-start | bytes 393224 | tf_op jit(solution)/shard_map/ppermute | solution.py:31
  8.3 6.9 %collective-permute-start.4 = (bf16[128,256]{1,0:T(8,128)(2,1)S(1)}, bf16[128,256]{1,0:T(8,128)(2,1)S(1)}, u32[]{:S(2)}, u32[]{:S(2)}) collective-permute-start(bf16[128,256]{1,0:T(8,128)(2,1)S(1)} %get-tuple-element.50.refs_0_), channel_id=1, source_target_pairs={{0,8},{4,12},{8,0},{12,4},{1,9},{5,13},{9,1},{13,5},{2,10},{6,14},... | collective-permute-start | bytes 196616 | tf_op jit(solution)/shard_map/ppermute | solution.py:31
  11.2 6.8 %collective-permute-start.5 = (bf16[128,256]{1,0:T(8,128)(2,1)S(1)}, bf16[128,256]{1,0:T(8,128)(2,1)S(1)}, u32[]{:S(2)}, u32[]{:S(2)}) collective-permute-start(bf16[128,256]{1,0:T(8,128)(2,1)S(1)} %get-tuple-element.47.refs_8_), channel_id=1, source_target_pairs={{0,12},{4,8},{8,4},{12,0},{1,13},{5,9},{9,5},{13,1},{2,14},{6,10},... | collective-permute-start | bytes 196616 | tf_op jit(solution)/shard_map/ppermute | solution.py:31
  13.0 5.8 %collective-permute-start.3 = (bf16[128,384]{1,0:T(8,128)(2,1)S(1)}, bf16[128,384]{1,0:T(8,128)(2,1)S(1)}, u32[]{:S(2)}, u32[]{:S(2)}) collective-permute-start(bf16[128,384]{1,0:T(8,128)(2,1)S(1)} %get-tuple-element.49), channel_id=1, source_target_pairs={{0,4},{4,0},{8,12},{12,8},{1,5},{5,1},{9,13},{13,9},{2,6},{6,2},{1... | collective-permute-start | bytes 294920 | tf_op jit(solution)/shard_map/ppermute | solution.py:31
  19.3 4.0 %collective-permute-start.7 = (bf16[128,128]{1,0:T(8,128)(2,1)S(1)}, bf16[128,128]{1,0:T(8,128)(2,1)S(1)}, u32[]{:S(2)}, u32[]{:S(2)}) collective-permute-start(bf16[128,128]{1,0:T(8,128)(2,1)S(1)} %get-tuple-element.53.mixed_ref), channel_id=1, source_target_pairs={{0,2},{1,3},{2,0},{3,1},{4,6},{5,7},{6,4},{7,5},{8,10},{9,11},{10,... | collective-permute-start | bytes 98312 | tf_op jit(solution)/shard_map/ppermute | solution.py:31
  21.0 4.8 %collective-permute-start.8 = (bf16[128,128]{1,0:T(8,128)(2,1)S(1)}, bf16[128,128]{1,0:T(8,128)(2,1)S(1)}, u32[]{:S(2)}, u32[]{:S(2)}) collective-permute-start(bf16[128,128]{1,0:T(8,128)(2,1)S(1)} %get-tuple-element.51), channel_id=1, source_target_pairs={{0,6},{1,7},{2,4},{3,5},{4,2},{5,3},{6,0},{7,1},{8,14},{9,15},{10,... | collective-permute-start | bytes 98312 | tf_op jit(solution)/shard_map/ppermute | solution.py:31
  21.1 5.1 %collective-permute-start.6 = (bf16[128,128]{1,0:T(8,128)(2,1)S(1)}, bf16[128,128]{1,0:T(8,128)(2,1)S(1)}, u32[]{:S(2)}, u32[]{:S(2)}) collective-permute-start(bf16[128,128]{1,0:T(8,128)(2,1)S(1)} %get-tuple-element.51), channel_id=1, source_target_pairs={{0,4},{1,5},{2,6},{3,7},{4,0},{5,1},{6,2},{7,3},{8,12},{9,13},{10,... | collective-permute-start | bytes 98312 | tf_op jit(solution)/shard_map/ppermute | solution.py:31
  26.3 1.4 %collective-permute-start.10 = (bf16[128,512]{1,0:T(8,128)(2,1)S(1)}, bf16[128,512]{1,0:T(8,128)(2,1)S(1)}, u32[]{:S(2)}, u32[]{:S(2)}) collective-permute-start(bf16[128,512]{1,0:T(8,128)(2,1)S(1)} %sent.1), channel_id=1, source_target_pairs={{0,1},{1,0},{2,3},{3,2},{4,5},{5,4},{6,7},{7,6},{8,9},{9,8},{10,11... | collective-permute-start | bytes 393224 | tf_op jit(solution)/shard_map/ppermute | solution.py:31

commit v5 on v4

--- a/solution.py
+++ b/solution.py
@@ -35,7 +35,7 @@
     return lax.optimization_barrier((value, *others))[0]
 
 
-def prepare_kernel(mp, gain_ref, probe_ref, lookup_ref, content_ref, exit_ref, *refs):
+def prepare_kernel(mp, step, gain_ref, probe_ref, lookup_ref, content_ref, exit_ref, *refs):
     weight_refs, (sums_ref, gain_out_ref, own_ref, far_ref) = refs[:3], refs[3:7]
     rows_ref, sems, gain_sem, exit_sems = refs[7:]
     me = lax.axis_index("mp")
@@ -56,7 +56,8 @@
     exits = []
     for k in range(mp):
         to = own_ref.at[k] if k < half else far_ref.at[k - half]
-        columns = pl.ds(pl.multiple_of((me ^ k) * width, width), width)
+        owner = me ^ k if k < half else me ^ step ^ (k - half)
+        columns = pl.ds(pl.multiple_of(owner * width, width), width)
         exits.append(pltpu.make_async_copy(exit_ref.at[:, columns], to, exit_sems.at[k]))
         exits[k].start()
     gain_copy.wait()
@@ -80,13 +81,13 @@
         copy.wait()
 
 
-def prepare(mp, gain, probe, lookup, content, exit_matrix):
+def prepare(mp, step, gain, probe, lookup, content, exit_matrix):
     depth, cols = probe.shape
     deep, wide = exit_matrix.shape
     parts = 4
     stack = pltpu.VMEM((mp // 2, deep, wide // mp), BF16)
     probe, lookup, content, sums, gain, own, far = call(
-        functools.partial(prepare_kernel, mp),
+        functools.partial(prepare_kernel, mp, step),
         "prepare",
         [pltpu.VMEM((depth, cols), BF16)] * 3
         + [pltpu.VMEM((3, 8, cols), F32), pltpu.VMEM((1, depth), F32), stack, stack],
@@ -117,16 +118,14 @@
     return total
 
 
-def take_in(blocks, places, shift, gain_ref, scaled_refs, weight_refs):
+def take_in(blocks, places, shift, gain_ref, weight_refs):
     me = lax.axis_index("mp")
     one, two, scaled = 0.0, 0.0, []
-    for k, block, ref in zip(places, blocks, scaled_refs):
+    for k, block in zip(places, blocks):
         width = block.shape[1]
         gain = gain_ref[0:1, pl.ds(pl.multiple_of((me ^ k) * width, width), width)]
         moved = block[...].astype(F32) - shift
-        value = (moved * gain).astype(BF16)
-        ref[...] = value
-        scaled.append(value)
+        scaled.append((moved * gain).astype(BF16))
         one += jnp.sum(moved, axis=1, keepdims=True)
         two += jnp.sum(moved * moved, axis=1, keepdims=True)
     return one, two, [matmul(scaled, places, ref) for ref in weight_refs]
@@ -135,14 +134,17 @@
 def early_kernel(places, *refs):
     count = len(places)
     blocks = refs[:count]
-    lookup_ref, content_ref, gain_ref, stats_ref, keys_ref, values_ref = refs[count : count + 6]
-    scaled_refs = refs[count + 6 :]
+    weight_refs, (gain_ref, factor_ref, stats_ref), product_refs, (factor_out_ref,) = (
+        refs[count : count + 3],
+        refs[count + 3 : count + 6],
+        refs[count + 6 : count + 9],
+        refs[count + 9 :],
+    )
+    factor_out_ref[...] = factor_ref[...]
     shift = jnp.mean(blocks[0][...].astype(F32), axis=1, keepdims=True)
-    one, two, (keys, values) = take_in(
-        blocks, places, shift, gain_ref, scaled_refs, (lookup_ref, content_ref)
-    )
-    keys_ref[...] = keys
-    values_ref[...] = values
+    one, two, products = take_in(blocks, places, shift, gain_ref, weight_refs)
+    for ref, product in zip(product_refs, products):
+        ref[...] = product
     for i, value in enumerate((shift, one, two)):
         stats_ref[i] = jnp.broadcast_to(value, stats_ref.shape[1:])
 
@@ -153,73 +155,52 @@
 
 def late_kernel(places, depth, *refs):
     count = len(places)
-    blocks = refs[:count]
-    lookup_ref, content_ref, gain_ref, sums_ref, stats_ref, keys_ref, values_ref = refs[count : count + 7]
-    mine_ref, other_ref, final_ref, *scaled_refs = refs[count + 7 :]
-    one, two, products = take_in(
-        blocks, places, stats_ref[0, :, 0:1], gain_ref, scaled_refs, (lookup_ref, content_ref)
-    )
+    blocks, refs = refs[:count], refs[count:]
+    weight_refs, (gain_ref, sums_ref, stats_ref, factor_ref), product_refs = refs[:3], refs[3:7], refs[7:10]
+    queries_ref, mine_ref, other_ref, bundle_ref = refs[10:]
+    one, two, products = take_in(blocks, places, stats_ref[0, :, 0:1], gain_ref, weight_refs)
     offset = (one + stats_ref[1, :, 0:1]) / depth
     scale = lax.rsqrt((two + stats_ref[2, :, 0:1]) / depth - offset * offset + 1e-05)
     first = parity() == 0
-    for i, (product, ref) in enumerate(zip(products, (keys_ref, values_ref))):
+    parts = []
+    for i, (product, ref) in enumerate(zip(products, product_refs)):
         product = product + ref[...]
-        product = scale * (product - offset * sums_ref[i + 1, 0:1, :])
+        product = scale * (product - offset * sums_ref[i, 0:1, :])
+        if i == 0:
+            product = product * factor_ref[...]
         half = product.shape[1] // 2
         low, high = product[:, :half], product[:, half:]
-        for out_ref, part in (
-            (mine_ref, jnp.where(first, low, high)),
-            (other_ref, jnp.where(first, high, low)),
-        ):
-            part = part.astype(BF16)
-            for h in range(half // LANES):
-                out_ref[:, pl.ds((2 * h + i) * LANES, LANES)] = part[:, h * LANES : (h + 1) * LANES]
-    final_ref[0] = jnp.broadcast_to(offset, final_ref.shape[1:])
-    final_ref[1] = jnp.broadcast_to(scale, final_ref.shape[1:])
-
-
-def query_kernel(count, *refs):
-    blocks = refs[:count]
-    probe_ref, sums_ref, final_ref, factor_ref, other_ref, mine_ref, bundle_ref = refs[count:]
-    total = matmul(blocks, range(count), probe_ref) - final_ref[0, :, 0:1] * sums_ref[0, 0:1, :]
-    total = final_ref[1, :, 0:1] * factor_ref[...] * total
-    half = total.shape[1] // 2
-    low, high = total[:, :half], total[:, half:]
-    first = parity() == 0
-    mine_ref[...] = jnp.where(first, low, high).astype(BF16)
-    bundle_ref[:, pl.ds(0, 2 * half)] = other_ref[...]
-    bundle_ref[:, pl.ds(2 * half, half)] = jnp.where(first, high, low).astype(BF16)
-
-
-def project(blocks, weights, sums, gain, factor):
+        parts.append([jnp.where(first, *v).astype(BF16) for v in ((low, high), (high, low))])
+    for i in range(2):
+        for h in range(half // LANES):
+            span = slice(h * LANES, (h + 1) * LANES)
+            to = pl.ds((2 * h + i) * LANES, LANES)
+            mine_ref[:, to] = parts[i + 1][0][:, span]
+            other_ref[:, to] = parts[i + 1][1][:, span]
+            bundle_ref[:, to] = parts[i + 1][1][:, span]
+    queries_ref[...] = parts[0][0]
+    bundle_ref[:, pl.ds(2 * half, half)] = parts[0][1]
+
+
+def project(blocks, places, weights, sums, gain, factor):
     rows, width = blocks[0].shape
-    probe, lookup, content = weights
-    cols = probe.shape[1]
+    cols = weights[0].shape[1]
     count = len(blocks)
     product = pltpu.VMEM((rows, cols), F32)
-    block = pltpu.VMEM((rows, width), BF16)
-    stats, keys, values, *scaled = call(
-        functools.partial(early_kernel, range(count - 1)),
+    stats, *products, factor = call(
+        functools.partial(early_kernel, places[:-1]),
         "early",
-        [pltpu.VMEM((3, rows, LANES), F32), product, product] + [block] * (count - 1),
-        [*blocks[:-1], lookup, content, gain],
-        work=16 * rows * probe.size,
+        [pltpu.VMEM((3, rows, LANES), F32), product, product, product, pltpu.VMEM(factor.shape, F32)],
+        [*blocks[:-1], *weights, gain, factor],
+        work=16 * rows * weights[0].size,
     )
     pair = pltpu.VMEM((rows, cols), BF16)
-    mine, other, final, last = call(
-        functools.partial(late_kernel, range(count - 1, count), count * width),
+    return call(
+        functools.partial(late_kernel, places[-1:], count * width),
         "late",
-        [pair, pair, pltpu.VMEM((2, rows, LANES), F32), block],
-        [blocks[-1], lookup, content, gain, sums, stats, keys, values],
-    )
-    queries, bundle = call(
-        functools.partial(query_kernel, count),
-        "queries",
-        [pltpu.VMEM((rows, cols // 2), BF16), pltpu.VMEM((rows, 3 * cols // 2), BF16)],
-        [*scaled, last, probe, sums, final, factor, other],
-        work=16 * rows * probe.size,
-    )
-    return queries, mine, other, bundle
+        [pltpu.VMEM((rows, cols // 2), BF16), pair, pair, pltpu.VMEM((rows, 3 * cols // 2), BF16)],
+        [blocks[-1], *weights, gain, sums, stats, factor, *products],
+    )
 
 
 def merge_kernel(*refs):
@@ -263,7 +244,7 @@
         "merge",
         [pltpu.VMEM((len(blocks) * rows, wide), BF16)],
         blocks,
-        work=10000 * rows * wide * len(blocks),
+        work=30000 * rows * wide * len(blocks),
     )
     size = merged.shape[0]
     return call(
@@ -302,21 +283,22 @@
     cols = probe.shape[1]
     span = cols // heads
     top = mp // 2
+    step = top | 1
     factor = jnp.repeat(softness * (math.log2(math.e) / math.sqrt(span)), span)[None, :]
 
-    weights, sums, gains, own, far = prepare(mp, gain, probe, lookup, content, exit_matrix)
-    blocks = {0: node_vectors}
-    distance = top
+    weights, sums, gains, own, far = prepare(mp, step, gain, probe, lookup, content, exit_matrix)
+    blocks, distance = {0: node_vectors}, step
     while distance:
         new = {k ^ distance: swap(b, "mp", mp, distance) for k, b in blocks.items()}
-        if distance == top:
+        if distance == step:
             new, sums = lax.optimization_barrier((new, sums))
         blocks.update(new)
-        distance //= 2
+        distance = top // 2 if distance == step else distance // 2
+    places = sorted(blocks, key=lambda k: (k & top, bool(k & top) and k ^ step))
     queries, mine, other, bundle = project(
-        [blocks[k] for k in range(mp)], weights, sums, gains, factor
-    )
-    theirs = swap(far, "mp", mp, top)
+        [blocks[k] for k in places], places, weights, sums, gains, factor
+    )
+    theirs = swap(far, "mp", mp, step)
 
     found = {0: mine}
     for k in sorted(range(1, seq), key=lambda k: (k == 1, k)):
@@ -326,9 +308,9 @@
     rows, width = node_vectors.shape
     product, half = pltpu.VMEM((rows, width), F32), pltpu.VMEM((rows, width), BF16)
     both = ("seq", "mp")
-    across = swap(mixed, both, seq * mp, top)
+    across = swap(mixed, both, seq * mp, step)
     beside = swap(mixed_beside, both, seq * mp, mp)
-    corner = swap(mixed_beside, both, seq * mp, mp + top)
+    corner = swap(mixed_beside, both, seq * mp, mp + step)
     parts = call(
         own_kernel, "own", [product] * top, [node_vectors, mixed, own], work=1 * rows * own.size
     )

time: 28.6 us -> 28.1 us (0.983)
  waiting for transfers between devices: 10.9 us -> 9.43 us
  starting transfers between devices: 11.2 us -> 12.4 us
    ppermute x11, waiting for transfers between devices: 10.9 us -> 9.43 us  [swap(): return lax.ppermute(block, axis, [(i, i ^ distance) for i in range(count)])]
    ppermute x11, starting transfers between devices: 11.2 us -> 12.4 us  [swap(): return lax.ppermute(block, axis, [(i, i ^ distance) for i in range(count)])]
    pallas_call x10 -> x9, Pallas kernels: 5.45 us -> 5.25 us  [call(): pl.pallas_call(kernel, out_shape=out_shape, in_specs=specs or [VMEM] * le...]
  transfers between devices with their start and end apart: 11 -> 11, of which waited for: 8 -> 8; matrix products, arithmetic and copies ran while one was open for 0% -> 0% of each run, Pallas kernels for 19% -> 18%
where the time goes in v5:
time: 28.1 us; the launch traced here: 27.9 us
  starting transfers between devices  12.4 us (44%)
  waiting for transfers between devices  9.43 us (34%)
  Pallas kernels  5.25 us (19%)
  other arithmetic  0.68 us (2%)
    ppermute x11, starting transfers between devices, swap(): return lax.ppermute(block, axis, [(i, i ^ distance) for i in range(count)])  12.4 us
    ppermute x11, waiting for transfers between devices, swap(): return lax.ppermute(block, axis, [(i, i ^ distance) for i in range(count)])  9.43 us
    pallas_call x9, Pallas kernels, call(): pl.pallas_call(kernel, out_shape=out_shape, in_specs=specs or [VMEM] * le...  5.25 us
    convert_element_type x1, other arithmetic, per_device(): return shares[0].astype(node_vectors.dtype)  0.68 us
  transfers between devices with their start and end apart: 11, of which 8 were waited for; matrix products, arithmetic and copies ran while one was open for 0% of the time, Pallas kernels for 18%

profile of v5, /device:TPU:0, one launch (start us, length us, event | category | flops | bytes accessed | tf_op | source)
XLA Modules:
  0.0 27.9 jit_solution(373736839749906678)
XLA Ops:
  0.0 2.4 %collective-permute-start = (bf16[128,512]{1,0:T(8,128)(2,1)}, bf16[128,512]{1,0:T(8,128)(2,1)S(1)}, u32[]{:S(2)}, u32[]{:S(2)}) collective-permute-start(bf16[128,512]{1,0:T(8,128)(2,1)} %x_ref.1), channel_id=1, source_target_pairs={{0,3},{1,2},{2,1},{3,0},{4,7},{5,6},{6,5},{7,4},{8,11},{9,10},{10,... | collective-permute-start | bytes 393224 | tf_op jit(solution)/shard_map/ppermute | solution.py:31
  2.4 0.7 %collective-permute-start.2 = (bf16[128,512]{1,0:T(8,128)(2,1)}, bf16[128,512]{1,0:T(8,128)(2,1)S(1)}, u32[]{:S(2)}, u32[]{:S(2)}) collective-permute-start(bf16[128,512]{1,0:T(8,128)(2,1)} %x_ref.1), channel_id=1, source_target_pairs={{0,1},{1,0},{2,3},{3,2},{4,5},{5,4},{6,7},{7,6},{8,9},{9,8},{10,11... | collective-permute-start | bytes 393224 | tf_op jit(solution)/shard_map/ppermute | solution.py:31
  3.1 0.0 copy-start
  3.1 2.9 %prepare.1 = (bf16[2048,256]{1,0:T(8,128)(2,1)S(1)}, bf16[2048,256]{1,0:T(8,128)(2,1)S(1)}, bf16[2048,256]{1,0:T(8,128)(2,1)S(1)}, f32[3,8,256]{2,1,0:T(8,128)S(...) custom-call(f32[1,2048]{1,0:T(1,128)} %bitcast.3, ...), custom_call_target="tpu_custom_call" | custom-call | flops 25165824 | bytes 393216 | tf_op jit(solution)/shard_map/prepare/pallas_call | solution.py:18
  6.0 0.0 copy-start.1
  6.0 0.1 collective-permute-start.9
  6.1 0.5 %collective-permute-done.refs_2_ = bf16[128,512]{1,0:T(8,128)(2,1)S(1)} collective-permute-done((bf16[128,512]{1,0:T(8,128)(2,1)}, bf16[128,512]{1,0:T(8,128)(2,1)S(1)}, u32[]{:S(2)}, u32[]{:S(2)}) %collective-permute-start) | collective-permute-done | bytes 131104 | tf_op jit(solution)/shard_map/ppermute | solution.py:31
  6.6 0.1 collective-permute-start.1
  6.7 0.0 copy-done.1
  6.7 0.0 collective-permute-done.2.refs_1_
  6.7 0.1 broadcast_in_dim.7
  6.8 0.0 copy-done
  6.8 0.6 %early.1 = (f32[3,128,128]{2,1,0:T(8,128)S(1)}, f32[128,256]{1,0:T(8,128)S(1)}, f32[128,256]{1,0:T(8,128)S(1)}, f32[128,256]{1,0:T(8,128)S(1)}, f32[1,256]{1,0:T(1,128)S(1)}) custom-call(bf16[128,512]{1,0:T(8,128)(2,1)S(1)} %copy-done, bf16[128,512]{1,0:T(8,128)(2,1)S(1)} %collective-permute-done.2.refs_1_, ...), custom_call_target="tpu_custom_call" | custom-call | flops 1073741824 | bytes 16777216 | tf_op jit(solution)/shard_map/early/pallas_call | solution.py:18
  7.4 0.6 %collective-permute-done.1.refs_0_ = bf16[128,512]{1,0:T(8,128)(2,1)S(1)} collective-permute-done((bf16[128,512]{1,0:T(8,128)(2,1)S(1)}, bf16[128,512]{1,0:T(8,128)(2,1)S(1)}, u32[]{:S(2)}, u32[]{:S(2)}) %collective-permute-start.1) | collective-permute-done | bytes 131104 | tf_op jit(solution)/shard_map/ppermute | solution.py:31
  7.9 0.4 %late.1 = (bf16[128,128]{1,0:T(8,128)(2,1)S(1)}, bf16[128,256]{1,0:T(8,128)(2,1)S(1)}, bf16[128,256]{1,0:T(8,128)(2,1)S(1)}, bf16[128,384]{1,0:T(8,128)(2,1)S(1)}) custom-call(bf16[128,512]{1,0:T(8,128)(2,1)S(1)} %collective-permute-done.1.refs_0_, bf16[2048,256]{1,0:T(8,128)(2,1)S(1)} %get-tuple-element.31.refs_3_.refs_1_, ...), custom_call_target="tpu_custom_call" | custom-call | tf_op jit(solution)/shard_map/late/pallas_call | solution.py:18
  8.3 3.5 %collective-permute-start.4 = (bf16[128,256]{1,0:T(8,128)(2,1)S(1)}, bf16[128,256]{1,0:T(8,128)(2,1)S(1)}, u32[]{:S(2)}, u32[]{:S(2)}) collective-permute-start(bf16[128,256]{1,0:T(8,128)(2,1)S(1)} %get-tuple-element.43.refs_0_), channel_id=1, source_target_pairs={{0,8},{4,12},{8,0},{12,4},{1,9},{5,13},{9,1},{13,5},{2,10},{6,14},... | collective-permute-start | bytes 196616 | tf_op jit(solution)/shard_map/ppermute | solution.py:31
  11.8 1.4 %collective-permute-start.5 = (bf16[128,256]{1,0:T(8,128)(2,1)S(1)}, bf16[128,256]{1,0:T(8,128)(2,1)S(1)}, u32[]{:S(2)}, u32[]{:S(2)}) collective-permute-start(bf16[128,256]{1,0:T(8,128)(2,1)S(1)} %get-tuple-element.44), channel_id=1, source_target_pairs={{0,12},{4,8},{8,4},{12,0},{1,13},{5,9},{9,5},{13,1},{2,14},{6,10},... | collective-permute-start | bytes 196616 | tf_op jit(solution)/shard_map/ppermute | solution.py:31
  13.1 0.2 collective-permute-start.3
  13.4 2.4 %collective-permute-done.4.refs_1_ = bf16[128,256]{1,0:T(8,128)(2,1)S(1)} collective-permute-done((bf16[128,256]{1,0:T(8,128)(2,1)S(1)}, bf16[128,256]{1,0:T(8,128)(2,1)S(1)}, u32[]{:S(2)}, u32[]{:S(2)}) %collective-permute-start.4) | collective-permute-done | bytes 65568 | tf_op jit(solution)/shard_map/ppermute | solution.py:31
  15.7 2.8 %collective-permute-done.5.refs_2_ = bf16[128,256]{1,0:T(8,128)(2,1)S(1)} collective-permute-done((bf16[128,256]{1,0:T(8,128)(2,1)S(1)}, bf16[128,256]{1,0:T(8,128)(2,1)S(1)}, u32[]{:S(2)}, u32[]{:S(2)}) %collective-permute-start.5) | collective-permute-done | bytes 65568 | tf_op jit(solution)/shard_map/ppermute | solution.py:31
  18.5 0.5 %collective-permute-done.3.bundle_ref.refs_0_ = bf16[128,384]{1,0:T(8,128)(2,1)S(1)} collective-permute-done((bf16[128,384]{1,0:T(8,128)(2,1)S(1)}, bf16[128,384]{1,0:T(8,128)(2,1)S(1)}, u32[]{:S(2)}, u32[]{:S(2)}) %collective-permute-start.3) | collective-permute-done | bytes 98336 | tf_op jit(solution)/shard_map/ppermute | solution.py:31
  19.1 0.5 %attend.1 = (bf16[128,128]{1,0:T(8,128)(2,1)S(1)}, bf16[128,128]{1,0:T(8,128)(2,1)S(1)}) custom-call(bf16[128,128]{1,0:T(8,128)(2,1)S(1)} %get-tuple-element.41.mine_ref, bf16[128,384]{1,0:T(8,128)(2,1)S(1)} %collective-permute-done.3.bundle_ref.refs_0_, bf16[128,384]{1,0:T(8,128)(2,1)S(1)} %collective-permute-done.3.bundle_ref.refs_0_, ...), custom_call_target="tpu_custom_call" | custom-call | tf_op jit(solution)/shard_map/attend/pallas_call | solution.py:18
  19.6 0.9 %collective-permute-start.7 = (bf16[128,128]{1,0:T(8,128)(2,1)S(1)}, bf16[128,128]{1,0:T(8,128)(2,1)S(1)}, u32[]{:S(2)}, u32[]{:S(2)}) collective-permute-start(bf16[128,128]{1,0:T(8,128)(2,1)S(1)} %get-tuple-element.47.mixed_ref), channel_id=1, source_target_pairs={{0,3},{1,2},{2,1},{3,0},{4,7},{5,6},{6,5},{7,4},{8,11},{9,10},{10,... | collective-permute-start | bytes 98312 | tf_op jit(solution)/shard_map/ppermute | solution.py:31
  20.5 0.8 %collective-permute-start.8 = (bf16[128,128]{1,0:T(8,128)(2,1)S(1)}, bf16[128,128]{1,0:T(8,128)(2,1)S(1)}, u32[]{:S(2)}, u32[]{:S(2)}) collective-permute-start(bf16[128,128]{1,0:T(8,128)(2,1)S(1)} %get-tuple-element.45), channel_id=1, source_target_pairs={{0,7},{1,6},{2,5},{3,4},{4,3},{5,2},{6,1},{7,0},{8,15},{9,14},{10,... | collective-permute-start | bytes 98312 | tf_op jit(solution)/shard_map/ppermute | solution.py:31
  21.3 1.5 %collective-permute-start.6 = (bf16[128,128]{1,0:T(8,128)(2,1)S(1)}, bf16[128,128]{1,0:T(8,128)(2,1)S(1)}, u32[]{:S(2)}, u32[]{:S(2)}) collective-permute-start(bf16[128,128]{1,0:T(8,128)(2,1)S(1)} %get-tuple-element.45), channel_id=1, source_target_pairs={{0,4},{1,5},{2,6},{3,7},{4,0},{5,1},{6,2},{7,3},{8,12},{9,13},{10,... | collective-permute-start | bytes 98312 | tf_op jit(solution)/shard_map/ppermute | solution.py:31
  22.8 0.2 own.1
  23.1 0.0 collective-permute-done.7.refs_0_
  23.1 1.7 %collective-permute-done.8.refs_1_ = bf16[128,128]{1,0:T(8,128)(2,1)S(1)} collective-permute-done((bf16[128,128]{1,0:T(8,128)(2,1)S(1)}, bf16[128,128]{1,0:T(8,128)(2,1)S(1)}, u32[]{:S(2)}, u32[]{:S(2)}) %collective-permute-start.8) | collective-permute-done | bytes 32800 | tf_op jit(solution)/shard_map/ppermute | solution.py:31
  24.8 0.0 collective-permute-done.9.refs_2_.refs_3_
  24.8 0.3 %crossed.1 = (f32[128,512]{1,0:T(8,128)S(1)}, f32[128,512]{1,0:T(8,128)S(1)}) custom-call(bf16[128,128]{1,0:T(8,128)(2,1)S(1)} %collective-permute-done.7.refs_0_, bf16[128,128]{1,0:T(8,128)(2,1)S(1)} %collective-permute-done.8.refs_1_, bf16[2,256,512]{2,1,0:T(8,128)(2,1)S(1)} %collective-permute-done.9.refs_2_.refs_3_, ...), custom_call_target="tpu_custom_call" | custom-call | flops 2147483648 | bytes 33554432 | tf_op jit(solution)/shard_map/crossed/pallas_call | solution.py:18
  25.1 0.2 collective-permute-done.6.refs_0_
  25.3 0.2 sent.1
  25.4 0.8 %collective-permute-start.10 = (bf16[128,512]{1,0:T(8,128)(2,1)S(1)}, bf16[128,512]{1,0:T(8,128)(2,1)S(1)}, u32[]{:S(2)}, u32[]{:S(2)}) collective-permute-start(bf16[128,512]{1,0:T(8,128)(2,1)S(1)} %sent.1), channel_id=1, source_target_pairs={{0,1},{1,0},{2,3},{3,2},{4,5},{5,4},{6,7},{7,6},{8,9},{9,8},{10,11... | collective-permute-start | bytes 393224 | tf_op jit(solution)/shard_map/ppermute | solution.py:31
  26.2 0.2 kept.1
  26.4 0.8 %collective-permute-done.10 = bf16[128,512]{1,0:T(8,128)(2,1)S(1)} collective-permute-done((bf16[128,512]{1,0:T(8,128)(2,1)S(1)}, bf16[128,512]{1,0:T(8,128)(2,1)S(1)}, u32[]{:S(2)}, u32[]{:S(2)}) %collective-permute-start.10) | collective-permute-done | bytes 131104 | tf_op jit(solution)/shard_map/ppermute | solution.py:31
  27.2 0.7 %add_convert_fusion = bf16[128,512]{1,0:T(8,128)(2,1)} fusion(f32[128,512]{1,0:T(8,128)S(1)} %kept.1, bf16[128,512]{1,0:T(8,128)(2,1)S(1)} %collective-permute-done.10), kind=kLoop, calls=%fused_computation | loop fusion | flops 196608 | bytes 524288 | tf_op jit(solution)/shard_map/convert_element_type | solution.py:344
  (2 shorter events, 0.0 us)
Async XLA Ops:
  0.0 6.6 %collective-permute-start = (bf16[128,512]{1,0:T(8,128)(2,1)}, bf16[128,512]{1,0:T(8,128)(2,1)S(1)}, u32[]{:S(2)}, u32[]{:S(2)}) collective-permute-start(bf16[128,512]{1,0:T(8,128)(2,1)} %x_ref.1), channel_id=1, source_target_pairs={{0,3},{1,2},{2,1},{3,0},{4,7},{5,6},{6,5},{7,4},{8,11},{9,10},{10,... | collective-permute-start | bytes 393224 | tf_op jit(solution)/shard_map/ppermute | solution.py:31
  2.4 4.3 %collective-permute-start.2 = (bf16[128,512]{1,0:T(8,128)(2,1)}, bf16[128,512]{1,0:T(8,128)(2,1)S(1)}, u32[]{:S(2)}, u32[]{:S(2)}) collective-permute-start(bf16[128,512]{1,0:T(8,128)(2,1)} %x_ref.1), channel_id=1, source_target_pairs={{0,1},{1,0},{2,3},{3,2},{4,5},{5,4},{6,7},{7,6},{8,9},{9,8},{10,11... | collective-permute-start | bytes 393224 | tf_op jit(solution)/shard_map/ppermute | solution.py:31
  3.1 3.7 %copy-start = (bf16[128,512]{1,0:T(8,128)(2,1)S(1)}, bf16[128,512]{1,0:T(8,128)(2,1)}, u32[]{:S(2)}) copy-start(bf16[128,512]{1,0:T(8,128)(2,1)} %x_ref.1) | copy-start | bytes 393220
  6.0 0.7 %copy-start.1 = (f32[2]{0:T(128)S(1)}, f32[2]{0:T(128)}, u32[]{:S(2)}) copy-start(f32[2]{0:T(128)} %param.12) | copy-start | bytes 28
  6.0 18.8 %collective-permute-start.9 = (bf16[2,256,512]{2,1,0:T(8,128)(2,1)S(1)}, bf16[2,256,512]{2,1,0:T(8,128)(2,1)S(1)}, u32[]{:S(2)}, u32[]{:S(2)}) collective-permute-start(bf16[2,256,512]{2,1,0:T(8,128)(2,1)S(1)} %get-tuple-element.48), channel_id=1, source_target_pairs={{0,3},{1,2},{2,1},{3,0},{4,7},{5,6},{6,5},{7,4},{8,11},{9,10},{10,... | collective-permute-start | bytes 1572872 | tf_op jit(solution)/shard_map/ppermute | solution.py:31
  6.6 1.3 %collective-permute-start.1 = (bf16[128,512]{1,0:T(8,128)(2,1)S(1)}, bf16[128,512]{1,0:T(8,128)(2,1)S(1)}, u32[]{:S(2)}, u32[]{:S(2)}) collective-permute-start(bf16[128,512]{1,0:T(8,128)(2,1)S(1)} %collective-permute-done.refs_2_), channel_id=1, source_target_pairs={{0,1},{1,0},{2,3},{3,2},{4,5},{5,4},{6,7},{7,6},{8,9},{9,8},{10,11... | collective-permute-start | bytes 393224 | tf_op jit(solution)/shard_map/ppermute | solution.py:31
  8.3 7.5 %collective-permute-start.4 = (bf16[128,256]{1,0:T(8,128)(2,1)S(1)}, bf16[128,256]{1,0:T(8,128)(2,1)S(1)}, u32[]{:S(2)}, u32[]{:S(2)}) collective-permute-start(bf16[128,256]{1,0:T(8,128)(2,1)S(1)} %get-tuple-element.43.refs_0_), channel_id=1, source_target_pairs={{0,8},{4,12},{8,0},{12,4},{1,9},{5,13},{9,1},{13,5},{2,10},{6,14},... | collective-permute-start | bytes 196616 | tf_op jit(solution)/shard_map/ppermute | solution.py:31
  11.8 6.7 %collective-permute-start.5 = (bf16[128,256]{1,0:T(8,128)(2,1)S(1)}, bf16[128,256]{1,0:T(8,128)(2,1)S(1)}, u32[]{:S(2)}, u32[]{:S(2)}) collective-permute-start(bf16[128,256]{1,0:T(8,128)(2,1)S(1)} %get-tuple-element.44), channel_id=1, source_target_pairs={{0,12},{4,8},{8,4},{12,0},{1,13},{5,9},{9,5},{13,1},{2,14},{6,10},... | collective-permute-start | bytes 196616 | tf_op jit(solution)/shard_map/ppermute | solution.py:31
  13.1 5.9 %collective-permute-start.3 = (bf16[128,384]{1,0:T(8,128)(2,1)S(1)}, bf16[128,384]{1,0:T(8,128)(2,1)S(1)}, u32[]{:S(2)}, u32[]{:S(2)}) collective-permute-start(bf16[128,384]{1,0:T(8,128)(2,1)S(1)} %get-tuple-element.42), channel_id=1, source_target_pairs={{0,4},{4,0},{8,12},{12,8},{1,5},{5,1},{9,13},{13,9},{2,6},{6,2},{1... | collective-permute-start | bytes 294920 | tf_op jit(solution)/shard_map/ppermute | solution.py:31
  19.6 3.5 %collective-permute-start.7 = (bf16[128,128]{1,0:T(8,128)(2,1)S(1)}, bf16[128,128]{1,0:T(8,128)(2,1)S(1)}, u32[]{:S(2)}, u32[]{:S(2)}) collective-permute-start(bf16[128,128]{1,0:T(8,128)(2,1)S(1)} %get-tuple-element.47.mixed_ref), channel_id=1, source_target_pairs={{0,3},{1,2},{2,1},{3,0},{4,7},{5,6},{6,5},{7,4},{8,11},{9,10},{10,... | collective-permute-start | bytes 98312 | tf_op jit(solution)/shard_map/ppermute | solution.py:31
  20.5 4.2 %collective-permute-start.8 = (bf16[128,128]{1,0:T(8,128)(2,1)S(1)}, bf16[128,128]{1,0:T(8,128)(2,1)S(1)}, u32[]{:S(2)}, u32[]{:S(2)}) collective-permute-start(bf16[128,128]{1,0:T(8,128)(2,1)S(1)} %get-tuple-element.45), channel_id=1, source_target_pairs={{0,7},{1,6},{2,5},{3,4},{4,3},{5,2},{6,1},{7,0},{8,15},{9,14},{10,... | collective-permute-start | bytes 98312 | tf_op jit(solution)/shard_map/ppermute | solution.py:31
  21.3 3.9 %collective-permute-start.6 = (bf16[128,128]{1,0:T(8,128)(2,1)S(1)}, bf16[128,128]{1,0:T(8,128)(2,1)S(1)}, u32[]{:S(2)}, u32[]{:S(2)}) collective-permute-start(bf16[128,128]{1,0:T(8,128)(2,1)S(1)} %get-tuple-element.45), channel_id=1, source_target_pairs={{0,4},{1,5},{2,6},{3,7},{4,0},{5,1},{6,2},{7,3},{8,12},{9,13},{10,... | collective-permute-start | bytes 98312 | tf_op jit(solution)/shard_map/ppermute | solution.py:31
  25.4 1.8 %collective-permute-start.10 = (bf16[128,512]{1,0:T(8,128)(2,1)S(1)}, bf16[128,512]{1,0:T(8,128)(2,1)S(1)}, u32[]{:S(2)}, u32[]{:S(2)}) collective-permute-start(bf16[128,512]{1,0:T(8,128)(2,1)S(1)} %sent.1), channel_id=1, source_target_pairs={{0,1},{1,0},{2,3},{3,2},{4,5},{5,4},{6,7},{7,6},{8,9},{9,8},{10,11... | collective-permute-start | bytes 393224 | tf_op jit(solution)/shard_map/ppermute | solution.py:31

commit v6 on v5

--- a/solution.py
+++ b/solution.py
@@ -287,14 +287,14 @@
     factor = jnp.repeat(softness * (math.log2(math.e) / math.sqrt(span)), span)[None, :]
 
     weights, sums, gains, own, far = prepare(mp, step, gain, probe, lookup, content, exit_matrix)
-    blocks, distance = {0: node_vectors}, step
+    blocks, distance = {0: node_vectors}, top
     while distance:
         new = {k ^ distance: swap(b, "mp", mp, distance) for k, b in blocks.items()}
-        if distance == step:
+        if distance == top:
             new, sums = lax.optimization_barrier((new, sums))
         blocks.update(new)
-        distance = top // 2 if distance == step else distance // 2
-    places = sorted(blocks, key=lambda k: (k & top, bool(k & top) and k ^ step))
+        distance //= 2
+    places = range(mp)
     queries, mine, other, bundle = project(
         [blocks[k] for k in places], places, weights, sums, gains, factor
     )

time: 28.1 us -> 27.5 us (0.979)
  starting transfers between devices: 12.4 us -> 11.7 us
    ppermute x11, starting transfers between devices: 12.4 us -> 11.7 us  [swap(): return lax.ppermute(block, axis, [(i, i ^ distance) for i in range(count)])]
where the time goes in v6:
time: 27.5 us; the launch traced here: 27.4 us
  starting transfers between devices  11.7 us (43%)
  waiting for transfers between devices  9.56 us (35%)
  Pallas kernels  5.24 us (19%)
  other arithmetic  0.68 us (2%)
    ppermute x11, starting transfers between devices, swap(): return lax.ppermute(block, axis, [(i, i ^ distance) for i in range(count)])  11.7 us
    ppermute x11, waiting for transfers between devices, swap(): return lax.ppermute(block, axis, [(i, i ^ distance) for i in range(count)])  9.56 us
    pallas_call x9, Pallas kernels, call(): pl.pallas_call(kernel, out_shape=out_shape, in_specs=specs or [VMEM] * le...  5.24 us
    convert_element_type x1, other arithmetic, per_device(): return shares[0].astype(node_vectors.dtype)  0.68 us
  transfers between devices with their start and end apart: 11, of which 8 were waited for; matrix products, arithmetic and copies ran while one was open for 0% of the time, Pallas kernels for 18%

profile of v6, /device:TPU:0, one launch (start us, length us, event | category | flops | bytes accessed | tf_op | source)
XLA Modules:
  0.0 27.4 jit_solution(785057558063970143)
XLA Ops:
  0.0 2.9 %collective-permute-start = (bf16[128,512]{1,0:T(8,128)(2,1)}, bf16[128,512]{1,0:T(8,128)(2,1)S(1)}, u32[]{:S(2)}, u32[]{:S(2)}) collective-permute-start(bf16[128,512]{1,0:T(8,128)(2,1)} %x_ref.1), channel_id=1, source_target_pairs={{0,2},{1,3},{2,0},{3,1},{4,6},{5,7},{6,4},{7,5},{8,10},{9,11},{10,... | collective-permute-start | bytes 393224 | tf_op jit(solution)/shard_map/ppermute | solution.py:31
  2.9 0.0 collective-permute-start.2
  2.9 0.0 copy-start
  2.9 2.9 %prepare.1 = (bf16[2048,256]{1,0:T(8,128)(2,1)S(1)}, bf16[2048,256]{1,0:T(8,128)(2,1)S(1)}, bf16[2048,256]{1,0:T(8,128)(2,1)S(1)}, f32[3,8,256]{2,1,0:T(8,128)S(...) custom-call(f32[1,2048]{1,0:T(1,128)} %bitcast.3, ...), custom_call_target="tpu_custom_call" | custom-call | flops 25165824 | bytes 393216 | tf_op jit(solution)/shard_map/prepare/pallas_call | solution.py:18
  5.9 0.0 copy-start.1
  5.9 0.2 collective-permute-start.9
  6.1 0.6 %collective-permute-done.refs_2_ = bf16[128,512]{1,0:T(8,128)(2,1)S(1)} collective-permute-done((bf16[128,512]{1,0:T(8,128)(2,1)}, bf16[128,512]{1,0:T(8,128)(2,1)S(1)}, u32[]{:S(2)}, u32[]{:S(2)}) %collective-permute-start) | collective-permute-done | bytes 131104 | tf_op jit(solution)/shard_map/ppermute | solution.py:31
  6.6 0.0 collective-permute-start.1
  6.6 0.0 copy-done.1
  6.7 0.0 collective-permute-done.2.refs_1_
  6.7 0.1 broadcast_in_dim.7
  6.7 0.0 copy-done
  6.7 0.6 %early.1 = (f32[3,128,128]{2,1,0:T(8,128)S(1)}, f32[128,256]{1,0:T(8,128)S(1)}, f32[128,256]{1,0:T(8,128)S(1)}, f32[128,256]{1,0:T(8,128)S(1)}, f32[1,256]{1,0:T(1,128)S(1)}) custom-call(bf16[128,512]{1,0:T(8,128)(2,1)S(1)} %copy-done, bf16[128,512]{1,0:T(8,128)(2,1)S(1)} %collective-permute-done.2.refs_1_, ...), custom_call_target="tpu_custom_call" | custom-call | flops 1073741824 | bytes 16777216 | tf_op jit(solution)/shard_map/early/pallas_call | solution.py:18
  7.3 0.6 %collective-permute-done.1.refs_0_ = bf16[128,512]{1,0:T(8,128)(2,1)S(1)} collective-permute-done((bf16[128,512]{1,0:T(8,128)(2,1)S(1)}, bf16[128,512]{1,0:T(8,128)(2,1)S(1)}, u32[]{:S(2)}, u32[]{:S(2)}) %collective-permute-start.1) | collective-permute-done | bytes 131104 | tf_op jit(solution)/shard_map/ppermute | solution.py:31
  8.0 0.3 %late.1 = (bf16[128,128]{1,0:T(8,128)(2,1)S(1)}, bf16[128,256]{1,0:T(8,128)(2,1)S(1)}, bf16[128,256]{1,0:T(8,128)(2,1)S(1)}, bf16[128,384]{1,0:T(8,128)(2,1)S(1)}) custom-call(bf16[128,512]{1,0:T(8,128)(2,1)S(1)} %collective-permute-done.1.refs_0_, bf16[2048,256]{1,0:T(8,128)(2,1)S(1)} %get-tuple-element.31.refs_3_.refs_1_, ...), custom_call_target="tpu_custom_call" | custom-call | tf_op jit(solution)/shard_map/late/pallas_call | solution.py:18
  8.3 2.9 %collective-permute-start.4 = (bf16[128,256]{1,0:T(8,128)(2,1)S(1)}, bf16[128,256]{1,0:T(8,128)(2,1)S(1)}, u32[]{:S(2)}, u32[]{:S(2)}) collective-permute-start(bf16[128,256]{1,0:T(8,128)(2,1)S(1)} %get-tuple-element.43.refs_0_), channel_id=1, source_target_pairs={{0,8},{4,12},{8,0},{12,4},{1,9},{5,13},{9,1},{13,5},{2,10},{6,14},... | collective-permute-start | bytes 196616 | tf_op jit(solution)/shard_map/ppermute | solution.py:31
  11.3 1.3 %collective-permute-start.5 = (bf16[128,256]{1,0:T(8,128)(2,1)S(1)}, bf16[128,256]{1,0:T(8,128)(2,1)S(1)}, u32[]{:S(2)}, u32[]{:S(2)}) collective-permute-start(bf16[128,256]{1,0:T(8,128)(2,1)S(1)} %get-tuple-element.44), channel_id=1, source_target_pairs={{0,12},{4,8},{8,4},{12,0},{1,13},{5,9},{9,5},{13,1},{2,14},{6,10},... | collective-permute-start | bytes 196616 | tf_op jit(solution)/shard_map/ppermute | solution.py:31
  12.6 0.2 collective-permute-start.3
  12.8 2.4 %collective-permute-done.4.refs_1_ = bf16[128,256]{1,0:T(8,128)(2,1)S(1)} collective-permute-done((bf16[128,256]{1,0:T(8,128)(2,1)S(1)}, bf16[128,256]{1,0:T(8,128)(2,1)S(1)}, u32[]{:S(2)}, u32[]{:S(2)}) %collective-permute-start.4) | collective-permute-done | bytes 65568 | tf_op jit(solution)/shard_map/ppermute | solution.py:31
  15.2 2.8 %collective-permute-done.5.refs_2_ = bf16[128,256]{1,0:T(8,128)(2,1)S(1)} collective-permute-done((bf16[128,256]{1,0:T(8,128)(2,1)S(1)}, bf16[128,256]{1,0:T(8,128)(2,1)S(1)}, u32[]{:S(2)}, u32[]{:S(2)}) %collective-permute-start.5) | collective-permute-done | bytes 65568 | tf_op jit(solution)/shard_map/ppermute | solution.py:31
  18.0 0.5 %collective-permute-done.3.bundle_ref.refs_0_ = bf16[128,384]{1,0:T(8,128)(2,1)S(1)} collective-permute-done((bf16[128,384]{1,0:T(8,128)(2,1)S(1)}, bf16[128,384]{1,0:T(8,128)(2,1)S(1)}, u32[]{:S(2)}, u32[]{:S(2)}) %collective-permute-start.3) | collective-permute-done | bytes 98336 | tf_op jit(solution)/shard_map/ppermute | solution.py:31
  18.5 0.5 %attend.1 = (bf16[128,128]{1,0:T(8,128)(2,1)S(1)}, bf16[128,128]{1,0:T(8,128)(2,1)S(1)}) custom-call(bf16[128,128]{1,0:T(8,128)(2,1)S(1)} %get-tuple-element.41.mine_ref, bf16[128,384]{1,0:T(8,128)(2,1)S(1)} %collective-permute-done.3.bundle_ref.refs_0_, bf16[128,384]{1,0:T(8,128)(2,1)S(1)} %collective-permute-done.3.bundle_ref.refs_0_, ...), custom_call_target="tpu_custom_call" | custom-call | tf_op jit(solution)/shard_map/attend/pallas_call | solution.py:18
  19.1 0.9 %collective-permute-start.7 = (bf16[128,128]{1,0:T(8,128)(2,1)S(1)}, bf16[128,128]{1,0:T(8,128)(2,1)S(1)}, u32[]{:S(2)}, u32[]{:S(2)}) collective-permute-start(bf16[128,128]{1,0:T(8,128)(2,1)S(1)} %get-tuple-element.47.mixed_ref), channel_id=1, source_target_pairs={{0,3},{1,2},{2,1},{3,0},{4,7},{5,6},{6,5},{7,4},{8,11},{9,10},{10,... | collective-permute-start | bytes 98312 | tf_op jit(solution)/shard_map/ppermute | solution.py:31
  20.0 0.8 %collective-permute-start.8 = (bf16[128,128]{1,0:T(8,128)(2,1)S(1)}, bf16[128,128]{1,0:T(8,128)(2,1)S(1)}, u32[]{:S(2)}, u32[]{:S(2)}) collective-permute-start(bf16[128,128]{1,0:T(8,128)(2,1)S(1)} %get-tuple-element.45), channel_id=1, source_target_pairs={{0,7},{1,6},{2,5},{3,4},{4,3},{5,2},{6,1},{7,0},{8,15},{9,14},{10,... | collective-permute-start | bytes 98312 | tf_op jit(solution)/shard_map/ppermute | solution.py:31
  20.8 1.6 %collective-permute-start.6 = (bf16[128,128]{1,0:T(8,128)(2,1)S(1)}, bf16[128,128]{1,0:T(8,128)(2,1)S(1)}, u32[]{:S(2)}, u32[]{:S(2)}) collective-permute-start(bf16[128,128]{1,0:T(8,128)(2,1)S(1)} %get-tuple-element.45), channel_id=1, source_target_pairs={{0,4},{1,5},{2,6},{3,7},{4,0},{5,1},{6,2},{7,3},{8,12},{9,13},{10,... | collective-permute-start | bytes 98312 | tf_op jit(solution)/shard_map/ppermute | solution.py:31
  22.4 0.2 own.1
  22.6 0.0 collective-permute-done.7.refs_0_
  22.6 1.6 %collective-permute-done.8.refs_1_ = bf16[128,128]{1,0:T(8,128)(2,1)S(1)} collective-permute-done((bf16[128,128]{1,0:T(8,128)(2,1)S(1)}, bf16[128,128]{1,0:T(8,128)(2,1)S(1)}, u32[]{:S(2)}, u32[]{:S(2)}) %collective-permute-start.8) | collective-permute-done | bytes 32800 | tf_op jit(solution)/shard_map/ppermute | solution.py:31
  24.2 0.0 collective-permute-done.9.refs_2_.refs_3_
  24.2 0.3 %crossed.1 = (f32[128,512]{1,0:T(8,128)S(1)}, f32[128,512]{1,0:T(8,128)S(1)}) custom-call(bf16[128,128]{1,0:T(8,128)(2,1)S(1)} %collective-permute-done.7.refs_0_, bf16[128,128]{1,0:T(8,128)(2,1)S(1)} %collective-permute-done.8.refs_1_, bf16[2,256,512]{2,1,0:T(8,128)(2,1)S(1)} %collective-permute-done.9.refs_2_.refs_3_, ...), custom_call_target="tpu_custom_call" | custom-call | flops 2147483648 | bytes 33554432 | tf_op jit(solution)/shard_map/crossed/pallas_call | solution.py:18
  24.5 0.2 collective-permute-done.6.refs_0_
  24.7 0.2 sent.1
  24.9 0.8 %collective-permute-start.10 = (bf16[128,512]{1,0:T(8,128)(2,1)S(1)}, bf16[128,512]{1,0:T(8,128)(2,1)S(1)}, u32[]{:S(2)}, u32[]{:S(2)}) collective-permute-start(bf16[128,512]{1,0:T(8,128)(2,1)S(1)} %sent.1), channel_id=1, source_target_pairs={{0,1},{1,0},{2,3},{3,2},{4,5},{5,4},{6,7},{7,6},{8,9},{9,8},{10,11... | collective-permute-start | bytes 393224 | tf_op jit(solution)/shard_map/ppermute | solution.py:31
  25.7 0.2 kept.1
  25.9 0.8 %collective-permute-done.10 = bf16[128,512]{1,0:T(8,128)(2,1)S(1)} collective-permute-done((bf16[128,512]{1,0:T(8,128)(2,1)S(1)}, bf16[128,512]{1,0:T(8,128)(2,1)S(1)}, u32[]{:S(2)}, u32[]{:S(2)}) %collective-permute-start.10) | collective-permute-done | bytes 131104 | tf_op jit(solution)/shard_map/ppermute | solution.py:31
  26.7 0.7 %add_convert_fusion = bf16[128,512]{1,0:T(8,128)(2,1)} fusion(f32[128,512]{1,0:T(8,128)S(1)} %kept.1, bf16[128,512]{1,0:T(8,128)(2,1)S(1)} %collective-permute-done.10), kind=kLoop, calls=%fused_computation | loop fusion | flops 196608 | bytes 524288 | tf_op jit(solution)/shard_map/convert_element_type | solution.py:344
  (2 shorter events, 0.0 us)
Async XLA Ops:
  0.0 6.6 %collective-permute-start = (bf16[128,512]{1,0:T(8,128)(2,1)}, bf16[128,512]{1,0:T(8,128)(2,1)S(1)}, u32[]{:S(2)}, u32[]{:S(2)}) collective-permute-start(bf16[128,512]{1,0:T(8,128)(2,1)} %x_ref.1), channel_id=1, source_target_pairs={{0,2},{1,3},{2,0},{3,1},{4,6},{5,7},{6,4},{7,5},{8,10},{9,11},{10,... | collective-permute-start | bytes 393224 | tf_op jit(solution)/shard_map/ppermute | solution.py:31
  2.9 3.7 %collective-permute-start.2 = (bf16[128,512]{1,0:T(8,128)(2,1)}, bf16[128,512]{1,0:T(8,128)(2,1)S(1)}, u32[]{:S(2)}, u32[]{:S(2)}) collective-permute-start(bf16[128,512]{1,0:T(8,128)(2,1)} %x_ref.1), channel_id=1, source_target_pairs={{0,1},{1,0},{2,3},{3,2},{4,5},{5,4},{6,7},{7,6},{8,9},{9,8},{10,11... | collective-permute-start | bytes 393224 | tf_op jit(solution)/shard_map/ppermute | solution.py:31
  2.9 3.8 %copy-start = (bf16[128,512]{1,0:T(8,128)(2,1)S(1)}, bf16[128,512]{1,0:T(8,128)(2,1)}, u32[]{:S(2)}) copy-start(bf16[128,512]{1,0:T(8,128)(2,1)} %x_ref.1) | copy-start | bytes 393220
  5.9 0.8 %copy-start.1 = (f32[2]{0:T(128)S(1)}, f32[2]{0:T(128)}, u32[]{:S(2)}) copy-start(f32[2]{0:T(128)} %param.12) | copy-start | bytes 28
  5.9 18.3 %collective-permute-start.9 = (bf16[2,256,512]{2,1,0:T(8,128)(2,1)S(1)}, bf16[2,256,512]{2,1,0:T(8,128)(2,1)S(1)}, u32[]{:S(2)}, u32[]{:S(2)}) collective-permute-start(bf16[2,256,512]{2,1,0:T(8,128)(2,1)S(1)} %get-tuple-element.48), channel_id=1, source_target_pairs={{0,3},{1,2},{2,1},{3,0},{4,7},{5,6},{6,5},{7,4},{8,11},{9,10},{10,... | collective-permute-start | bytes 1572872 | tf_op jit(solution)/shard_map/ppermute | solution.py:31
  6.6 1.3 %collective-permute-start.1 = (bf16[128,512]{1,0:T(8,128)(2,1)S(1)}, bf16[128,512]{1,0:T(8,128)(2,1)S(1)}, u32[]{:S(2)}, u32[]{:S(2)}) collective-permute-start(bf16[128,512]{1,0:T(8,128)(2,1)S(1)} %collective-permute-done.refs_2_), channel_id=1, source_target_pairs={{0,1},{1,0},{2,3},{3,2},{4,5},{5,4},{6,7},{7,6},{8,9},{9,8},{10,11... | collective-permute-start | bytes 393224 | tf_op jit(solution)/shard_map/ppermute | solution.py:31
  8.3 6.9 %collective-permute-start.4 = (bf16[128,256]{1,0:T(8,128)(2,1)S(1)}, bf16[128,256]{1,0:T(8,128)(2,1)S(1)}, u32[]{:S(2)}, u32[]{:S(2)}) collective-permute-start(bf16[128,256]{1,0:T(8,128)(2,1)S(1)} %get-tuple-element.43.refs_0_), channel_id=1, source_target_pairs={{0,8},{4,12},{8,0},{12,4},{1,9},{5,13},{9,1},{13,5},{2,10},{6,14},... | collective-permute-start | bytes 196616 | tf_op jit(solution)/shard_map/ppermute | solution.py:31
  11.3 6.7 %collective-permute-start.5 = (bf16[128,256]{1,0:T(8,128)(2,1)S(1)}, bf16[128,256]{1,0:T(8,128)(2,1)S(1)}, u32[]{:S(2)}, u32[]{:S(2)}) collective-permute-start(bf16[128,256]{1,0:T(8,128)(2,1)S(1)} %get-tuple-element.44), channel_id=1, source_target_pairs={{0,12},{4,8},{8,4},{12,0},{1,13},{5,9},{9,5},{13,1},{2,14},{6,10},... | collective-permute-start | bytes 196616 | tf_op jit(solution)/shard_map/ppermute | solution.py:31
  12.6 5.9 %collective-permute-start.3 = (bf16[128,384]{1,0:T(8,128)(2,1)S(1)}, bf16[128,384]{1,0:T(8,128)(2,1)S(1)}, u32[]{:S(2)}, u32[]{:S(2)}) collective-permute-start(bf16[128,384]{1,0:T(8,128)(2,1)S(1)} %get-tuple-element.42), channel_id=1, source_target_pairs={{0,4},{4,0},{8,12},{12,8},{1,5},{5,1},{9,13},{13,9},{2,6},{6,2},{1... | collective-permute-start | bytes 294920 | tf_op jit(solution)/shard_map/ppermute | solution.py:31
  19.1 3.5 %collective-permute-start.7 = (bf16[128,128]{1,0:T(8,128)(2,1)S(1)}, bf16[128,128]{1,0:T(8,128)(2,1)S(1)}, u32[]{:S(2)}, u32[]{:S(2)}) collective-permute-start(bf16[128,128]{1,0:T(8,128)(2,1)S(1)} %get-tuple-element.47.mixed_ref), channel_id=1, source_target_pairs={{0,3},{1,2},{2,1},{3,0},{4,7},{5,6},{6,5},{7,4},{8,11},{9,10},{10,... | collective-permute-start | bytes 98312 | tf_op jit(solution)/shard_map/ppermute | solution.py:31
  20.0 4.2 %collective-permute-start.8 = (bf16[128,128]{1,0:T(8,128)(2,1)S(1)}, bf16[128,128]{1,0:T(8,128)(2,1)S(1)}, u32[]{:S(2)}, u32[]{:S(2)}) collective-permute-start(bf16[128,128]{1,0:T(8,128)(2,1)S(1)} %get-tuple-element.45), channel_id=1, source_target_pairs={{0,7},{1,6},{2,5},{3,4},{4,3},{5,2},{6,1},{7,0},{8,15},{9,14},{10,... | collective-permute-start | bytes 98312 | tf_op jit(solution)/shard_map/ppermute | solution.py:31
  20.8 3.9 %collective-permute-start.6 = (bf16[128,128]{1,0:T(8,128)(2,1)S(1)}, bf16[128,128]{1,0:T(8,128)(2,1)S(1)}, u32[]{:S(2)}, u32[]{:S(2)}) collective-permute-start(bf16[128,128]{1,0:T(8,128)(2,1)S(1)} %get-tuple-element.45), channel_id=1, source_target_pairs={{0,4},{1,5},{2,6},{3,7},{4,0},{5,1},{6,2},{7,3},{8,12},{9,13},{10,... | collective-permute-start | bytes 98312 | tf_op jit(solution)/shard_map/ppermute | solution.py:31
  24.9 1.8 %collective-permute-start.10 = (bf16[128,512]{1,0:T(8,128)(2,1)S(1)}, bf16[128,512]{1,0:T(8,128)(2,1)S(1)}, u32[]{:S(2)}, u32[]{:S(2)}) collective-permute-start(bf16[128,512]{1,0:T(8,128)(2,1)S(1)} %sent.1), channel_id=1, source_target_pairs={{0,1},{1,0},{2,3},{3,2},{4,5},{5,4},{6,7},{7,6},{8,9},{9,8},{10,11... | collective-permute-start | bytes 393224 | tf_op jit(solution)/shard_map/ppermute | solution.py:31

commit v7 on v6

--- a/solution.py
+++ b/solution.py
@@ -315,20 +315,23 @@
         own_kernel, "own", [product] * top, [node_vectors, mixed, own], work=1 * rows * own.size
     )
     parts = call(
-        functools.partial(add_kernel, range(top), (0, 1)),
+        functools.partial(add_kernel, range(top), (0,)),
         "crossed",
         [product] * top,
-        [across, corner, theirs, theirs, *parts],
+        [across, theirs, *parts],
         work=64 * rows * own.size,
     )
     sent = call(
-        functools.partial(add_kernel, range(1, top), (1,)), "sent", [half] * (top - 1), [beside, own, *parts[1:]]
+        functools.partial(add_kernel, range(1, top), (1, 1)),
+        "sent",
+        [half] * (top - 1),
+        [corner, beside, theirs, own, *parts[1:]],
     )
     (kept,) = call(
-        functools.partial(add_kernel, range(1), (1,)),
+        functools.partial(add_kernel, range(1), (1, 1)),
         "kept",
         [product],
-        [beside, own, parts[0]],
+        [corner, beside, theirs, own, parts[0]],
         work=64 * rows * own.size,
     )
     shares = {0: kept, **{k: sent[k - 1] for k in range(1, top)}}

time: 27.5 us -> 27.2 us (0.989)
  starting transfers between devices: 11.7 us -> 11.4 us
    ppermute x11, starting transfers between devices: 11.7 us -> 11.4 us  [swap(): return lax.ppermute(block, axis, [(i, i ^ distance) for i in range(count)])]
  transfers between devices with their start and end apart: 11 -> 11, of which waited for: 8 -> 8; matrix products, arithmetic and copies ran while one was open for 0% -> 0% of each run, Pallas kernels for 18% -> 19%
where the time goes in v7:
time: 27.2 us; the launch traced here: 27.1 us
  starting transfers between devices  11.4 us (42%)
  waiting for transfers between devices  9.59 us (35%)
  Pallas kernels  5.25 us (19%)
  other arithmetic  0.68 us (2%)
    ppermute x11, starting transfers between devices, swap(): return lax.ppermute(block, axis, [(i, i ^ distance) for i in range(count)])  11.4 us
    ppermute x11, waiting for transfers between devices, swap(): return lax.ppermute(block, axis, [(i, i ^ distance) for i in range(count)])  9.59 us
    pallas_call x9, Pallas kernels, call(): pl.pallas_call(kernel, out_shape=out_shape, in_specs=specs or [VMEM] * le...  5.25 us
    convert_element_type x1, other arithmetic, per_device(): return shares[0].astype(node_vectors.dtype)  0.68 us
  transfers between devices with their start and end apart: 11, of which 8 were waited for; matrix products, arithmetic and copies ran while one was open for 0% of the time, Pallas kernels for 19%

profile of v7, /device:TPU:0, one launch (start us, length us, event | category | flops | bytes accessed | tf_op | source)
XLA Modules:
  0.0 27.1 jit_solution(10675967805317721843)
XLA Ops:
  0.0 2.9 %collective-permute-start = (bf16[128,512]{1,0:T(8,128)(2,1)}, bf16[128,512]{1,0:T(8,128)(2,1)S(1)}, u32[]{:S(2)}, u32[]{:S(2)}) collective-permute-start(bf16[128,512]{1,0:T(8,128)(2,1)} %x_ref.1), channel_id=1, source_target_pairs={{0,2},{1,3},{2,0},{3,1},{4,6},{5,7},{6,4},{7,5},{8,10},{9,11},{10,... | collective-permute-start | bytes 393224 | tf_op jit(solution)/shard_map/ppermute | solution.py:31
  2.9 0.0 collective-permute-start.2
  2.9 0.0 copy-start
  2.9 2.9 %prepare.1 = (bf16[2048,256]{1,0:T(8,128)(2,1)S(1)}, bf16[2048,256]{1,0:T(8,128)(2,1)S(1)}, bf16[2048,256]{1,0:T(8,128)(2,1)S(1)}, f32[3,8,256]{2,1,0:T(8,128)S(...) custom-call(f32[1,2048]{1,0:T(1,128)} %bitcast.3, ...), custom_call_target="tpu_custom_call" | custom-call | flops 25165824 | bytes 393216 | tf_op jit(solution)/shard_map/prepare/pallas_call | solution.py:18
  5.9 0.0 copy-start.1
  5.9 0.2 collective-permute-start.8
  6.1 0.6 %collective-permute-done.refs_2_ = bf16[128,512]{1,0:T(8,128)(2,1)S(1)} collective-permute-done((bf16[128,512]{1,0:T(8,128)(2,1)}, bf16[128,512]{1,0:T(8,128)(2,1)S(1)}, u32[]{:S(2)}, u32[]{:S(2)}) %collective-permute-start) | collective-permute-done | bytes 131104 | tf_op jit(solution)/shard_map/ppermute | solution.py:31
  6.6 0.0 collective-permute-start.1
  6.6 0.0 copy-done.1
  6.7 0.0 collective-permute-done.2.refs_1_
  6.7 0.1 broadcast_in_dim.7
  6.7 0.0 copy-done
  6.7 0.6 %early.1 = (f32[3,128,128]{2,1,0:T(8,128)S(1)}, f32[128,256]{1,0:T(8,128)S(1)}, f32[128,256]{1,0:T(8,128)S(1)}, f32[128,256]{1,0:T(8,128)S(1)}, f32[1,256]{1,0:T(1,128)S(1)}) custom-call(bf16[128,512]{1,0:T(8,128)(2,1)S(1)} %copy-done, bf16[128,512]{1,0:T(8,128)(2,1)S(1)} %collective-permute-done.2.refs_1_, ...), custom_call_target="tpu_custom_call" | custom-call | flops 1073741824 | bytes 16777216 | tf_op jit(solution)/shard_map/early/pallas_call | solution.py:18
  7.3 0.6 %collective-permute-done.1.refs_0_ = bf16[128,512]{1,0:T(8,128)(2,1)S(1)} collective-permute-done((bf16[128,512]{1,0:T(8,128)(2,1)S(1)}, bf16[128,512]{1,0:T(8,128)(2,1)S(1)}, u32[]{:S(2)}, u32[]{:S(2)}) %collective-permute-start.1) | collective-permute-done | bytes 131104 | tf_op jit(solution)/shard_map/ppermute | solution.py:31
  8.0 0.3 %late.1 = (bf16[128,128]{1,0:T(8,128)(2,1)S(1)}, bf16[128,256]{1,0:T(8,128)(2,1)S(1)}, bf16[128,256]{1,0:T(8,128)(2,1)S(1)}, bf16[128,384]{1,0:T(8,128)(2,1)S(1)}) custom-call(bf16[128,512]{1,0:T(8,128)(2,1)S(1)} %collective-permute-done.1.refs_0_, bf16[2048,256]{1,0:T(8,128)(2,1)S(1)} %get-tuple-element.31.refs_3_.refs_1_, ...), custom_call_target="tpu_custom_call" | custom-call | tf_op jit(solution)/shard_map/late/pallas_call | solution.py:18
  8.3 2.9 %collective-permute-start.4 = (bf16[128,256]{1,0:T(8,128)(2,1)S(1)}, bf16[128,256]{1,0:T(8,128)(2,1)S(1)}, u32[]{:S(2)}, u32[]{:S(2)}) collective-permute-start(bf16[128,256]{1,0:T(8,128)(2,1)S(1)} %get-tuple-element.43.refs_0_), channel_id=1, source_target_pairs={{0,8},{4,12},{8,0},{12,4},{1,9},{5,13},{9,1},{13,5},{2,10},{6,14},... | collective-permute-start | bytes 196616 | tf_op jit(solution)/shard_map/ppermute | solution.py:31
  11.3 1.3 %collective-permute-start.5 = (bf16[128,256]{1,0:T(8,128)(2,1)S(1)}, bf16[128,256]{1,0:T(8,128)(2,1)S(1)}, u32[]{:S(2)}, u32[]{:S(2)}) collective-permute-start(bf16[128,256]{1,0:T(8,128)(2,1)S(1)} %get-tuple-element.44), channel_id=1, source_target_pairs={{0,12},{4,8},{8,4},{12,0},{1,13},{5,9},{9,5},{13,1},{2,14},{6,10},... | collective-permute-start | bytes 196616 | tf_op jit(solution)/shard_map/ppermute | solution.py:31
  12.6 0.2 collective-permute-start.3
  12.8 2.4 %collective-permute-done.4.refs_1_ = bf16[128,256]{1,0:T(8,128)(2,1)S(1)} collective-permute-done((bf16[128,256]{1,0:T(8,128)(2,1)S(1)}, bf16[128,256]{1,0:T(8,128)(2,1)S(1)}, u32[]{:S(2)}, u32[]{:S(2)}) %collective-permute-start.4) | collective-permute-done | bytes 65568 | tf_op jit(solution)/shard_map/ppermute | solution.py:31
  15.2 2.8 %collective-permute-done.5.refs_2_ = bf16[128,256]{1,0:T(8,128)(2,1)S(1)} collective-permute-done((bf16[128,256]{1,0:T(8,128)(2,1)S(1)}, bf16[128,256]{1,0:T(8,128)(2,1)S(1)}, u32[]{:S(2)}, u32[]{:S(2)}) %collective-permute-start.5) | collective-permute-done | bytes 65568 | tf_op jit(solution)/shard_map/ppermute | solution.py:31
  18.0 0.5 %collective-permute-done.3.bundle_ref.refs_0_ = bf16[128,384]{1,0:T(8,128)(2,1)S(1)} collective-permute-done((bf16[128,384]{1,0:T(8,128)(2,1)S(1)}, bf16[128,384]{1,0:T(8,128)(2,1)S(1)}, u32[]{:S(2)}, u32[]{:S(2)}) %collective-permute-start.3) | collective-permute-done | bytes 98336 | tf_op jit(solution)/shard_map/ppermute | solution.py:31
  18.5 0.5 %attend.1 = (bf16[128,128]{1,0:T(8,128)(2,1)S(1)}, bf16[128,128]{1,0:T(8,128)(2,1)S(1)}) custom-call(bf16[128,128]{1,0:T(8,128)(2,1)S(1)} %get-tuple-element.41.mine_ref, bf16[128,384]{1,0:T(8,128)(2,1)S(1)} %collective-permute-done.3.bundle_ref.refs_0_, bf16[128,384]{1,0:T(8,128)(2,1)S(1)} %collective-permute-done.3.bundle_ref.refs_0_, ...), custom_call_target="tpu_custom_call" | custom-call | tf_op jit(solution)/shard_map/attend/pallas_call | solution.py:18
  19.1 0.9 %collective-permute-start.9 = (bf16[128,128]{1,0:T(8,128)(2,1)S(1)}, bf16[128,128]{1,0:T(8,128)(2,1)S(1)}, u32[]{:S(2)}, u32[]{:S(2)}) collective-permute-start(bf16[128,128]{1,0:T(8,128)(2,1)S(1)} %get-tuple-element.48.mixed_ref), channel_id=1, source_target_pairs={{0,3},{1,2},{2,1},{3,0},{4,7},{5,6},{6,5},{7,4},{8,11},{9,10},{10,... | collective-permute-start | bytes 98312 | tf_op jit(solution)/shard_map/ppermute | solution.py:31
  20.0 0.8 %collective-permute-start.6 = (bf16[128,128]{1,0:T(8,128)(2,1)S(1)}, bf16[128,128]{1,0:T(8,128)(2,1)S(1)}, u32[]{:S(2)}, u32[]{:S(2)}) collective-permute-start(bf16[128,128]{1,0:T(8,128)(2,1)S(1)} %get-tuple-element.45), channel_id=1, source_target_pairs={{0,7},{1,6},{2,5},{3,4},{4,3},{5,2},{6,1},{7,0},{8,15},{9,14},{10,... | collective-permute-start | bytes 98312 | tf_op jit(solution)/shard_map/ppermute | solution.py:31
  20.8 1.6 %collective-permute-start.7 = (bf16[128,128]{1,0:T(8,128)(2,1)S(1)}, bf16[128,128]{1,0:T(8,128)(2,1)S(1)}, u32[]{:S(2)}, u32[]{:S(2)}) collective-permute-start(bf16[128,128]{1,0:T(8,128)(2,1)S(1)} %get-tuple-element.45), channel_id=1, source_target_pairs={{0,4},{1,5},{2,6},{3,7},{4,0},{5,1},{6,2},{7,3},{8,12},{9,13},{10,... | collective-permute-start | bytes 98312 | tf_op jit(solution)/shard_map/ppermute | solution.py:31
  22.4 0.2 own.1
  22.6 0.0 collective-permute-done.9.refs_0_
  22.6 0.0 collective-permute-done.8.refs_1_.refs_2_
  22.6 0.2 crossed.1
  22.8 1.4 %collective-permute-done.6.refs_0_ = bf16[128,128]{1,0:T(8,128)(2,1)S(1)} collective-permute-done((bf16[128,128]{1,0:T(8,128)(2,1)S(1)}, bf16[128,128]{1,0:T(8,128)(2,1)S(1)}, u32[]{:S(2)}, u32[]{:S(2)}) %collective-permute-start.6) | collective-permute-done | bytes 32800 | tf_op jit(solution)/shard_map/ppermute | solution.py:31
  24.2 0.5 %collective-permute-done.7.refs_1_ = bf16[128,128]{1,0:T(8,128)(2,1)S(1)} collective-permute-done((bf16[128,128]{1,0:T(8,128)(2,1)S(1)}, bf16[128,128]{1,0:T(8,128)(2,1)S(1)}, u32[]{:S(2)}, u32[]{:S(2)}) %collective-permute-start.7) | collective-permute-done | bytes 32800 | tf_op jit(solution)/shard_map/ppermute | solution.py:31
  24.7 0.2 sent.1
  24.9 0.5 %collective-permute-start.10 = (bf16[128,512]{1,0:T(8,128)(2,1)S(1)}, bf16[128,512]{1,0:T(8,128)(2,1)S(1)}, u32[]{:S(2)}, u32[]{:S(2)}) collective-permute-start(bf16[128,512]{1,0:T(8,128)(2,1)S(1)} %sent.1), channel_id=1, source_target_pairs={{0,1},{1,0},{2,3},{3,2},{4,5},{5,4},{6,7},{7,6},{8,9},{9,8},{10,11... | collective-permute-start | bytes 393224 | tf_op jit(solution)/shard_map/ppermute | solution.py:31
  25.4 0.2 kept.1
  25.6 0.8 %collective-permute-done.10 = bf16[128,512]{1,0:T(8,128)(2,1)S(1)} collective-permute-done((bf16[128,512]{1,0:T(8,128)(2,1)S(1)}, bf16[128,512]{1,0:T(8,128)(2,1)S(1)}, u32[]{:S(2)}, u32[]{:S(2)}) %collective-permute-start.10) | collective-permute-done | bytes 131104 | tf_op jit(solution)/shard_map/ppermute | solution.py:31
  26.4 0.7 %add_convert_fusion = bf16[128,512]{1,0:T(8,128)(2,1)} fusion(f32[128,512]{1,0:T(8,128)S(1)} %kept.1, bf16[128,512]{1,0:T(8,128)(2,1)S(1)} %collective-permute-done.10), kind=kLoop, calls=%fused_computation | loop fusion | flops 196608 | bytes 524288 | tf_op jit(solution)/shard_map/convert_element_type | solution.py:347
  (2 shorter events, 0.0 us)
Async XLA Ops:
  0.0 6.6 %collective-permute-start = (bf16[128,512]{1,0:T(8,128)(2,1)}, bf16[128,512]{1,0:T(8,128)(2,1)S(1)}, u32[]{:S(2)}, u32[]{:S(2)}) collective-permute-start(bf16[128,512]{1,0:T(8,128)(2,1)} %x_ref.1), channel_id=1, source_target_pairs={{0,2},{1,3},{2,0},{3,1},{4,6},{5,7},{6,4},{7,5},{8,10},{9,11},{10,... | collective-permute-start | bytes 393224 | tf_op jit(solution)/shard_map/ppermute | solution.py:31
  2.9 3.7 %collective-permute-start.2 = (bf16[128,512]{1,0:T(8,128)(2,1)}, bf16[128,512]{1,0:T(8,128)(2,1)S(1)}, u32[]{:S(2)}, u32[]{:S(2)}) collective-permute-start(bf16[128,512]{1,0:T(8,128)(2,1)} %x_ref.1), channel_id=1, source_target_pairs={{0,1},{1,0},{2,3},{3,2},{4,5},{5,4},{6,7},{7,6},{8,9},{9,8},{10,11... | collective-permute-start | bytes 393224 | tf_op jit(solution)/shard_map/ppermute | solution.py:31
  2.9 3.8 %copy-start = (bf16[128,512]{1,0:T(8,128)(2,1)S(1)}, bf16[128,512]{1,0:T(8,128)(2,1)}, u32[]{:S(2)}) copy-start(bf16[128,512]{1,0:T(8,128)(2,1)} %x_ref.1) | copy-start | bytes 393220
  5.9 0.8 %copy-start.1 = (f32[2]{0:T(128)S(1)}, f32[2]{0:T(128)}, u32[]{:S(2)}) copy-start(f32[2]{0:T(128)} %param.12) | copy-start | bytes 28
  5.9 16.7 %collective-permute-start.8 = (bf16[2,256,512]{2,1,0:T(8,128)(2,1)S(1)}, bf16[2,256,512]{2,1,0:T(8,128)(2,1)S(1)}, u32[]{:S(2)}, u32[]{:S(2)}) collective-permute-start(bf16[2,256,512]{2,1,0:T(8,128)(2,1)S(1)} %get-tuple-element.46), channel_id=1, source_target_pairs={{0,3},{1,2},{2,1},{3,0},{4,7},{5,6},{6,5},{7,4},{8,11},{9,10},{10,... | collective-permute-start | bytes 1572872 | tf_op jit(solution)/shard_map/ppermute | solution.py:31
  6.6 1.3 %collective-permute-start.1 = (bf16[128,512]{1,0:T(8,128)(2,1)S(1)}, bf16[128,512]{1,0:T(8,128)(2,1)S(1)}, u32[]{:S(2)}, u32[]{:S(2)}) collective-permute-start(bf16[128,512]{1,0:T(8,128)(2,1)S(1)} %collective-permute-done.refs_2_), channel_id=1, source_target_pairs={{0,1},{1,0},{2,3},{3,2},{4,5},{5,4},{6,7},{7,6},{8,9},{9,8},{10,11... | collective-permute-start | bytes 393224 | tf_op jit(solution)/shard_map/ppermute | solution.py:31
  8.3 6.9 %collective-permute-start.4 = (bf16[128,256]{1,0:T(8,128)(2,1)S(1)}, bf16[128,256]{1,0:T(8,128)(2,1)S(1)}, u32[]{:S(2)}, u32[]{:S(2)}) collective-permute-start(bf16[128,256]{1,0:T(8,128)(2,1)S(1)} %get-tuple-element.43.refs_0_), channel_id=1, source_target_pairs={{0,8},{4,12},{8,0},{12,4},{1,9},{5,13},{9,1},{13,5},{2,10},{6,14},... | collective-permute-start | bytes 196616 | tf_op jit(solution)/shard_map/ppermute | solution.py:31
  11.3 6.7 %collective-permute-start.5 = (bf16[128,256]{1,0:T(8,128)(2,1)S(1)}, bf16[128,256]{1,0:T(8,128)(2,1)S(1)}, u32[]{:S(2)}, u32[]{:S(2)}) collective-permute-start(bf16[128,256]{1,0:T(8,128)(2,1)S(1)} %get-tuple-element.44), channel_id=1, source_target_pairs={{0,12},{4,8},{8,4},{12,0},{1,13},{5,9},{9,5},{13,1},{2,14},{6,10},... | collective-permute-start | bytes 196616 | tf_op jit(solution)/shard_map/ppermute | solution.py:31
  12.6 5.9 %collective-permute-start.3 = (bf16[128,384]{1,0:T(8,128)(2,1)S(1)}, bf16[128,384]{1,0:T(8,128)(2,1)S(1)}, u32[]{:S(2)}, u32[]{:S(2)}) collective-permute-start(bf16[128,384]{1,0:T(8,128)(2,1)S(1)} %get-tuple-element.42), channel_id=1, source_target_pairs={{0,4},{4,0},{8,12},{12,8},{1,5},{5,1},{9,13},{13,9},{2,6},{6,2},{1... | collective-permute-start | bytes 294920 | tf_op jit(solution)/shard_map/ppermute | solution.py:31
  19.1 3.5 %collective-permute-start.9 = (bf16[128,128]{1,0:T(8,128)(2,1)S(1)}, bf16[128,128]{1,0:T(8,128)(2,1)S(1)}, u32[]{:S(2)}, u32[]{:S(2)}) collective-permute-start(bf16[128,128]{1,0:T(8,128)(2,1)S(1)} %get-tuple-element.48.mixed_ref), channel_id=1, source_target_pairs={{0,3},{1,2},{2,1},{3,0},{4,7},{5,6},{6,5},{7,4},{8,11},{9,10},{10,... | collective-permute-start | bytes 98312 | tf_op jit(solution)/shard_map/ppermute | solution.py:31
  20.0 4.2 %collective-permute-start.6 = (bf16[128,128]{1,0:T(8,128)(2,1)S(1)}, bf16[128,128]{1,0:T(8,128)(2,1)S(1)}, u32[]{:S(2)}, u32[]{:S(2)}) collective-permute-start(bf16[128,128]{1,0:T(8,128)(2,1)S(1)} %get-tuple-element.45), channel_id=1, source_target_pairs={{0,7},{1,6},{2,5},{3,4},{4,3},{5,2},{6,1},{7,0},{8,15},{9,14},{10,... | collective-permute-start | bytes 98312 | tf_op jit(solution)/shard_map/ppermute | solution.py:31
  20.8 3.9 %collective-permute-start.7 = (bf16[128,128]{1,0:T(8,128)(2,1)S(1)}, bf16[128,128]{1,0:T(8,128)(2,1)S(1)}, u32[]{:S(2)}, u32[]{:S(2)}) collective-permute-start(bf16[128,128]{1,0:T(8,128)(2,1)S(1)} %get-tuple-element.45), channel_id=1, source_target_pairs={{0,4},{1,5},{2,6},{3,7},{4,0},{5,1},{6,2},{7,3},{8,12},{9,13},{10,... | collective-permute-start | bytes 98312 | tf_op jit(solution)/shard_map/ppermute | solution.py:31
  24.9 1.5 %collective-permute-start.10 = (bf16[128,512]{1,0:T(8,128)(2,1)S(1)}, bf16[128,512]{1,0:T(8,128)(2,1)S(1)}, u32[]{:S(2)}, u32[]{:S(2)}) collective-permute-start(bf16[128,512]{1,0:T(8,128)(2,1)S(1)} %sent.1), channel_id=1, source_target_pairs={{0,1},{1,0},{2,3},{3,2},{4,5},{5,4},{6,7},{7,6},{8,9},{9,8},{10,11... | collective-permute-start | bytes 393224 | tf_op jit(solution)/shard_map/ppermute | solution.py:31

commit v8 on v6

--- a/solution.py
+++ b/solution.py
@@ -35,9 +35,13 @@
     return lax.optimization_barrier((value, *others))[0]
 
 
-def prepare_kernel(mp, step, gain_ref, probe_ref, lookup_ref, content_ref, exit_ref, *refs):
-    weight_refs, (sums_ref, gain_out_ref, own_ref, far_ref) = refs[:3], refs[3:7]
-    rows_ref, sems, gain_sem, exit_sems = refs[7:]
+def parity():
+    return lax.rem(lax.axis_index("seq"), 2)
+
+
+def prepare_kernel(mp, gain_ref, probe_ref, lookup_ref, content_ref, exit_ref, *refs):
+    weight_refs, (sums_ref, gain_out_ref, own_ref, twin_ref, far_ref) = refs[:3], refs[3:8]
+    rows_ref, sems, gain_sem, exit_sems = refs[8:]
     me = lax.axis_index("mp")
     depth, cols = probe_ref.shape
     parts = sems.shape[0]
@@ -52,14 +56,19 @@
             copy = pltpu.make_async_copy(ref.at[rows, :], weight_refs[i].at[rows, :], sems.at[c, i])
             copy.start()
             copies[c].append(copy)
-    half, _, width = own_ref.shape
+    half, deep, width = own_ref.shape
+    mine = pl.ds(pl.multiple_of(parity() * deep, deep), deep)
+    other = pl.ds(pl.multiple_of((1 - parity()) * deep, deep), deep)
     exits = []
-    for k in range(mp):
-        to = own_ref.at[k] if k < half else far_ref.at[k - half]
-        owner = me ^ k if k < half else me ^ step ^ (k - half)
-        columns = pl.ds(pl.multiple_of(owner * width, width), width)
-        exits.append(pltpu.make_async_copy(exit_ref.at[:, columns], to, exit_sems.at[k]))
-        exits[k].start()
+    for j, (to_ref, rows, distance) in enumerate(
+        ((own_ref, other, 0), (twin_ref, mine, 1), (far_ref, slice(None), half))
+    ):
+        for k in range(half):
+            columns = pl.ds(pl.multiple_of((me ^ distance ^ k) * width, width), width)
+            exits.append(
+                pltpu.make_async_copy(exit_ref.at[rows, columns], to_ref.at[k], exit_sems.at[j * half + k])
+            )
+            exits[-1].start()
     gain_copy.wait()
     gain = gain_out_ref[...]
     high = gain.astype(BF16)
@@ -81,16 +90,16 @@
         copy.wait()
 
 
-def prepare(mp, step, gain, probe, lookup, content, exit_matrix):
+def prepare(mp, gain, probe, lookup, content, exit_matrix):
     depth, cols = probe.shape
     deep, wide = exit_matrix.shape
     parts = 4
-    stack = pltpu.VMEM((mp // 2, deep, wide // mp), BF16)
-    probe, lookup, content, sums, gain, own, far = call(
-        functools.partial(prepare_kernel, mp, step),
+    half, stack = (pltpu.VMEM((mp // 2, d, wide // mp), BF16) for d in (deep // 2, deep))
+    probe, lookup, content, sums, gain, own, twin, far = call(
+        functools.partial(prepare_kernel, mp),
         "prepare",
         [pltpu.VMEM((depth, cols), BF16)] * 3
-        + [pltpu.VMEM((3, 8, cols), F32), pltpu.VMEM((1, depth), F32), stack, stack],
+        + [pltpu.VMEM((3, 8, cols), F32), pltpu.VMEM((1, depth), F32), half, half, stack],
         [
             pltpu.with_memory_space_constraint(w, pltpu.HBM)
             for w in (gain[None, :], probe, lookup, content, exit_matrix)
@@ -101,10 +110,10 @@
             pltpu.VMEM((32, depth), BF16),
             pltpu.SemaphoreType.DMA((parts, 3)),
             pltpu.SemaphoreType.DMA,
-            pltpu.SemaphoreType.DMA((mp,)),
+            pltpu.SemaphoreType.DMA((3 * mp // 2,)),
         ],
     )
-    return (probe, lookup, content), sums, gain, own, far
+    return (probe, lookup, content), sums, gain, own, twin, far
 
 
 def matmul(blocks, places, weight_ref):
@@ -149,15 +158,11 @@
         stats_ref[i] = jnp.broadcast_to(value, stats_ref.shape[1:])
 
 
-def parity():
-    return lax.rem(lax.axis_index("seq"), 2)
-
-
 def late_kernel(places, depth, *refs):
     count = len(places)
     blocks, refs = refs[:count], refs[count:]
     weight_refs, (gain_ref, sums_ref, stats_ref, factor_ref), product_refs = refs[:3], refs[3:7], refs[7:10]
-    queries_ref, mine_ref, other_ref, bundle_ref = refs[10:]
+    out_refs = refs[10:]
     one, two, products = take_in(blocks, places, stats_ref[0, :, 0:1], gain_ref, weight_refs)
     offset = (one + stats_ref[1, :, 0:1]) / depth
     scale = lax.rsqrt((two + stats_ref[2, :, 0:1]) / depth - offset * offset + 1e-05)
@@ -171,15 +176,13 @@
         half = product.shape[1] // 2
         low, high = product[:, :half], product[:, half:]
         parts.append([jnp.where(first, *v).astype(BF16) for v in ((low, high), (high, low))])
-    for i in range(2):
-        for h in range(half // LANES):
-            span = slice(h * LANES, (h + 1) * LANES)
-            to = pl.ds((2 * h + i) * LANES, LANES)
-            mine_ref[:, to] = parts[i + 1][0][:, span]
-            other_ref[:, to] = parts[i + 1][1][:, span]
-            bundle_ref[:, to] = parts[i + 1][1][:, span]
-    queries_ref[...] = parts[0][0]
-    bundle_ref[:, pl.ds(2 * half, half)] = parts[0][1]
+    for g in range(2):
+        for ref in out_refs[2 * g : 2 * g + 2]:
+            for i in range(2):
+                for h in range(half // LANES):
+                    part = parts[i + 1][g][:, h * LANES : (h + 1) * LANES]
+                    ref[:, pl.ds((2 * h + i) * LANES, LANES)] = part
+        out_refs[2 * g + 1][:, pl.ds(2 * half, half)] = parts[0][g]
 
 
 def project(blocks, places, weights, sums, gain, factor):
@@ -198,7 +201,7 @@
     return call(
         functools.partial(late_kernel, places[-1:], count * width),
         "late",
-        [pltpu.VMEM((rows, cols // 2), BF16), pair, pair, pltpu.VMEM((rows, 3 * cols // 2), BF16)],
+        [pair, pltpu.VMEM((rows, 3 * cols // 2), BF16)] * 2,
         [blocks[-1], *weights, gain, sums, stats, factor, *products],
     )
 
@@ -209,14 +212,11 @@
         refs[-1][pl.ds(i * rows, rows), :] = ref[...]
 
 
-def attend_kernel(count, mine_ref, bundle_ref, *refs):
-    blocks, out_refs = refs[:count], refs[count:]
-    half = mine_ref.shape[1]
-    rows = mine_ref.shape[0]
+def attend_kernel(*refs):
+    bundles, blocks, out_refs = refs[:2], refs[:3], refs[3:]
+    rows, half = out_refs[0].shape
     for h in range(half // LANES):
-        q = jnp.concatenate(
-            [mine_ref[:, pl.ds(h * LANES, LANES)], bundle_ref[:, pl.ds(2 * half + h * LANES, LANES)]], axis=0
-        )
+        q = jnp.concatenate([b[:, pl.ds(2 * half + h * LANES, LANES)] for b in bundles], axis=0)
         scores = [
             lax.dot_general(
                 q, b[:, pl.ds(2 * h * LANES, LANES)], (((1,), (1,)), ((), ())), preferred_element_type=F32
@@ -237,7 +237,7 @@
             ref[:, pl.ds(h * LANES, LANES)] = out[i * rows : (i + 1) * rows, :]
 
 
-def attend(queries, bundle, blocks):
+def attend(bundles, blocks):
     rows, wide = blocks[0].shape
     (merged,) = call(
         merge_kernel,
@@ -246,32 +246,38 @@
         blocks,
         work=30000 * rows * wide * len(blocks),
     )
-    size = merged.shape[0]
+    (beside,) = call(
+        merge_kernel,
+        "hold",
+        [pltpu.VMEM(bundles[1].shape, BF16)],
+        bundles[1:],
+        work=30000 * rows * wide,
+    )
     return call(
-        functools.partial(attend_kernel, 2),
+        attend_kernel,
         "attend",
-        [pltpu.VMEM(queries.shape, BF16)] * 2,
-        [queries, bundle, bundle, merged],
-        limit=56 if size > 2048 else 16,
+        [pltpu.VMEM((rows, wide // 2), BF16)] * 2,
+        [bundles[0], beside, merged],
+        limit=56 if merged.shape[0] > 2048 else 16,
     )
 
 
 def own_kernel(x_ref, mixed_ref, exit_ref, *out_refs):
-    deep = mixed_ref.shape[1]
-    rows = pl.ds(pl.multiple_of(parity() * deep, deep), deep)
     for k, ref in enumerate(out_refs):
-        part = jnp.dot(mixed_ref[...], exit_ref[k, rows, :], preferred_element_type=F32)
+        part = jnp.dot(mixed_ref[...], exit_ref[k], preferred_element_type=F32)
         ref[...] = part + x_ref[...].astype(F32) if k == 0 else part
 
 
-def add_kernel(which, flips, *refs):
-    count, values = len(which), len(flips)
+def add_kernel(which, halves, *refs):
+    count, values = len(which), len(halves)
     for i, k in enumerate(which):
         total = refs[2 * values + i][...]
-        for j, flip in enumerate(flips):
+        for j, half in enumerate(halves):
             deep = refs[j].shape[1]
-            at = 1 - parity() if flip else parity()
-            rows = pl.ds(pl.multiple_of(at * deep, deep), deep)
+            rows = slice(None)
+            if half is not None:
+                at = 1 - parity() if half else parity()
+                rows = pl.ds(pl.multiple_of(at * deep, deep), deep)
             total += jnp.dot(refs[j][...], refs[values + j][k, rows, :], preferred_element_type=F32)
         out_ref = refs[2 * values + count + i]
         out_ref[...] = total.astype(out_ref.dtype)
@@ -286,7 +292,7 @@
     step = top | 1
     factor = jnp.repeat(softness * (math.log2(math.e) / math.sqrt(span)), span)[None, :]
 
-    weights, sums, gains, own, far = prepare(mp, step, gain, probe, lookup, content, exit_matrix)
+    weights, sums, gains, own, twin, far = prepare(mp, gain, probe, lookup, content, exit_matrix)
     blocks, distance = {0: node_vectors}, top
     while distance:
         new = {k ^ distance: swap(b, "mp", mp, distance) for k, b in blocks.items()}
@@ -295,24 +301,26 @@
         blocks.update(new)
         distance //= 2
     places = range(mp)
-    queries, mine, other, bundle = project(
+    mine, mine_bundle, other, other_bundle = project(
         [blocks[k] for k in places], places, weights, sums, gains, factor
     )
-    theirs = swap(far, "mp", mp, step)
-
-    found = {0: mine}
-    for k in sorted(range(1, seq), key=lambda k: (k == 1, k)):
-        found[k] = swap(bundle if k == 1 else other if k % 2 else mine, "seq", seq, k)
-    mixed, mixed_beside = attend(queries, found[1], [found[k] for k in range(seq) if k != 1])
+    theirs = swap(far, "mp", mp, top)
+
+    both = ("seq", "mp")
+    found = {}
+    for k in range(2, seq):
+        found[k] = swap(other if k % 2 else mine, both, seq * mp, k * mp + 1)
+    bundles = [swap(after(mine_bundle, found[2]), "mp", mp, 1), swap(other_bundle, both, seq * mp, mp + 1)]
+    twins = swap(after(twin, found[2]), "mp", mp, 1)
+    mixed, mixed_beside = attend(bundles, [found[k] for k in range(2, seq)])
 
     rows, width = node_vectors.shape
     product, half = pltpu.VMEM((rows, width), F32), pltpu.VMEM((rows, width), BF16)
-    both = ("seq", "mp")
     across = swap(mixed, both, seq * mp, step)
-    beside = swap(mixed_beside, both, seq * mp, mp)
+    beside = swap(mixed_beside, both, seq * mp, mp + 1)
     corner = swap(mixed_beside, both, seq * mp, mp + step)
     parts = call(
-        own_kernel, "own", [product] * top, [node_vectors, mixed, own], work=1 * rows * own.size
+        own_kernel, "own", [product] * top, [node_vectors, mixed, twins], work=1 * rows * own.size
     )
     parts = call(
         functools.partial(add_kernel, range(top), (0, 1)),
@@ -322,10 +330,13 @@
         work=64 * rows * own.size,
     )
     sent = call(
-        functools.partial(add_kernel, range(1, top), (1,)), "sent", [half] * (top - 1), [beside, own, *parts[1:]]
+        functools.partial(add_kernel, range(1, top), (None,)),
+        "sent",
+        [half] * (top - 1),
+        [beside, own, *parts[1:]],
     )
     (kept,) = call(
-        functools.partial(add_kernel, range(1), (1,)),
+        functools.partial(add_kernel, range(1), (None,)),
         "kept",
         [product],
         [beside, own, parts[0]],

time: 27.5 us -> 27 us (0.982)
  waiting for transfers between devices: 9.56 us -> 8.13 us
  starting transfers between devices: 11.7 us -> 12.5 us
    ppermute x11 -> x13, waiting for transfers between devices: 9.56 us -> 8.13 us  [swap(): return lax.ppermute(block, axis, [(i, i ^ distance) for i in range(count)])]
    ppermute x11 -> x13, starting transfers between devices: 11.7 us -> 12.5 us  [swap(): return lax.ppermute(block, axis, [(i, i ^ distance) for i in range(count)])]
    pallas_call x9 -> x10, Pallas kernels: 5.24 us -> 5.38 us  [call(): pl.pallas_call(kernel, out_shape=out_shape, in_specs=specs or [VMEM] * le...]
  transfers between devices with their start and end apart: 11 -> 13, of which waited for: 8 -> 8; matrix products, arithmetic and copies ran while one was open for 0% -> 0% of each run, Pallas kernels for 18% -> 19%
where the time goes in v8:
time: 27 us; the launch traced here: 26.9 us
  starting transfers between devices  12.5 us (46%)
  waiting for transfers between devices  8.13 us (30%)
  Pallas kernels  5.38 us (20%)
  other arithmetic  0.68 us (3%)
    ppermute x13, starting transfers between devices, swap(): return lax.ppermute(block, axis, [(i, i ^ distance) for i in range(count)])  12.5 us
    ppermute x13, waiting for transfers between devices, swap(): return lax.ppermute(block, axis, [(i, i ^ distance) for i in range(count)])  8.13 us
    pallas_call x10, Pallas kernels, call(): pl.pallas_call(kernel, out_shape=out_shape, in_specs=specs or [VMEM] * le...  5.38 us
    convert_element_type x1, other arithmetic, per_device(): return shares[0].astype(node_vectors.dtype)  0.68 us
  transfers between devices with their start and end apart: 13, of which 8 were waited for; matrix products, arithmetic and copies ran while one was open for 0% of the time, Pallas kernels for 19%

profile of v8, /device:TPU:0, one launch (start us, length us, event | category | flops | bytes accessed | tf_op | source)
XLA Modules:
  0.0 26.9 jit_solution(7855307033117452866)
XLA Ops:
  0.0 2.9 %collective-permute-start = (bf16[128,512]{1,0:T(8,128)(2,1)}, bf16[128,512]{1,0:T(8,128)(2,1)S(1)}, u32[]{:S(2)}, u32[]{:S(2)}) collective-permute-start(bf16[128,512]{1,0:T(8,128)(2,1)} %x_ref.1), channel_id=1, source_target_pairs={{0,2},{1,3},{2,0},{3,1},{4,6},{5,7},{6,4},{7,5},{8,10},{9,11},{10,... | collective-permute-start | bytes 393224 | tf_op jit(solution)/shard_map/ppermute | solution.py:31
  2.9 0.0 collective-permute-start.2
  2.9 0.0 copy-start
  2.9 3.1 %prepare.1 = (bf16[2048,256]{1,0:T(8,128)(2,1)S(1)}, bf16[2048,256]{1,0:T(8,128)(2,1)S(1)}, bf16[2048,256]{1,0:T(8,128)(2,1)S(1)}, f32[3,8,256]{2,1,0:T(8,128)S(...) custom-call(f32[1,2048]{1,0:T(1,128)} %bitcast.3, ...), custom_call_target="tpu_custom_call" | custom-call | flops 25165824 | bytes 393216 | tf_op jit(solution)/shard_map/prepare/pallas_call | solution.py:18
  6.0 0.0 copy-start.1
  6.0 0.1 collective-permute-start.10
  6.1 0.5 %collective-permute-done.refs_2_ = bf16[128,512]{1,0:T(8,128)(2,1)S(1)} collective-permute-done((bf16[128,512]{1,0:T(8,128)(2,1)}, bf16[128,512]{1,0:T(8,128)(2,1)S(1)}, u32[]{:S(2)}, u32[]{:S(2)}) %collective-permute-start) | collective-permute-done | bytes 131104 | tf_op jit(solution)/shard_map/ppermute | solution.py:31
  6.6 0.0 collective-permute-start.1
  6.7 0.0 copy-done.1
  6.7 0.0 collective-permute-done.2.refs_1_
  6.7 0.1 broadcast_in_dim.7
  6.8 0.0 copy-done
  6.8 0.6 %early.1 = (f32[3,128,128]{2,1,0:T(8,128)S(1)}, f32[128,256]{1,0:T(8,128)S(1)}, f32[128,256]{1,0:T(8,128)S(1)}, f32[128,256]{1,0:T(8,128)S(1)}, f32[1,256]{1,0:T(1,128)S(1)}) custom-call(bf16[128,512]{1,0:T(8,128)(2,1)S(1)} %copy-done, bf16[128,512]{1,0:T(8,128)(2,1)S(1)} %collective-permute-done.2.refs_1_, ...), custom_call_target="tpu_custom_call" | custom-call | flops 1073741824 | bytes 16777216 | tf_op jit(solution)/shard_map/early/pallas_call | solution.py:18
  7.4 0.6 %collective-permute-done.1.refs_0_ = bf16[128,512]{1,0:T(8,128)(2,1)S(1)} collective-permute-done((bf16[128,512]{1,0:T(8,128)(2,1)S(1)}, bf16[128,512]{1,0:T(8,128)(2,1)S(1)}, u32[]{:S(2)}, u32[]{:S(2)}) %collective-permute-start.1) | collective-permute-done | bytes 131104 | tf_op jit(solution)/shard_map/ppermute | solution.py:31
  8.0 0.4 %late.1 = (bf16[128,256]{1,0:T(8,128)(2,1)S(1)}, bf16[128,384]{1,0:T(8,128)(2,1)S(1)}, bf16[128,256]{1,0:T(8,128)(2,1)S(1)}, bf16[128,384]{1,0:T(8,128)(2,1)S(1)}) custom-call(bf16[128,512]{1,0:T(8,128)(2,1)S(1)} %collective-permute-done.1.refs_0_, bf16[2048,256]{1,0:T(8,128)(2,1)S(1)} %get-tuple-element.34.refs_3_.refs_1_, ...), custom_call_target="tpu_custom_call" | custom-call | tf_op jit(solution)/shard_map/late/pallas_call | solution.py:18
  8.4 2.7 %collective-permute-start.3 = (bf16[128,256]{1,0:T(8,128)(2,1)S(1)}, bf16[128,256]{1,0:T(8,128)(2,1)S(1)}, u32[]{:S(2)}, u32[]{:S(2)}) collective-permute-start(bf16[128,256]{1,0:T(8,128)(2,1)S(1)} %get-tuple-element.45), channel_id=1, source_target_pairs={{0,9},{1,8},{2,11},{3,10},{4,13},{5,12},{6,15},{7,14},{8,1},{9,0},... | collective-permute-start | bytes 196616 | tf_op jit(solution)/shard_map/ppermute | solution.py:31
  11.0 1.3 %collective-permute-start.6 = (bf16[128,256]{1,0:T(8,128)(2,1)S(1)}, bf16[128,256]{1,0:T(8,128)(2,1)S(1)}, u32[]{:S(2)}, u32[]{:S(2)}) collective-permute-start(bf16[128,256]{1,0:T(8,128)(2,1)S(1)} %get-tuple-element.48), channel_id=1, source_target_pairs={{0,13},{1,12},{2,15},{3,14},{4,9},{5,8},{6,11},{7,10},{8,5},{9,4},... | collective-permute-start | bytes 196616 | tf_op jit(solution)/shard_map/ppermute | solution.py:31
  12.3 0.2 collective-permute-start.5
  12.6 0.9 %collective-permute-done.3.refs_0_ = bf16[128,256]{1,0:T(8,128)(2,1)S(1)} collective-permute-done((bf16[128,256]{1,0:T(8,128)(2,1)S(1)}, bf16[128,256]{1,0:T(8,128)(2,1)S(1)}, u32[]{:S(2)}, u32[]{:S(2)}) %collective-permute-start.3) | collective-permute-done | bytes 65568 | tf_op jit(solution)/shard_map/ppermute | solution.py:31
  13.5 1.4 %collective-permute-start.4 = (bf16[128,384]{1,0:T(8,128)(2,1)S(1)}, bf16[128,384]{1,0:T(8,128)(2,1)S(1)}, u32[]{:S(2)}, u32[]{:S(2)}) collective-permute-start(bf16[128,384]{1,0:T(8,128)(2,1)S(1)} %get-tuple-element.46), channel_id=1, source_target_pairs={{0,1},{1,0},{2,3},{3,2},{4,5},{5,4},{6,7},{7,6},{8,9},{9,8},{10,11... | collective-permute-start | bytes 294920 | tf_op jit(solution)/shard_map/ppermute | solution.py:31
  14.9 0.0 collective-permute-start.11
  14.9 2.0 %collective-permute-done.6.refs_1_ = bf16[128,256]{1,0:T(8,128)(2,1)S(1)} collective-permute-done((bf16[128,256]{1,0:T(8,128)(2,1)S(1)}, bf16[128,256]{1,0:T(8,128)(2,1)S(1)}, u32[]{:S(2)}, u32[]{:S(2)}) %collective-permute-start.6) | collective-permute-done | bytes 65568 | tf_op jit(solution)/shard_map/ppermute | solution.py:31
  16.9 1.6 %collective-permute-done.5.refs_0_ = bf16[128,384]{1,0:T(8,128)(2,1)S(1)} collective-permute-done((bf16[128,384]{1,0:T(8,128)(2,1)S(1)}, bf16[128,384]{1,0:T(8,128)(2,1)S(1)}, u32[]{:S(2)}, u32[]{:S(2)}) %collective-permute-start.5) | collective-permute-done | bytes 98336 | tf_op jit(solution)/shard_map/ppermute | solution.py:31
  18.5 0.0 collective-permute-done.4.refs_0_
  18.5 0.5 %attend.1 = (bf16[128,128]{1,0:T(8,128)(2,1)S(1)}, bf16[128,128]{1,0:T(8,128)(2,1)S(1)}) custom-call(bf16[128,384]{1,0:T(8,128)(2,1)S(1)} %collective-permute-done.4.refs_0_, bf16[128,384]{1,0:T(8,128)(2,1)S(1)} %hold.1.refs_1_, bf16[256,256]{1,0:T(8,128)(2,1)S(1)} %merge.1.refs_2_), custom_call_target="tpu_custom_call" | custom-call | tf_op jit(solution)/shard_map/attend/pallas_call | solution.py:18
  19.1 1.4 %collective-permute-start.9 = (bf16[128,128]{1,0:T(8,128)(2,1)S(1)}, bf16[128,128]{1,0:T(8,128)(2,1)S(1)}, u32[]{:S(2)}, u32[]{:S(2)}) collective-permute-start(bf16[128,128]{1,0:T(8,128)(2,1)S(1)} %get-tuple-element.49), channel_id=1, source_target_pairs={{0,7},{1,6},{2,5},{3,4},{4,3},{5,2},{6,1},{7,0},{8,15},{9,14},{10,... | collective-permute-start | bytes 98312 | tf_op jit(solution)/shard_map/ppermute | solution.py:31
  20.5 0.4 %collective-permute-start.8 = (bf16[128,128]{1,0:T(8,128)(2,1)S(1)}, bf16[128,128]{1,0:T(8,128)(2,1)S(1)}, u32[]{:S(2)}, u32[]{:S(2)}) collective-permute-start(bf16[128,128]{1,0:T(8,128)(2,1)S(1)} %get-tuple-element.51.mixed_ref), channel_id=1, source_target_pairs={{0,3},{1,2},{2,1},{3,0},{4,7},{5,6},{6,5},{7,4},{8,11},{9,10},{10,... | collective-permute-start | bytes 98312 | tf_op jit(solution)/shard_map/ppermute | solution.py:31
  20.9 1.5 %collective-permute-start.7 = (bf16[128,128]{1,0:T(8,128)(2,1)S(1)}, bf16[128,128]{1,0:T(8,128)(2,1)S(1)}, u32[]{:S(2)}, u32[]{:S(2)}) collective-permute-start(bf16[128,128]{1,0:T(8,128)(2,1)S(1)} %get-tuple-element.49), channel_id=1, source_target_pairs={{0,5},{1,4},{2,7},{3,6},{4,1},{5,0},{6,3},{7,2},{8,13},{9,12},{10,... | collective-permute-start | bytes 98312 | tf_op jit(solution)/shard_map/ppermute | solution.py:31
  22.4 0.0 collective-permute-done.11.exit_ref
  22.4 0.2 own.1
  22.6 0.7 %collective-permute-done.9.refs_1_ = bf16[128,128]{1,0:T(8,128)(2,1)S(1)} collective-permute-done((bf16[128,128]{1,0:T(8,128)(2,1)S(1)}, bf16[128,128]{1,0:T(8,128)(2,1)S(1)}, u32[]{:S(2)}, u32[]{:S(2)}) %collective-permute-start.9) | collective-permute-done | bytes 32800 | tf_op jit(solution)/shard_map/ppermute | solution.py:31
  23.4 0.9 %collective-permute-done.8.refs_0_ = bf16[128,128]{1,0:T(8,128)(2,1)S(1)} collective-permute-done((bf16[128,128]{1,0:T(8,128)(2,1)S(1)}, bf16[128,128]{1,0:T(8,128)(2,1)S(1)}, u32[]{:S(2)}, u32[]{:S(2)}) %collective-permute-start.8) | collective-permute-done | bytes 32800 | tf_op jit(solution)/shard_map/ppermute | solution.py:31
  24.2 0.0 collective-permute-done.10.refs_2_.refs_3_
  24.2 0.3 %crossed.1 = (f32[128,512]{1,0:T(8,128)S(1)}, f32[128,512]{1,0:T(8,128)S(1)}) custom-call(bf16[128,128]{1,0:T(8,128)(2,1)S(1)} %collective-permute-done.8.refs_0_, bf16[128,128]{1,0:T(8,128)(2,1)S(1)} %collective-permute-done.9.refs_1_, bf16[2,256,512]{2,1,0:T(8,128)(2,1)S(1)} %collective-permute-done.10.refs_2_.refs_3_, ...), custom_call_target="tpu_custom_call" | custom-call | flops 1073741824 | bytes 16777216 | tf_op jit(solution)/shard_map/crossed/pallas_call | solution.py:18
  24.5 0.0 collective-permute-done.7.refs_0_
  24.6 0.2 sent.1
  24.7 0.4 %collective-permute-start.12 = (bf16[128,512]{1,0:T(8,128)(2,1)S(1)}, bf16[128,512]{1,0:T(8,128)(2,1)S(1)}, u32[]{:S(2)}, u32[]{:S(2)}) collective-permute-start(bf16[128,512]{1,0:T(8,128)(2,1)S(1)} %sent.1), channel_id=1, source_target_pairs={{0,1},{1,0},{2,3},{3,2},{4,5},{5,4},{6,7},{7,6},{8,9},{9,8},{10,11... | collective-permute-start | bytes 393224 | tf_op jit(solution)/shard_map/ppermute | solution.py:31
  25.2 0.2 kept.1
  25.4 0.8 %collective-permute-done.12 = bf16[128,512]{1,0:T(8,128)(2,1)S(1)} collective-permute-done((bf16[128,512]{1,0:T(8,128)(2,1)S(1)}, bf16[128,512]{1,0:T(8,128)(2,1)S(1)}, u32[]{:S(2)}, u32[]{:S(2)}) %collective-permute-start.12) | collective-permute-done | bytes 131104 | tf_op jit(solution)/shard_map/ppermute | solution.py:31
  26.2 0.7 %add_convert_fusion = bf16[128,512]{1,0:T(8,128)(2,1)} fusion(f32[128,512]{1,0:T(8,128)S(1)} %kept.1, bf16[128,512]{1,0:T(8,128)(2,1)S(1)} %collective-permute-done.12), kind=kLoop, calls=%fused_computation | loop fusion | flops 196608 | bytes 524288 | tf_op jit(solution)/shard_map/convert_element_type | solution.py:355
  (3 shorter events, 0.0 us)
Async XLA Ops:
  0.0 6.6 %collective-permute-start = (bf16[128,512]{1,0:T(8,128)(2,1)}, bf16[128,512]{1,0:T(8,128)(2,1)S(1)}, u32[]{:S(2)}, u32[]{:S(2)}) collective-permute-start(bf16[128,512]{1,0:T(8,128)(2,1)} %x_ref.1), channel_id=1, source_target_pairs={{0,2},{1,3},{2,0},{3,1},{4,6},{5,7},{6,4},{7,5},{8,10},{9,11},{10,... | collective-permute-start | bytes 393224 | tf_op jit(solution)/shard_map/ppermute | solution.py:31
  2.9 3.8 %collective-permute-start.2 = (bf16[128,512]{1,0:T(8,128)(2,1)}, bf16[128,512]{1,0:T(8,128)(2,1)S(1)}, u32[]{:S(2)}, u32[]{:S(2)}) collective-permute-start(bf16[128,512]{1,0:T(8,128)(2,1)} %x_ref.1), channel_id=1, source_target_pairs={{0,1},{1,0},{2,3},{3,2},{4,5},{5,4},{6,7},{7,6},{8,9},{9,8},{10,11... | collective-permute-start | bytes 393224 | tf_op jit(solution)/shard_map/ppermute | solution.py:31
  2.9 3.8 %copy-start = (bf16[128,512]{1,0:T(8,128)(2,1)S(1)}, bf16[128,512]{1,0:T(8,128)(2,1)}, u32[]{:S(2)}) copy-start(bf16[128,512]{1,0:T(8,128)(2,1)} %x_ref.1) | copy-start | bytes 393220
  6.0 0.7 %copy-start.1 = (f32[2]{0:T(128)S(1)}, f32[2]{0:T(128)}, u32[]{:S(2)}) copy-start(f32[2]{0:T(128)} %param.12) | copy-start | bytes 28
  6.0 18.2 %collective-permute-start.10 = (bf16[2,256,512]{2,1,0:T(8,128)(2,1)S(1)}, bf16[2,256,512]{2,1,0:T(8,128)(2,1)S(1)}, u32[]{:S(2)}, u32[]{:S(2)}) collective-permute-start(bf16[2,256,512]{2,1,0:T(8,128)(2,1)S(1)} %get-tuple-element.52), channel_id=1, source_target_pairs={{0,2},{1,3},{2,0},{3,1},{4,6},{5,7},{6,4},{7,5},{8,10},{9,11},{10,... | collective-permute-start | bytes 1572872 | tf_op jit(solution)/shard_map/ppermute | solution.py:31
  6.6 1.3 %collective-permute-start.1 = (bf16[128,512]{1,0:T(8,128)(2,1)S(1)}, bf16[128,512]{1,0:T(8,128)(2,1)S(1)}, u32[]{:S(2)}, u32[]{:S(2)}) collective-permute-start(bf16[128,512]{1,0:T(8,128)(2,1)S(1)} %collective-permute-done.refs_2_), channel_id=1, source_target_pairs={{0,1},{1,0},{2,3},{3,2},{4,5},{5,4},{6,7},{7,6},{8,9},{9,8},{10,11... | collective-permute-start | bytes 393224 | tf_op jit(solution)/shard_map/ppermute | solution.py:31
  8.4 5.2 %collective-permute-start.3 = (bf16[128,256]{1,0:T(8,128)(2,1)S(1)}, bf16[128,256]{1,0:T(8,128)(2,1)S(1)}, u32[]{:S(2)}, u32[]{:S(2)}) collective-permute-start(bf16[128,256]{1,0:T(8,128)(2,1)S(1)} %get-tuple-element.45), channel_id=1, source_target_pairs={{0,9},{1,8},{2,11},{3,10},{4,13},{5,12},{6,15},{7,14},{8,1},{9,0},... | collective-permute-start | bytes 196616 | tf_op jit(solution)/shard_map/ppermute | solution.py:31
  11.0 5.9 %collective-permute-start.6 = (bf16[128,256]{1,0:T(8,128)(2,1)S(1)}, bf16[128,256]{1,0:T(8,128)(2,1)S(1)}, u32[]{:S(2)}, u32[]{:S(2)}) collective-permute-start(bf16[128,256]{1,0:T(8,128)(2,1)S(1)} %get-tuple-element.48), channel_id=1, source_target_pairs={{0,13},{1,12},{2,15},{3,14},{4,9},{5,8},{6,11},{7,10},{8,5},{9,4},... | collective-permute-start | bytes 196616 | tf_op jit(solution)/shard_map/ppermute | solution.py:31
  12.3 6.2 %collective-permute-start.5 = (bf16[128,384]{1,0:T(8,128)(2,1)S(1)}, bf16[128,384]{1,0:T(8,128)(2,1)S(1)}, u32[]{:S(2)}, u32[]{:S(2)}) collective-permute-start(bf16[128,384]{1,0:T(8,128)(2,1)S(1)} %get-tuple-element.47), channel_id=1, source_target_pairs={{0,5},{1,4},{2,7},{3,6},{4,1},{5,0},{6,3},{7,2},{8,13},{9,12},{10,... | collective-permute-start | bytes 294920 | tf_op jit(solution)/shard_map/ppermute | solution.py:31
  13.5 5.0 %collective-permute-start.4 = (bf16[128,384]{1,0:T(8,128)(2,1)S(1)}, bf16[128,384]{1,0:T(8,128)(2,1)S(1)}, u32[]{:S(2)}, u32[]{:S(2)}) collective-permute-start(bf16[128,384]{1,0:T(8,128)(2,1)S(1)} %get-tuple-element.46), channel_id=1, source_target_pairs={{0,1},{1,0},{2,3},{3,2},{4,5},{5,4},{6,7},{7,6},{8,9},{9,8},{10,11... | collective-permute-start | bytes 294920 | tf_op jit(solution)/shard_map/ppermute | solution.py:31
  14.9 7.5 %collective-permute-start.11 = (bf16[2,128,512]{2,1,0:T(8,128)(2,1)S(1)}, bf16[2,128,512]{2,1,0:T(8,128)(2,1)S(1)}, u32[]{:S(2)}, u32[]{:S(2)}) collective-permute-start(bf16[2,128,512]{2,1,0:T(8,128)(2,1)S(1)} %get-tuple-element.54), channel_id=1, source_target_pairs={{0,1},{1,0},{2,3},{3,2},{4,5},{5,4},{6,7},{7,6},{8,9},{9,8},{10,11... | collective-permute-start | bytes 786440 | tf_op jit(solution)/shard_map/ppermute | solution.py:31
  19.1 4.3 %collective-permute-start.9 = (bf16[128,128]{1,0:T(8,128)(2,1)S(1)}, bf16[128,128]{1,0:T(8,128)(2,1)S(1)}, u32[]{:S(2)}, u32[]{:S(2)}) collective-permute-start(bf16[128,128]{1,0:T(8,128)(2,1)S(1)} %get-tuple-element.49), channel_id=1, source_target_pairs={{0,7},{1,6},{2,5},{3,4},{4,3},{5,2},{6,1},{7,0},{8,15},{9,14},{10,... | collective-permute-start | bytes 98312 | tf_op jit(solution)/shard_map/ppermute | solution.py:31
  20.5 3.8 %collective-permute-start.8 = (bf16[128,128]{1,0:T(8,128)(2,1)S(1)}, bf16[128,128]{1,0:T(8,128)(2,1)S(1)}, u32[]{:S(2)}, u32[]{:S(2)}) collective-permute-start(bf16[128,128]{1,0:T(8,128)(2,1)S(1)} %get-tuple-element.51.mixed_ref), channel_id=1, source_target_pairs={{0,3},{1,2},{2,1},{3,0},{4,7},{5,6},{6,5},{7,4},{8,11},{9,10},{10,... | collective-permute-start | bytes 98312 | tf_op jit(solution)/shard_map/ppermute | solution.py:31
  20.9 3.7 %collective-permute-start.7 = (bf16[128,128]{1,0:T(8,128)(2,1)S(1)}, bf16[128,128]{1,0:T(8,128)(2,1)S(1)}, u32[]{:S(2)}, u32[]{:S(2)}) collective-permute-start(bf16[128,128]{1,0:T(8,128)(2,1)S(1)} %get-tuple-element.49), channel_id=1, source_target_pairs={{0,5},{1,4},{2,7},{3,6},{4,1},{5,0},{6,3},{7,2},{8,13},{9,12},{10,... | collective-permute-start | bytes 98312 | tf_op jit(solution)/shard_map/ppermute | solution.py:31
  24.7 1.4 %collective-permute-start.12 = (bf16[128,512]{1,0:T(8,128)(2,1)S(1)}, bf16[128,512]{1,0:T(8,128)(2,1)S(1)}, u32[]{:S(2)}, u32[]{:S(2)}) collective-permute-start(bf16[128,512]{1,0:T(8,128)(2,1)S(1)} %sent.1), channel_id=1, source_target_pairs={{0,1},{1,0},{2,3},{3,2},{4,5},{5,4},{6,7},{7,6},{8,9},{9,8},{10,11... | collective-permute-start | bytes 393224 | tf_op jit(solution)/shard_map/ppermute | solution.py:31

commit v9 on v8

--- a/solution.py
+++ b/solution.py
@@ -322,24 +322,24 @@
     parts = call(
         own_kernel, "own", [product] * top, [node_vectors, mixed, twins], work=1 * rows * own.size
     )
-    parts = call(
-        functools.partial(add_kernel, range(top), (0, 1)),
+    crossed = call(
+        functools.partial(add_kernel, range(1, top), (1, 0)),
         "crossed",
-        [product] * top,
-        [across, corner, theirs, theirs, *parts],
+        [product] * (top - 1),
+        [corner, across, theirs, theirs, *parts[1:]],
         work=64 * rows * own.size,
     )
     sent = call(
         functools.partial(add_kernel, range(1, top), (None,)),
         "sent",
         [half] * (top - 1),
-        [beside, own, *parts[1:]],
+        [beside, own, *crossed],
     )
     (kept,) = call(
-        functools.partial(add_kernel, range(1), (None,)),
+        functools.partial(add_kernel, range(1), (1, 0, None)),
         "kept",
         [product],
-        [beside, own, parts[0]],
+        [corner, across, beside, theirs, theirs, own, parts[0]],
         work=64 * rows * own.size,
     )
     shares = {0: kept, **{k: sent[k - 1] for k in range(1, top)}}

time: 27 us -> 27 us (level)
  transfers between devices with their start and end apart: 13 -> 13, of which waited for: 8 -> 9; matrix products, arithmetic and copies ran while one was open for 0% -> 0% of each run, Pallas kernels for 19% -> 19%
where the time goes in v9:
time: 27 us; the launch traced here: 26.8 us
  starting transfers between devices  12.4 us (46%)
  waiting for transfers between devices  8.18 us (30%)
  Pallas kernels  5.39 us (20%)
  other arithmetic  0.68 us (3%)
    ppermute x13, starting transfers between devices, swap(): return lax.ppermute(block, axis, [(i, i ^ distance) for i in range(count)])  12.4 us
    ppermute x13, waiting for transfers between devices, swap(): return lax.ppermute(block, axis, [(i, i ^ distance) for i in range(count)])  8.18 us
    pallas_call x10, Pallas kernels, call(): pl.pallas_call(kernel, out_shape=out_shape, in_specs=specs or [VMEM] * le...  5.39 us
    convert_element_type x1, other arithmetic, per_device(): return shares[0].astype(node_vectors.dtype)  0.68 us
  transfers between devices with their start and end apart: 13, of which 9 were waited for; matrix products, arithmetic and copies ran while one was open for 0% of the time, Pallas kernels for 19%

profile of v9, /device:TPU:0, one launch (start us, length us, event | category | flops | bytes accessed | tf_op | source)
XLA Modules:
  0.0 26.8 jit_solution(14808317907830433834)
XLA Ops:
  0.0 2.9 %collective-permute-start = (bf16[128,512]{1,0:T(8,128)(2,1)}, bf16[128,512]{1,0:T(8,128)(2,1)S(1)}, u32[]{:S(2)}, u32[]{:S(2)}) collective-permute-start(bf16[128,512]{1,0:T(8,128)(2,1)} %x_ref.1), channel_id=1, source_target_pairs={{0,2},{1,3},{2,0},{3,1},{4,6},{5,7},{6,4},{7,5},{8,10},{9,11},{10,... | collective-permute-start | bytes 393224 | tf_op jit(solution)/shard_map/ppermute | solution.py:31
  2.9 0.0 collective-permute-start.2
  2.9 0.0 copy-start
  2.9 3.1 %prepare.1 = (bf16[2048,256]{1,0:T(8,128)(2,1)S(1)}, bf16[2048,256]{1,0:T(8,128)(2,1)S(1)}, bf16[2048,256]{1,0:T(8,128)(2,1)S(1)}, f32[3,8,256]{2,1,0:T(8,128)S(...) custom-call(f32[1,2048]{1,0:T(1,128)} %bitcast.3, ...), custom_call_target="tpu_custom_call" | custom-call | flops 25165824 | bytes 393216 | tf_op jit(solution)/shard_map/prepare/pallas_call | solution.py:18
  6.0 0.0 copy-start.1
  6.0 0.1 collective-permute-start.10
  6.1 0.5 %collective-permute-done.refs_2_ = bf16[128,512]{1,0:T(8,128)(2,1)S(1)} collective-permute-done((bf16[128,512]{1,0:T(8,128)(2,1)}, bf16[128,512]{1,0:T(8,128)(2,1)S(1)}, u32[]{:S(2)}, u32[]{:S(2)}) %collective-permute-start) | collective-permute-done | bytes 131104 | tf_op jit(solution)/shard_map/ppermute | solution.py:31
  6.6 0.0 collective-permute-start.1
  6.7 0.0 copy-done.1
  6.7 0.0 collective-permute-done.2.refs_1_
  6.7 0.1 broadcast_in_dim.7
  6.8 0.0 copy-done
  6.8 0.6 %early.1 = (f32[3,128,128]{2,1,0:T(8,128)S(1)}, f32[128,256]{1,0:T(8,128)S(1)}, f32[128,256]{1,0:T(8,128)S(1)}, f32[128,256]{1,0:T(8,128)S(1)}, f32[1,256]{1,0:T(1,128)S(1)}) custom-call(bf16[128,512]{1,0:T(8,128)(2,1)S(1)} %copy-done, bf16[128,512]{1,0:T(8,128)(2,1)S(1)} %collective-permute-done.2.refs_1_, ...), custom_call_target="tpu_custom_call" | custom-call | flops 1073741824 | bytes 16777216 | tf_op jit(solution)/shard_map/early/pallas_call | solution.py:18
  7.4 0.6 %collective-permute-done.1.refs_0_ = bf16[128,512]{1,0:T(8,128)(2,1)S(1)} collective-permute-done((bf16[128,512]{1,0:T(8,128)(2,1)S(1)}, bf16[128,512]{1,0:T(8,128)(2,1)S(1)}, u32[]{:S(2)}, u32[]{:S(2)}) %collective-permute-start.1) | collective-permute-done | bytes 131104 | tf_op jit(solution)/shard_map/ppermute | solution.py:31
  8.0 0.4 %late.1 = (bf16[128,256]{1,0:T(8,128)(2,1)S(1)}, bf16[128,384]{1,0:T(8,128)(2,1)S(1)}, bf16[128,256]{1,0:T(8,128)(2,1)S(1)}, bf16[128,384]{1,0:T(8,128)(2,1)S(1)}) custom-call(bf16[128,512]{1,0:T(8,128)(2,1)S(1)} %collective-permute-done.1.refs_0_, bf16[2048,256]{1,0:T(8,128)(2,1)S(1)} %get-tuple-element.32.refs_3_.refs_1_, ...), custom_call_target="tpu_custom_call" | custom-call | tf_op jit(solution)/shard_map/late/pallas_call | solution.py:18
  8.4 2.7 %collective-permute-start.3 = (bf16[128,256]{1,0:T(8,128)(2,1)S(1)}, bf16[128,256]{1,0:T(8,128)(2,1)S(1)}, u32[]{:S(2)}, u32[]{:S(2)}) collective-permute-start(bf16[128,256]{1,0:T(8,128)(2,1)S(1)} %get-tuple-element.43), channel_id=1, source_target_pairs={{0,9},{1,8},{2,11},{3,10},{4,13},{5,12},{6,15},{7,14},{8,1},{9,0},... | collective-permute-start | bytes 196616 | tf_op jit(solution)/shard_map/ppermute | solution.py:31
  11.0 1.3 %collective-permute-start.6 = (bf16[128,256]{1,0:T(8,128)(2,1)S(1)}, bf16[128,256]{1,0:T(8,128)(2,1)S(1)}, u32[]{:S(2)}, u32[]{:S(2)}) collective-permute-start(bf16[128,256]{1,0:T(8,128)(2,1)S(1)} %get-tuple-element.46), channel_id=1, source_target_pairs={{0,13},{1,12},{2,15},{3,14},{4,9},{5,8},{6,11},{7,10},{8,5},{9,4},... | collective-permute-start | bytes 196616 | tf_op jit(solution)/shard_map/ppermute | solution.py:31
  12.3 0.2 collective-permute-start.5
  12.6 0.9 %collective-permute-done.3.refs_0_ = bf16[128,256]{1,0:T(8,128)(2,1)S(1)} collective-permute-done((bf16[128,256]{1,0:T(8,128)(2,1)S(1)}, bf16[128,256]{1,0:T(8,128)(2,1)S(1)}, u32[]{:S(2)}, u32[]{:S(2)}) %collective-permute-start.3) | collective-permute-done | bytes 65568 | tf_op jit(solution)/shard_map/ppermute | solution.py:31
  13.5 1.4 %collective-permute-start.4 = (bf16[128,384]{1,0:T(8,128)(2,1)S(1)}, bf16[128,384]{1,0:T(8,128)(2,1)S(1)}, u32[]{:S(2)}, u32[]{:S(2)}) collective-permute-start(bf16[128,384]{1,0:T(8,128)(2,1)S(1)} %get-tuple-element.44), channel_id=1, source_target_pairs={{0,1},{1,0},{2,3},{3,2},{4,5},{5,4},{6,7},{7,6},{8,9},{9,8},{10,11... | collective-permute-start | bytes 294920 | tf_op jit(solution)/shard_map/ppermute | solution.py:31
  14.9 0.0 collective-permute-start.11
  14.9 2.0 %collective-permute-done.6.refs_1_ = bf16[128,256]{1,0:T(8,128)(2,1)S(1)} collective-permute-done((bf16[128,256]{1,0:T(8,128)(2,1)S(1)}, bf16[128,256]{1,0:T(8,128)(2,1)S(1)}, u32[]{:S(2)}, u32[]{:S(2)}) %collective-permute-start.6) | collective-permute-done | bytes 65568 | tf_op jit(solution)/shard_map/ppermute | solution.py:31
  16.9 1.6 %collective-permute-done.5.refs_0_ = bf16[128,384]{1,0:T(8,128)(2,1)S(1)} collective-permute-done((bf16[128,384]{1,0:T(8,128)(2,1)S(1)}, bf16[128,384]{1,0:T(8,128)(2,1)S(1)}, u32[]{:S(2)}, u32[]{:S(2)}) %collective-permute-start.5) | collective-permute-done | bytes 98336 | tf_op jit(solution)/shard_map/ppermute | solution.py:31
  18.5 0.0 collective-permute-done.4.refs_0_
  18.5 0.5 %attend.1 = (bf16[128,128]{1,0:T(8,128)(2,1)S(1)}, bf16[128,128]{1,0:T(8,128)(2,1)S(1)}) custom-call(bf16[128,384]{1,0:T(8,128)(2,1)S(1)} %collective-permute-done.4.refs_0_, bf16[128,384]{1,0:T(8,128)(2,1)S(1)} %hold.1.refs_1_, bf16[256,256]{1,0:T(8,128)(2,1)S(1)} %merge.1.refs_2_), custom_call_target="tpu_custom_call" | custom-call | tf_op jit(solution)/shard_map/attend/pallas_call | solution.py:18
  19.1 1.4 %collective-permute-start.7 = (bf16[128,128]{1,0:T(8,128)(2,1)S(1)}, bf16[128,128]{1,0:T(8,128)(2,1)S(1)}, u32[]{:S(2)}, u32[]{:S(2)}) collective-permute-start(bf16[128,128]{1,0:T(8,128)(2,1)S(1)} %get-tuple-element.47), channel_id=1, source_target_pairs={{0,7},{1,6},{2,5},{3,4},{4,3},{5,2},{6,1},{7,0},{8,15},{9,14},{10,... | collective-permute-start | bytes 98312 | tf_op jit(solution)/shard_map/ppermute | solution.py:31
  20.5 0.4 %collective-permute-start.8 = (bf16[128,128]{1,0:T(8,128)(2,1)S(1)}, bf16[128,128]{1,0:T(8,128)(2,1)S(1)}, u32[]{:S(2)}, u32[]{:S(2)}) collective-permute-start(bf16[128,128]{1,0:T(8,128)(2,1)S(1)} %get-tuple-element.48.mixed_ref), channel_id=1, source_target_pairs={{0,3},{1,2},{2,1},{3,0},{4,7},{5,6},{6,5},{7,4},{8,11},{9,10},{10,... | collective-permute-start | bytes 98312 | tf_op jit(solution)/shard_map/ppermute | solution.py:31
  20.9 1.5 %collective-permute-start.9 = (bf16[128,128]{1,0:T(8,128)(2,1)S(1)}, bf16[128,128]{1,0:T(8,128)(2,1)S(1)}, u32[]{:S(2)}, u32[]{:S(2)}) collective-permute-start(bf16[128,128]{1,0:T(8,128)(2,1)S(1)} %get-tuple-element.47), channel_id=1, source_target_pairs={{0,5},{1,4},{2,7},{3,6},{4,1},{5,0},{6,3},{7,2},{8,13},{9,12},{10,... | collective-permute-start | bytes 98312 | tf_op jit(solution)/shard_map/ppermute | solution.py:31
  22.4 0.0 collective-permute-done.11.exit_ref
  22.4 0.2 own.1
  22.6 0.7 %collective-permute-done.7.refs_0_ = bf16[128,128]{1,0:T(8,128)(2,1)S(1)} collective-permute-done((bf16[128,128]{1,0:T(8,128)(2,1)S(1)}, bf16[128,128]{1,0:T(8,128)(2,1)S(1)}, u32[]{:S(2)}, u32[]{:S(2)}) %collective-permute-start.7) | collective-permute-done | bytes 32800 | tf_op jit(solution)/shard_map/ppermute | solution.py:31
  23.4 0.9 %collective-permute-done.8.refs_1_ = bf16[128,128]{1,0:T(8,128)(2,1)S(1)} collective-permute-done((bf16[128,128]{1,0:T(8,128)(2,1)S(1)}, bf16[128,128]{1,0:T(8,128)(2,1)S(1)}, u32[]{:S(2)}, u32[]{:S(2)}) %collective-permute-start.8) | collective-permute-done | bytes 32800 | tf_op jit(solution)/shard_map/ppermute | solution.py:31
  24.2 0.0 collective-permute-done.10.refs_3_.refs_4_.refs_2_
  24.2 0.2 crossed.1.refs_2_
  24.5 0.1 collective-permute-done.9.refs_2_.refs_0_
  24.6 0.2 sent.1
  24.7 0.4 %collective-permute-start.12 = (bf16[128,512]{1,0:T(8,128)(2,1)S(1)}, bf16[128,512]{1,0:T(8,128)(2,1)S(1)}, u32[]{:S(2)}, u32[]{:S(2)}) collective-permute-start(bf16[128,512]{1,0:T(8,128)(2,1)S(1)} %sent.1), channel_id=1, source_target_pairs={{0,1},{1,0},{2,3},{3,2},{4,5},{5,4},{6,7},{7,6},{8,9},{9,8},{10,11... | collective-permute-start | bytes 393224 | tf_op jit(solution)/shard_map/ppermute | solution.py:31
  25.1 0.2 kept.1
  25.4 0.8 %collective-permute-done.12 = bf16[128,512]{1,0:T(8,128)(2,1)S(1)} collective-permute-done((bf16[128,512]{1,0:T(8,128)(2,1)S(1)}, bf16[128,512]{1,0:T(8,128)(2,1)S(1)}, u32[]{:S(2)}, u32[]{:S(2)}) %collective-permute-start.12) | collective-permute-done | bytes 131104 | tf_op jit(solution)/shard_map/ppermute | solution.py:31
  26.2 0.7 %add_convert_fusion = bf16[128,512]{1,0:T(8,128)(2,1)} fusion(f32[128,512]{1,0:T(8,128)S(1)} %kept.1, bf16[128,512]{1,0:T(8,128)(2,1)S(1)} %collective-permute-done.12), kind=kLoop, calls=%fused_computation | loop fusion | flops 196608 | bytes 524288 | tf_op jit(solution)/shard_map/convert_element_type | solution.py:355
  (3 shorter events, 0.0 us)
Async XLA Ops:
  0.0 6.6 %collective-permute-start = (bf16[128,512]{1,0:T(8,128)(2,1)}, bf16[128,512]{1,0:T(8,128)(2,1)S(1)}, u32[]{:S(2)}, u32[]{:S(2)}) collective-permute-start(bf16[128,512]{1,0:T(8,128)(2,1)} %x_ref.1), channel_id=1, source_target_pairs={{0,2},{1,3},{2,0},{3,1},{4,6},{5,7},{6,4},{7,5},{8,10},{9,11},{10,... | collective-permute-start | bytes 393224 | tf_op jit(solution)/shard_map/ppermute | solution.py:31
  2.9 3.8 %collective-permute-start.2 = (bf16[128,512]{1,0:T(8,128)(2,1)}, bf16[128,512]{1,0:T(8,128)(2,1)S(1)}, u32[]{:S(2)}, u32[]{:S(2)}) collective-permute-start(bf16[128,512]{1,0:T(8,128)(2,1)} %x_ref.1), channel_id=1, source_target_pairs={{0,1},{1,0},{2,3},{3,2},{4,5},{5,4},{6,7},{7,6},{8,9},{9,8},{10,11... | collective-permute-start | bytes 393224 | tf_op jit(solution)/shard_map/ppermute | solution.py:31
  2.9 3.8 %copy-start = (bf16[128,512]{1,0:T(8,128)(2,1)S(1)}, bf16[128,512]{1,0:T(8,128)(2,1)}, u32[]{:S(2)}) copy-start(bf16[128,512]{1,0:T(8,128)(2,1)} %x_ref.1) | copy-start | bytes 393220
  6.0 0.7 %copy-start.1 = (f32[2]{0:T(128)S(1)}, f32[2]{0:T(128)}, u32[]{:S(2)}) copy-start(f32[2]{0:T(128)} %param.12) | copy-start | bytes 28
  6.0 18.2 %collective-permute-start.10 = (bf16[2,256,512]{2,1,0:T(8,128)(2,1)S(1)}, bf16[2,256,512]{2,1,0:T(8,128)(2,1)S(1)}, u32[]{:S(2)}, u32[]{:S(2)}) collective-permute-start(bf16[2,256,512]{2,1,0:T(8,128)(2,1)S(1)} %get-tuple-element.49), channel_id=1, source_target_pairs={{0,2},{1,3},{2,0},{3,1},{4,6},{5,7},{6,4},{7,5},{8,10},{9,11},{10,... | collective-permute-start | bytes 1572872 | tf_op jit(solution)/shard_map/ppermute | solution.py:31
  6.6 1.3 %collective-permute-start.1 = (bf16[128,512]{1,0:T(8,128)(2,1)S(1)}, bf16[128,512]{1,0:T(8,128)(2,1)S(1)}, u32[]{:S(2)}, u32[]{:S(2)}) collective-permute-start(bf16[128,512]{1,0:T(8,128)(2,1)S(1)} %collective-permute-done.refs_2_), channel_id=1, source_target_pairs={{0,1},{1,0},{2,3},{3,2},{4,5},{5,4},{6,7},{7,6},{8,9},{9,8},{10,11... | collective-permute-start | bytes 393224 | tf_op jit(solution)/shard_map/ppermute | solution.py:31
  8.4 5.2 %collective-permute-start.3 = (bf16[128,256]{1,0:T(8,128)(2,1)S(1)}, bf16[128,256]{1,0:T(8,128)(2,1)S(1)}, u32[]{:S(2)}, u32[]{:S(2)}) collective-permute-start(bf16[128,256]{1,0:T(8,128)(2,1)S(1)} %get-tuple-element.43), channel_id=1, source_target_pairs={{0,9},{1,8},{2,11},{3,10},{4,13},{5,12},{6,15},{7,14},{8,1},{9,0},... | collective-permute-start | bytes 196616 | tf_op jit(solution)/shard_map/ppermute | solution.py:31
  11.0 5.9 %collective-permute-start.6 = (bf16[128,256]{1,0:T(8,128)(2,1)S(1)}, bf16[128,256]{1,0:T(8,128)(2,1)S(1)}, u32[]{:S(2)}, u32[]{:S(2)}) collective-permute-start(bf16[128,256]{1,0:T(8,128)(2,1)S(1)} %get-tuple-element.46), channel_id=1, source_target_pairs={{0,13},{1,12},{2,15},{3,14},{4,9},{5,8},{6,11},{7,10},{8,5},{9,4},... | collective-permute-start | bytes 196616 | tf_op jit(solution)/shard_map/ppermute | solution.py:31
  12.3 6.2 %collective-permute-start.5 = (bf16[128,384]{1,0:T(8,128)(2,1)S(1)}, bf16[128,384]{1,0:T(8,128)(2,1)S(1)}, u32[]{:S(2)}, u32[]{:S(2)}) collective-permute-start(bf16[128,384]{1,0:T(8,128)(2,1)S(1)} %get-tuple-element.45), channel_id=1, source_target_pairs={{0,5},{1,4},{2,7},{3,6},{4,1},{5,0},{6,3},{7,2},{8,13},{9,12},{10,... | collective-permute-start | bytes 294920 | tf_op jit(solution)/shard_map/ppermute | solution.py:31
  13.5 5.0 %collective-permute-start.4 = (bf16[128,384]{1,0:T(8,128)(2,1)S(1)}, bf16[128,384]{1,0:T(8,128)(2,1)S(1)}, u32[]{:S(2)}, u32[]{:S(2)}) collective-permute-start(bf16[128,384]{1,0:T(8,128)(2,1)S(1)} %get-tuple-element.44), channel_id=1, source_target_pairs={{0,1},{1,0},{2,3},{3,2},{4,5},{5,4},{6,7},{7,6},{8,9},{9,8},{10,11... | collective-permute-start | bytes 294920 | tf_op jit(solution)/shard_map/ppermute | solution.py:31
  14.9 7.5 %collective-permute-start.11 = (bf16[2,128,512]{2,1,0:T(8,128)(2,1)S(1)}, bf16[2,128,512]{2,1,0:T(8,128)(2,1)S(1)}, u32[]{:S(2)}, u32[]{:S(2)}) collective-permute-start(bf16[2,128,512]{2,1,0:T(8,128)(2,1)S(1)} %get-tuple-element.52), channel_id=1, source_target_pairs={{0,1},{1,0},{2,3},{3,2},{4,5},{5,4},{6,7},{7,6},{8,9},{9,8},{10,11... | collective-permute-start | bytes 786440 | tf_op jit(solution)/shard_map/ppermute | solution.py:31
  19.1 4.3 %collective-permute-start.7 = (bf16[128,128]{1,0:T(8,128)(2,1)S(1)}, bf16[128,128]{1,0:T(8,128)(2,1)S(1)}, u32[]{:S(2)}, u32[]{:S(2)}) collective-permute-start(bf16[128,128]{1,0:T(8,128)(2,1)S(1)} %get-tuple-element.47), channel_id=1, source_target_pairs={{0,7},{1,6},{2,5},{3,4},{4,3},{5,2},{6,1},{7,0},{8,15},{9,14},{10,... | collective-permute-start | bytes 98312 | tf_op jit(solution)/shard_map/ppermute | solution.py:31
  20.5 3.8 %collective-permute-start.8 = (bf16[128,128]{1,0:T(8,128)(2,1)S(1)}, bf16[128,128]{1,0:T(8,128)(2,1)S(1)}, u32[]{:S(2)}, u32[]{:S(2)}) collective-permute-start(bf16[128,128]{1,0:T(8,128)(2,1)S(1)} %get-tuple-element.48.mixed_ref), channel_id=1, source_target_pairs={{0,3},{1,2},{2,1},{3,0},{4,7},{5,6},{6,5},{7,4},{8,11},{9,10},{10,... | collective-permute-start | bytes 98312 | tf_op jit(solution)/shard_map/ppermute | solution.py:31
  20.9 3.7 %collective-permute-start.9 = (bf16[128,128]{1,0:T(8,128)(2,1)S(1)}, bf16[128,128]{1,0:T(8,128)(2,1)S(1)}, u32[]{:S(2)}, u32[]{:S(2)}) collective-permute-start(bf16[128,128]{1,0:T(8,128)(2,1)S(1)} %get-tuple-element.47), channel_id=1, source_target_pairs={{0,5},{1,4},{2,7},{3,6},{4,1},{5,0},{6,3},{7,2},{8,13},{9,12},{10,... | collective-permute-start | bytes 98312 | tf_op jit(solution)/shard_map/ppermute | solution.py:31
  24.7 1.4 %collective-permute-start.12 = (bf16[128,512]{1,0:T(8,128)(2,1)S(1)}, bf16[128,512]{1,0:T(8,128)(2,1)S(1)}, u32[]{:S(2)}, u32[]{:S(2)}) collective-permute-start(bf16[128,512]{1,0:T(8,128)(2,1)S(1)} %sent.1), channel_id=1, source_target_pairs={{0,1},{1,0},{2,3},{3,2},{4,5},{5,4},{6,7},{7,6},{8,9},{9,8},{10,11... | collective-permute-start | bytes 393224 | tf_op jit(solution)/shard_map/ppermute | solution.py:31

commit v10 on v8

--- a/solution.py
+++ b/solution.py
@@ -93,7 +93,7 @@
 def prepare(mp, gain, probe, lookup, content, exit_matrix):
     depth, cols = probe.shape
     deep, wide = exit_matrix.shape
-    parts = 4
+    parts = 2
     half, stack = (pltpu.VMEM((mp // 2, d, wide // mp), BF16) for d in (deep // 2, deep))
     probe, lookup, content, sums, gain, own, twin, far = call(
         functools.partial(prepare_kernel, mp),

time: 27 us -> 27 us (level)
  waiting for transfers between devices: 8.13 us -> 8.59 us
  Pallas kernels: 5.38 us -> 4.99 us
    ppermute x13, waiting for transfers between devices: 8.13 us -> 8.59 us  [swap(): return lax.ppermute(block, axis, [(i, i ^ distance) for i in range(count)])]
    pallas_call x10, Pallas kernels: 5.38 us -> 4.99 us  [call(): pl.pallas_call(kernel, out_shape=out_shape, in_specs=specs or [VMEM] * le...]
  transfers between devices with their start and end apart: 13 -> 13, of which waited for: 8 -> 8; matrix products, arithmetic and copies ran while one was open for 0% -> 0% of each run, Pallas kernels for 19% -> 18%
where the time goes in v10:
time: 27 us; the launch traced here: 26.8 us
  starting transfers between devices  12.4 us (46%)
  waiting for transfers between devices  8.59 us (32%)
  Pallas kernels  4.99 us (18%)
  other arithmetic  0.68 us (3%)
    ppermute x13, starting transfers between devices, swap(): return lax.ppermute(block, axis, [(i, i ^ distance) for i in range(count)])  12.4 us
    ppermute x13, waiting for transfers between devices, swap(): return lax.ppermute(block, axis, [(i, i ^ distance) for i in range(count)])  8.59 us
    pallas_call x10, Pallas kernels, call(): pl.pallas_call(kernel, out_shape=out_shape, in_specs=specs or [VMEM] * le...  4.99 us
    convert_element_type x1, other arithmetic, per_device(): return shares[0].astype(node_vectors.dtype)  0.68 us
  transfers between devices with their start and end apart: 13, of which 8 were waited for; matrix products, arithmetic and copies ran while one was open for 0% of the time, Pallas kernels for 18%

profile of v10, /device:TPU:0, one launch (start us, length us, event | category | flops | bytes accessed | tf_op | source)
XLA Modules:
  0.0 26.8 jit_solution(14250889608439697492)
XLA Ops:
  0.0 2.9 %collective-permute-start = (bf16[128,512]{1,0:T(8,128)(2,1)}, bf16[128,512]{1,0:T(8,128)(2,1)S(1)}, u32[]{:S(2)}, u32[]{:S(2)}) collective-permute-start(bf16[128,512]{1,0:T(8,128)(2,1)} %x_ref.1), channel_id=1, source_target_pairs={{0,2},{1,3},{2,0},{3,1},{4,6},{5,7},{6,4},{7,5},{8,10},{9,11},{10,... | collective-permute-start | bytes 393224 | tf_op jit(solution)/shard_map/ppermute | solution.py:31
  2.9 0.0 collective-permute-start.2
  2.9 0.0 copy-start
  2.9 2.7 %prepare.1 = (bf16[2048,256]{1,0:T(8,128)(2,1)S(1)}, bf16[2048,256]{1,0:T(8,128)(2,1)S(1)}, bf16[2048,256]{1,0:T(8,128)(2,1)S(1)}, f32[3,8,256]{2,1,0:T(8,128)S(...) custom-call(f32[1,2048]{1,0:T(1,128)} %bitcast.3, ...), custom_call_target="tpu_custom_call" | custom-call | flops 25165824 | bytes 393216 | tf_op jit(solution)/shard_map/prepare/pallas_call | solution.py:18
  5.6 0.0 copy-start.1
  5.6 0.1 collective-permute-start.10
  5.7 0.9 %collective-permute-done.refs_2_ = bf16[128,512]{1,0:T(8,128)(2,1)S(1)} collective-permute-done((bf16[128,512]{1,0:T(8,128)(2,1)}, bf16[128,512]{1,0:T(8,128)(2,1)S(1)}, u32[]{:S(2)}, u32[]{:S(2)}) %collective-permute-start) | collective-permute-done | bytes 131104 | tf_op jit(solution)/shard_map/ppermute | solution.py:31
  6.6 0.0 collective-permute-start.1
  6.6 0.0 copy-done.1
  6.7 0.0 collective-permute-done.2.refs_1_
  6.7 0.1 broadcast_in_dim.7
  6.7 0.0 copy-done
  6.7 0.6 %early.1 = (f32[3,128,128]{2,1,0:T(8,128)S(1)}, f32[128,256]{1,0:T(8,128)S(1)}, f32[128,256]{1,0:T(8,128)S(1)}, f32[128,256]{1,0:T(8,128)S(1)}, f32[1,256]{1,0:T(1,128)S(1)}) custom-call(bf16[128,512]{1,0:T(8,128)(2,1)S(1)} %copy-done, bf16[128,512]{1,0:T(8,128)(2,1)S(1)} %collective-permute-done.2.refs_1_, ...), custom_call_target="tpu_custom_call" | custom-call | flops 1073741824 | bytes 16777216 | tf_op jit(solution)/shard_map/early/pallas_call | solution.py:18
  7.4 0.6 %collective-permute-done.1.refs_0_ = bf16[128,512]{1,0:T(8,128)(2,1)S(1)} collective-permute-done((bf16[128,512]{1,0:T(8,128)(2,1)S(1)}, bf16[128,512]{1,0:T(8,128)(2,1)S(1)}, u32[]{:S(2)}, u32[]{:S(2)}) %collective-permute-start.1) | collective-permute-done | bytes 131104 | tf_op jit(solution)/shard_map/ppermute | solution.py:31
  8.0 0.4 %late.1 = (bf16[128,256]{1,0:T(8,128)(2,1)S(1)}, bf16[128,384]{1,0:T(8,128)(2,1)S(1)}, bf16[128,256]{1,0:T(8,128)(2,1)S(1)}, bf16[128,384]{1,0:T(8,128)(2,1)S(1)}) custom-call(bf16[128,512]{1,0:T(8,128)(2,1)S(1)} %collective-permute-done.1.refs_0_, bf16[2048,256]{1,0:T(8,128)(2,1)S(1)} %get-tuple-element.34.refs_3_.refs_1_, ...), custom_call_target="tpu_custom_call" | custom-call | tf_op jit(solution)/shard_map/late/pallas_call | solution.py:18
  8.4 2.7 %collective-permute-start.3 = (bf16[128,256]{1,0:T(8,128)(2,1)S(1)}, bf16[128,256]{1,0:T(8,128)(2,1)S(1)}, u32[]{:S(2)}, u32[]{:S(2)}) collective-permute-start(bf16[128,256]{1,0:T(8,128)(2,1)S(1)} %get-tuple-element.45), channel_id=1, source_target_pairs={{0,9},{1,8},{2,11},{3,10},{4,13},{5,12},{6,15},{7,14},{8,1},{9,0},... | collective-permute-start | bytes 196616 | tf_op jit(solution)/shard_map/ppermute | solution.py:31
  11.0 1.3 %collective-permute-start.6 = (bf16[128,256]{1,0:T(8,128)(2,1)S(1)}, bf16[128,256]{1,0:T(8,128)(2,1)S(1)}, u32[]{:S(2)}, u32[]{:S(2)}) collective-permute-start(bf16[128,256]{1,0:T(8,128)(2,1)S(1)} %get-tuple-element.48), channel_id=1, source_target_pairs={{0,13},{1,12},{2,15},{3,14},{4,9},{5,8},{6,11},{7,10},{8,5},{9,4},... | collective-permute-start | bytes 196616 | tf_op jit(solution)/shard_map/ppermute | solution.py:31
  12.3 0.2 collective-permute-start.5
  12.6 0.9 %collective-permute-done.3.refs_0_ = bf16[128,256]{1,0:T(8,128)(2,1)S(1)} collective-permute-done((bf16[128,256]{1,0:T(8,128)(2,1)S(1)}, bf16[128,256]{1,0:T(8,128)(2,1)S(1)}, u32[]{:S(2)}, u32[]{:S(2)}) %collective-permute-start.3) | collective-permute-done | bytes 65568 | tf_op jit(solution)/shard_map/ppermute | solution.py:31
  13.5 1.4 %collective-permute-start.4 = (bf16[128,384]{1,0:T(8,128)(2,1)S(1)}, bf16[128,384]{1,0:T(8,128)(2,1)S(1)}, u32[]{:S(2)}, u32[]{:S(2)}) collective-permute-start(bf16[128,384]{1,0:T(8,128)(2,1)S(1)} %get-tuple-element.46), channel_id=1, source_target_pairs={{0,1},{1,0},{2,3},{3,2},{4,5},{5,4},{6,7},{7,6},{8,9},{9,8},{10,11... | collective-permute-start | bytes 294920 | tf_op jit(solution)/shard_map/ppermute | solution.py:31
  14.9 0.0 collective-permute-start.11
  14.9 2.0 %collective-permute-done.6.refs_1_ = bf16[128,256]{1,0:T(8,128)(2,1)S(1)} collective-permute-done((bf16[128,256]{1,0:T(8,128)(2,1)S(1)}, bf16[128,256]{1,0:T(8,128)(2,1)S(1)}, u32[]{:S(2)}, u32[]{:S(2)}) %collective-permute-start.6) | collective-permute-done | bytes 65568 | tf_op jit(solution)/shard_map/ppermute | solution.py:31
  16.9 1.6 %collective-permute-done.5.refs_0_ = bf16[128,384]{1,0:T(8,128)(2,1)S(1)} collective-permute-done((bf16[128,384]{1,0:T(8,128)(2,1)S(1)}, bf16[128,384]{1,0:T(8,128)(2,1)S(1)}, u32[]{:S(2)}, u32[]{:S(2)}) %collective-permute-start.5) | collective-permute-done | bytes 98336 | tf_op jit(solution)/shard_map/ppermute | solution.py:31
  18.5 0.0 collective-permute-done.4.refs_0_
  18.5 0.5 %attend.1 = (bf16[128,128]{1,0:T(8,128)(2,1)S(1)}, bf16[128,128]{1,0:T(8,128)(2,1)S(1)}) custom-call(bf16[128,384]{1,0:T(8,128)(2,1)S(1)} %collective-permute-done.4.refs_0_, bf16[128,384]{1,0:T(8,128)(2,1)S(1)} %hold.1.refs_1_, bf16[256,256]{1,0:T(8,128)(2,1)S(1)} %merge.1.refs_2_), custom_call_target="tpu_custom_call" | custom-call | tf_op jit(solution)/shard_map/attend/pallas_call | solution.py:18
  19.1 1.4 %collective-permute-start.9 = (bf16[128,128]{1,0:T(8,128)(2,1)S(1)}, bf16[128,128]{1,0:T(8,128)(2,1)S(1)}, u32[]{:S(2)}, u32[]{:S(2)}) collective-permute-start(bf16[128,128]{1,0:T(8,128)(2,1)S(1)} %get-tuple-element.49), channel_id=1, source_target_pairs={{0,7},{1,6},{2,5},{3,4},{4,3},{5,2},{6,1},{7,0},{8,15},{9,14},{10,... | collective-permute-start | bytes 98312 | tf_op jit(solution)/shard_map/ppermute | solution.py:31
  20.5 0.3 %collective-permute-start.8 = (bf16[128,128]{1,0:T(8,128)(2,1)S(1)}, bf16[128,128]{1,0:T(8,128)(2,1)S(1)}, u32[]{:S(2)}, u32[]{:S(2)}) collective-permute-start(bf16[128,128]{1,0:T(8,128)(2,1)S(1)} %get-tuple-element.51.mixed_ref), channel_id=1, source_target_pairs={{0,3},{1,2},{2,1},{3,0},{4,7},{5,6},{6,5},{7,4},{8,11},{9,10},{10,... | collective-permute-start | bytes 98312 | tf_op jit(solution)/shard_map/ppermute | solution.py:31
  20.8 1.6 %collective-permute-start.7 = (bf16[128,128]{1,0:T(8,128)(2,1)S(1)}, bf16[128,128]{1,0:T(8,128)(2,1)S(1)}, u32[]{:S(2)}, u32[]{:S(2)}) collective-permute-start(bf16[128,128]{1,0:T(8,128)(2,1)S(1)} %get-tuple-element.49), channel_id=1, source_target_pairs={{0,5},{1,4},{2,7},{3,6},{4,1},{5,0},{6,3},{7,2},{8,13},{9,12},{10,... | collective-permute-start | bytes 98312 | tf_op jit(solution)/shard_map/ppermute | solution.py:31
  22.4 0.0 collective-permute-done.11.exit_ref
  22.4 0.2 own.1
  22.6 0.7 %collective-permute-done.9.refs_1_ = bf16[128,128]{1,0:T(8,128)(2,1)S(1)} collective-permute-done((bf16[128,128]{1,0:T(8,128)(2,1)S(1)}, bf16[128,128]{1,0:T(8,128)(2,1)S(1)}, u32[]{:S(2)}, u32[]{:S(2)}) %collective-permute-start.9) | collective-permute-done | bytes 32800 | tf_op jit(solution)/shard_map/ppermute | solution.py:31
  23.4 0.9 %collective-permute-done.8.refs_0_ = bf16[128,128]{1,0:T(8,128)(2,1)S(1)} collective-permute-done((bf16[128,128]{1,0:T(8,128)(2,1)S(1)}, bf16[128,128]{1,0:T(8,128)(2,1)S(1)}, u32[]{:S(2)}, u32[]{:S(2)}) %collective-permute-start.8) | collective-permute-done | bytes 32800 | tf_op jit(solution)/shard_map/ppermute | solution.py:31
  24.2 0.0 collective-permute-done.10.refs_2_.refs_3_
  24.2 0.3 %crossed.1 = (f32[128,512]{1,0:T(8,128)S(1)}, f32[128,512]{1,0:T(8,128)S(1)}) custom-call(bf16[128,128]{1,0:T(8,128)(2,1)S(1)} %collective-permute-done.8.refs_0_, bf16[128,128]{1,0:T(8,128)(2,1)S(1)} %collective-permute-done.9.refs_1_, bf16[2,256,512]{2,1,0:T(8,128)(2,1)S(1)} %collective-permute-done.10.refs_2_.refs_3_, ...), custom_call_target="tpu_custom_call" | custom-call | flops 1073741824 | bytes 16777216 | tf_op jit(solution)/shard_map/crossed/pallas_call | solution.py:18
  24.5 0.0 collective-permute-done.7.refs_0_
  24.5 0.2 sent.1
  24.7 0.4 %collective-permute-start.12 = (bf16[128,512]{1,0:T(8,128)(2,1)S(1)}, bf16[128,512]{1,0:T(8,128)(2,1)S(1)}, u32[]{:S(2)}, u32[]{:S(2)}) collective-permute-start(bf16[128,512]{1,0:T(8,128)(2,1)S(1)} %sent.1), channel_id=1, source_target_pairs={{0,1},{1,0},{2,3},{3,2},{4,5},{5,4},{6,7},{7,6},{8,9},{9,8},{10,11... | collective-permute-start | bytes 393224 | tf_op jit(solution)/shard_map/ppermute | solution.py:31
  25.1 0.2 kept.1
  25.3 0.9 %collective-permute-done.12 = bf16[128,512]{1,0:T(8,128)(2,1)S(1)} collective-permute-done((bf16[128,512]{1,0:T(8,128)(2,1)S(1)}, bf16[128,512]{1,0:T(8,128)(2,1)S(1)}, u32[]{:S(2)}, u32[]{:S(2)}) %collective-permute-start.12) | collective-permute-done | bytes 131104 | tf_op jit(solution)/shard_map/ppermute | solution.py:31
  26.1 0.7 %add_convert_fusion = bf16[128,512]{1,0:T(8,128)(2,1)} fusion(f32[128,512]{1,0:T(8,128)S(1)} %kept.1, bf16[128,512]{1,0:T(8,128)(2,1)S(1)} %collective-permute-done.12), kind=kLoop, calls=%fused_computation | loop fusion | flops 196608 | bytes 524288 | tf_op jit(solution)/shard_map/convert_element_type | solution.py:355
  (3 shorter events, 0.0 us)
Async XLA Ops:
  0.0 6.6 %collective-permute-start = (bf16[128,512]{1,0:T(8,128)(2,1)}, bf16[128,512]{1,0:T(8,128)(2,1)S(1)}, u32[]{:S(2)}, u32[]{:S(2)}) collective-permute-start(bf16[128,512]{1,0:T(8,128)(2,1)} %x_ref.1), channel_id=1, source_target_pairs={{0,2},{1,3},{2,0},{3,1},{4,6},{5,7},{6,4},{7,5},{8,10},{9,11},{10,... | collective-permute-start | bytes 393224 | tf_op jit(solution)/shard_map/ppermute | solution.py:31
  2.9 3.7 %collective-permute-start.2 = (bf16[128,512]{1,0:T(8,128)(2,1)}, bf16[128,512]{1,0:T(8,128)(2,1)S(1)}, u32[]{:S(2)}, u32[]{:S(2)}) collective-permute-start(bf16[128,512]{1,0:T(8,128)(2,1)} %x_ref.1), channel_id=1, source_target_pairs={{0,1},{1,0},{2,3},{3,2},{4,5},{5,4},{6,7},{7,6},{8,9},{9,8},{10,11... | collective-permute-start | bytes 393224 | tf_op jit(solution)/shard_map/ppermute | solution.py:31
  2.9 3.8 %copy-start = (bf16[128,512]{1,0:T(8,128)(2,1)S(1)}, bf16[128,512]{1,0:T(8,128)(2,1)}, u32[]{:S(2)}) copy-start(bf16[128,512]{1,0:T(8,128)(2,1)} %x_ref.1) | copy-start | bytes 393220
  5.6 1.0 %copy-start.1 = (f32[2]{0:T(128)S(1)}, f32[2]{0:T(128)}, u32[]{:S(2)}) copy-start(f32[2]{0:T(128)} %param.12) | copy-start | bytes 28
  5.6 18.6 %collective-permute-start.10 = (bf16[2,256,512]{2,1,0:T(8,128)(2,1)S(1)}, bf16[2,256,512]{2,1,0:T(8,128)(2,1)S(1)}, u32[]{:S(2)}, u32[]{:S(2)}) collective-permute-start(bf16[2,256,512]{2,1,0:T(8,128)(2,1)S(1)} %get-tuple-element.52), channel_id=1, source_target_pairs={{0,2},{1,3},{2,0},{3,1},{4,6},{5,7},{6,4},{7,5},{8,10},{9,11},{10,... | collective-permute-start | bytes 1572872 | tf_op jit(solution)/shard_map/ppermute | solution.py:31
  6.6 1.3 %collective-permute-start.1 = (bf16[128,512]{1,0:T(8,128)(2,1)S(1)}, bf16[128,512]{1,0:T(8,128)(2,1)S(1)}, u32[]{:S(2)}, u32[]{:S(2)}) collective-permute-start(bf16[128,512]{1,0:T(8,128)(2,1)S(1)} %collective-permute-done.refs_2_), channel_id=1, source_target_pairs={{0,1},{1,0},{2,3},{3,2},{4,5},{5,4},{6,7},{7,6},{8,9},{9,8},{10,11... | collective-permute-start | bytes 393224 | tf_op jit(solution)/shard_map/ppermute | solution.py:31
  8.4 5.2 %collective-permute-start.3 = (bf16[128,256]{1,0:T(8,128)(2,1)S(1)}, bf16[128,256]{1,0:T(8,128)(2,1)S(1)}, u32[]{:S(2)}, u32[]{:S(2)}) collective-permute-start(bf16[128,256]{1,0:T(8,128)(2,1)S(1)} %get-tuple-element.45), channel_id=1, source_target_pairs={{0,9},{1,8},{2,11},{3,10},{4,13},{5,12},{6,15},{7,14},{8,1},{9,0},... | collective-permute-start | bytes 196616 | tf_op jit(solution)/shard_map/ppermute | solution.py:31
  11.0 5.9 %collective-permute-start.6 = (bf16[128,256]{1,0:T(8,128)(2,1)S(1)}, bf16[128,256]{1,0:T(8,128)(2,1)S(1)}, u32[]{:S(2)}, u32[]{:S(2)}) collective-permute-start(bf16[128,256]{1,0:T(8,128)(2,1)S(1)} %get-tuple-element.48), channel_id=1, source_target_pairs={{0,13},{1,12},{2,15},{3,14},{4,9},{5,8},{6,11},{7,10},{8,5},{9,4},... | collective-permute-start | bytes 196616 | tf_op jit(solution)/shard_map/ppermute | solution.py:31
  12.3 6.2 %collective-permute-start.5 = (bf16[128,384]{1,0:T(8,128)(2,1)S(1)}, bf16[128,384]{1,0:T(8,128)(2,1)S(1)}, u32[]{:S(2)}, u32[]{:S(2)}) collective-permute-start(bf16[128,384]{1,0:T(8,128)(2,1)S(1)} %get-tuple-element.47), channel_id=1, source_target_pairs={{0,5},{1,4},{2,7},{3,6},{4,1},{5,0},{6,3},{7,2},{8,13},{9,12},{10,... | collective-permute-start | bytes 294920 | tf_op jit(solution)/shard_map/ppermute | solution.py:31
  13.5 5.0 %collective-permute-start.4 = (bf16[128,384]{1,0:T(8,128)(2,1)S(1)}, bf16[128,384]{1,0:T(8,128)(2,1)S(1)}, u32[]{:S(2)}, u32[]{:S(2)}) collective-permute-start(bf16[128,384]{1,0:T(8,128)(2,1)S(1)} %get-tuple-element.46), channel_id=1, source_target_pairs={{0,1},{1,0},{2,3},{3,2},{4,5},{5,4},{6,7},{7,6},{8,9},{9,8},{10,11... | collective-permute-start | bytes 294920 | tf_op jit(solution)/shard_map/ppermute | solution.py:31
  14.9 7.5 %collective-permute-start.11 = (bf16[2,128,512]{2,1,0:T(8,128)(2,1)S(1)}, bf16[2,128,512]{2,1,0:T(8,128)(2,1)S(1)}, u32[]{:S(2)}, u32[]{:S(2)}) collective-permute-start(bf16[2,128,512]{2,1,0:T(8,128)(2,1)S(1)} %get-tuple-element.54), channel_id=1, source_target_pairs={{0,1},{1,0},{2,3},{3,2},{4,5},{5,4},{6,7},{7,6},{8,9},{9,8},{10,11... | collective-permute-start | bytes 786440 | tf_op jit(solution)/shard_map/ppermute | solution.py:31
  19.1 4.3 %collective-permute-start.9 = (bf16[128,128]{1,0:T(8,128)(2,1)S(1)}, bf16[128,128]{1,0:T(8,128)(2,1)S(1)}, u32[]{:S(2)}, u32[]{:S(2)}) collective-permute-start(bf16[128,128]{1,0:T(8,128)(2,1)S(1)} %get-tuple-element.49), channel_id=1, source_target_pairs={{0,7},{1,6},{2,5},{3,4},{4,3},{5,2},{6,1},{7,0},{8,15},{9,14},{10,... | collective-permute-start | bytes 98312 | tf_op jit(solution)/shard_map/ppermute | solution.py:31
  20.5 3.8 %collective-permute-start.8 = (bf16[128,128]{1,0:T(8,128)(2,1)S(1)}, bf16[128,128]{1,0:T(8,128)(2,1)S(1)}, u32[]{:S(2)}, u32[]{:S(2)}) collective-permute-start(bf16[128,128]{1,0:T(8,128)(2,1)S(1)} %get-tuple-element.51.mixed_ref), channel_id=1, source_target_pairs={{0,3},{1,2},{2,1},{3,0},{4,7},{5,6},{6,5},{7,4},{8,11},{9,10},{10,... | collective-permute-start | bytes 98312 | tf_op jit(solution)/shard_map/ppermute | solution.py:31
  20.8 3.8 %collective-permute-start.7 = (bf16[128,128]{1,0:T(8,128)(2,1)S(1)}, bf16[128,128]{1,0:T(8,128)(2,1)S(1)}, u32[]{:S(2)}, u32[]{:S(2)}) collective-permute-start(bf16[128,128]{1,0:T(8,128)(2,1)S(1)} %get-tuple-element.49), channel_id=1, source_target_pairs={{0,5},{1,4},{2,7},{3,6},{4,1},{5,0},{6,3},{7,2},{8,13},{9,12},{10,... | collective-permute-start | bytes 98312 | tf_op jit(solution)/shard_map/ppermute | solution.py:31
  24.7 1.4 %collective-permute-start.12 = (bf16[128,512]{1,0:T(8,128)(2,1)S(1)}, bf16[128,512]{1,0:T(8,128)(2,1)S(1)}, u32[]{:S(2)}, u32[]{:S(2)}) collective-permute-start(bf16[128,512]{1,0:T(8,128)(2,1)S(1)} %sent.1), channel_id=1, source_target_pairs={{0,1},{1,0},{2,3},{3,2},{4,5},{5,4},{6,7},{7,6},{8,9},{9,8},{10,11... | collective-permute-start | bytes 393224 | tf_op jit(solution)/shard_map/ppermute | solution.py:31
